TPU v7x, 32 devices: a whole 2x2x4 slice. The times are simulated.
32 devices in a mesh: lon: 16 (over z, y, core), lat: 2 (over x).
Axes of the slice: x: 2, y: 2, z: 4, core: 2. Of those that a mesh axis runs over, the one named last changes fastest.
Arguments:
- target: float32 [3, 32, 16384], P(None, 'lat', 'lon'), may hold values from -6 to 6
- grad_x: float32 [2, 3, 32, 16384], P(None, None, 'lat', 'lon'), may hold values from -6 to 6
- grad_y: float32 [2, 3, 32, 16384], P(None, None, 'lat', 'lon'), may hold values from -6 to 6
- labels: int32 [32, 16384], P('lat', 'lon'), may hold values from 0 to 1
- sweeps: int32 [3], replicated, may hold values from 2 to 4
Outputs:
- stitched: float32 [3, 32, 16384], P(None, 'lat', 'lon')
All inputs are finite; a program needn't handle non-finite values.
Results may differ from a plain program's by a relative error of at most 0.0004.
Values sent between devices are 32-bit elements; how exact they have to be, the bound alone decides.
No kernel may reach another device: no remote copies, remote signals or barrier semaphores. Data moves between devices by JAX's collectives and lax.ppermute only.
A program may use at most 64 MiB of HBM per device.

v0:
```python
import jax
import jax.numpy as jnp
from jax import lax
from jax.sharding import PartitionSpec as P

SOURCES = 2
LEVELS = 3
MAXS = 4


screening = 0.02
damping = 0.8


def with_halo(cells, sides, width, closed):
    for axis, dim in sides:
        count = lax.axis_size(axis)
        ends = count if closed else count - 1
        head = lax.slice_in_dim(cells, 0, width, axis=dim)
        tail = lax.slice_in_dim(cells, cells.shape[dim] - width, cells.shape[dim], axis=dim)
        cells = jnp.concatenate(
            [
                lax.ppermute(tail, axis, [(i, (i + 1) % count) for i in range(ends)]),
                cells,
                lax.ppermute(head, axis, [((i + 1) % count, i) for i in range(ends)]),
            ],
            axis=dim,
        )
    return cells


def shifted(block, axis, distance):
    devices = range(lax.axis_size(axis))
    route = [((i - distance) % len(devices), i) for i in devices]
    return lax.ppermute(block, axis, route)


def from_behind(value, axis, steps):
    count = lax.axis_size(axis)
    first, last = (max(0, -steps), min(count, count - steps))
    return lax.ppermute(value, axis, [(source, source + steps) for source in range(first, last)])


def extend(field, width):
    field = with_halo(field, (("lon", 2),), width, True)
    return with_halo(field, (("lat", 1),), width, False)


def stencil(padded, scale):
    inner = padded[:, 1:-1, 1:-1]
    beside = padded[:, :-2, 1:-1] + padded[:, 2:, 1:-1] + padded[:, 1:-1, :-2] + padded[:, 1:-1, 2:]
    return (screening + 4.0 * scale) * inner - scale * beside


def smooth(field, right, count, scale):
    diag = screening + 4.0 * scale
    rows = field.shape[1]
    both = extend(jnp.concatenate([field, right], 0), MAXS)
    value, wide_right = (both[:3], both[3:])
    first, total = (lax.axis_index("lat") * rows, rows * lax.axis_size("lat"))
    global_row = first - MAXS + lax.iota(jnp.int32, rows + 2 * MAXS)
    inside = ((global_row >= 0) & (global_row < total)).astype(jnp.float32)[None, :, None]

    def sweep_wide(step, value):
        padded = jnp.pad(value, ((0, 0), (1, 1), (1, 1)))
        return (value + damping * (wide_right - stencil(padded, scale)) / diag) * inside

    value = lax.fori_loop(0, count, sweep_wide, value)
    return value[:, MAXS:-MAXS, MAXS:-MAXS]


def restrict(field):
    chans, rows, cols = field.shape
    return field.reshape(chans, rows // 2, 2, cols // 2, 2).mean(axis=(2, 4))


def prolong_from(padded):
    center = padded[:, 1:-1, 1:-1]
    north = padded[:, :-2, 1:-1]
    south = padded[:, 2:, 1:-1]
    west = padded[:, 1:-1, :-2]
    east = padded[:, 1:-1, 2:]
    f00 = 0.5625 * center + 0.1875 * north + 0.1875 * west + 0.0625 * padded[:, :-2, :-2]
    f01 = 0.5625 * center + 0.1875 * north + 0.1875 * east + 0.0625 * padded[:, :-2, 2:]
    f10 = 0.5625 * center + 0.1875 * south + 0.1875 * west + 0.0625 * padded[:, 2:, :-2]
    f11 = 0.5625 * center + 0.1875 * south + 0.1875 * east + 0.0625 * padded[:, 2:, 2:]
    stacked = jnp.stack([jnp.stack([f00, f01], -1), jnp.stack([f10, f11], -1)], 2)
    chans, rows, two, cols, other = stacked.shape
    return stacked.reshape(chans, rows * 2, cols * 2)


def cycle(level, field, right, sweeps):
    scale = 0.25**level
    count = sweeps[level]
    field = smooth(field, right, count, scale)
    if level + 1 == LEVELS:
        return field
    resid = right - stencil(extend(field, 1), scale)
    coarse = restrict(resid)
    fix = cycle(level + 1, jnp.zeros_like(coarse), coarse, sweeps)
    field = field + prolong_from(extend(fix, 1))
    return smooth(field, right, count, scale)


def local(target, grad_x, grad_y, labels, sweeps):
    sel_x = jnp.zeros_like(target)
    sel_y = jnp.zeros_like(target)
    for source in range(SOURCES):
        picked = (labels == source)[None, :, :]
        sel_x = jnp.where(picked, grad_x[source], sel_x)
        sel_y = jnp.where(picked, grad_y[source], sel_y)
    west_col = shifted(sel_x[:, :, -1:], "lon", 1)
    north_row = from_behind(sel_y[:, -1:, :], "lat", 1)
    west = jnp.concatenate([west_col, sel_x[:, :, :-1]], axis=2)
    north = jnp.concatenate([north_row, sel_y[:, :-1, :]], axis=1)
    right = screening * target - (sel_x - west + (sel_y - north))
    return cycle(0, target, right, sweeps)


def solution(mesh):
    in_specs = (
        P(None, "lat", "lon"),
        P(None, None, "lat", "lon"),
        P(None, None, "lat", "lon"),
        P("lat", "lon"),
        P(),
    )
    out_specs = P(None, "lat", "lon")
    return jax.shard_map(local, mesh=mesh, in_specs=in_specs, out_specs=out_specs, check_vma=False)
```

profile of v0, /device:TPU:0, one launch (start us, length us, event | category | flops | bytes accessed | tf_op | source)
XLA Modules:
  0.0 203.9 jit_solution(4339111638617756510)
XLA Ops:
  2.2 4.8 %collective-permute-start.1 = (f32[3,1,1024]{2,1,0:T(1,128)S(1)}, f32[3,1,1024]{2,1,0:T(1,128)S(1)}, u32[]{:S(2)}, u32[]{:S(2)}) collective-permute-start(f32[3,1,1024]{2,1,0:T(1,128)S(1)} %slice.515), channel_id=1, source_target_pairs={{0,1},{2,3},{4,5},{6,7},{8,9},{10,11},{12,13},{14,15},{16,17},{18,... | collective-permute-start | bytes 36872 | tf_op jit(solution)/shard_map/ppermute | solution.py:41
  7.1 5.9 %collective-permute-done = f32[3,16,1]{2,1,0:T(8,128)S(1)} collective-permute-done((f32[3,16,1]{2,1,0:T(8,128)S(1)}, f32[3,16,1]{2,1,0:T(8,128)S(1)}, u32[]{:S(2)}, u32[]{:S(2)}) %collective-permute-start) | collective-permute-done | bytes 224 | tf_op jit(solution)/shard_map/ppermute | solution.py:35
  15.0 4.4 %collective-permute-start.3 = (f32[6,16,4]{2,1,0:T(8,128)S(1)}, f32[6,16,4]{2,1,0:T(8,128)S(1)}, u32[]{:S(2)}, u32[]{:S(2)}) collective-permute-start(f32[6,16,4]{2,1,0:T(8,128)S(1)} %get-tuple-element.485), channel_id=1, source_target_pairs={{2,0},{4,2},{6,4},{8,6},{10,8},{12,10},{14,12},{16,14},{18,16},{20... | collective-permute-start | bytes 4616 | tf_op jit(solution)/shard_map/ppermute | solution.py:25
  25.6 3.9 %collective-permute-done.5 = f32[6,4,1032]{2,1,0:T(4,128)S(1)} collective-permute-done((f32[6,4,1032]{2,1,0:T(4,128)S(1)}, f32[6,4,1032]{2,1,0:T(4,128)S(1)}, u32[]{:S(2)}, u32[]{:S(2)}) %collective-permute-start.5) | collective-permute-done | bytes 99104 | tf_op jit(solution)/shard_map/ppermute | solution.py:25
  29.7 3.5 %while.65 = (s32[]{:T(128)}, f32[3,24,1032]{2,1,0:T(8,128)S(1)}, s32[]{:T(128)}, f32[3,24,1032]{2,1,0:T(8,128)S(1)}, s32[]{:T(128)}, /*index=5*/s32[]{:T(128)}) while((s32[]{:T(128)}, f32[3,24,1032]{2,1,0:T(8,128)S(1)}, s32[]{:T(128)}, f32[3,24,1032]{2,1,0:T(8,128)S(1)}, s32[]{:T(128)}, /*index=5*/s32[]{:T(128)}) %tuple.162), condition=%wide.region_1.2_spmd.clone, body=%wide.region_0.1_spmd.clone.sunk | while | flops 668858 | bytes 1486345 | solution.py:68
  33.3 4.4 %collective-permute-start.7 = (f32[3,16,1]{2,1,0:T(8,128)S(1)}, f32[3,16,1]{2,1,0:T(8,128)S(1)}, u32[]{:S(2)}, u32[]{:S(2)}) collective-permute-start(f32[3,16,1]{2,1,0:T(8,128)S(1)} %get-tuple-element.488), channel_id=1, source_target_pairs={{2,0},{4,2},{6,4},{8,6},{10,8},{12,10},{14,12},{16,14},{18,16},{20... | collective-permute-start | bytes 584 | tf_op jit(solution)/shard_map/ppermute | solution.py:25
  42.4 4.2 %collective-permute-done.9 = f32[3,1,1026]{2,1,0:T(1,128)S(1)} collective-permute-done((f32[3,1,1026]{2,1,0:T(1,128)S(1)}, f32[3,1,1026]{2,1,0:T(1,128)S(1)}, u32[]{:S(2)}, u32[]{:S(2)}) %collective-permute-start.9) | collective-permute-done | bytes 12344 | tf_op jit(solution)/shard_map/ppermute | solution.py:25
  46.9 14.0 %reshape.71 = f32[3,8,2,512,2]{4,3,2,1,0:T(8,128)} reshape(f32[3,16,1024]{2,1,0:T(8,128)S(1)} %fusion.52) | data formatting | bytes 393216 | tf_op jit(solution)/shard_map/reshape | solution.py:74
  60.9 6.3 %reduce_sum.18 = f32[3,8,512]{2,1,0:T(8,128)S(1)} reduce(f32[3,8,2,512,2]{4,3,2,1,0:T(8,128)} %reshape.71, f32[]{:T(128)} %constant.174.clone.1), dimensions={2,4}, to_apply=%region_2.3 | reduce | flops 36864 | bytes 245764 | tf_op jit(solution)/shard_map/reduce_sum | solution.py:74
  67.3 4.4 %collective-permute-start.11 = (f32[6,8,4]{2,1,0:T(8,128)S(1)}, f32[6,8,4]{2,1,0:T(8,128)S(1)}, u32[]{:S(2)}, u32[]{:S(2)}) collective-permute-start(f32[6,8,4]{2,1,0:T(8,128)S(1)} %get-tuple-element.528), channel_id=1, source_target_pairs={{2,0},{4,2},{6,4},{8,6},{10,8},{12,10},{14,12},{16,14},{18,16},{20... | collective-permute-start | bytes 2312 | tf_op jit(solution)/shard_map/ppermute | solution.py:25
  76.9 4.3 %collective-permute-done.13 = f32[6,4,520]{2,1,0:T(4,128)S(1)} collective-permute-done((f32[6,4,520]{2,1,0:T(4,128)S(1)}, f32[6,4,520]{2,1,0:T(4,128)S(1)}, u32[]{:S(2)}, u32[]{:S(2)}) %collective-permute-start.13) | collective-permute-done | bytes 49952 | tf_op jit(solution)/shard_map/ppermute | solution.py:25
  81.3 2.5 %while.66 = (s32[]{:T(128)}, f32[3,16,520]{2,1,0:T(8,128)S(1)}, s32[]{:T(128)}, f32[3,16,520]{2,1,0:T(8,128)S(1)}, s32[]{:T(128)}, /*index=5*/s32[]{:T(128)}) while((s32[]{:T(128)}, f32[3,16,520]{2,1,0:T(8,128)S(1)}, s32[]{:T(128)}, f32[3,16,520]{2,1,0:T(8,128)S(1)}, s32[]{:T(128)}, /*index=5*/s32[]{:T(128)}) %tuple.165), condition=%wide.region_4.5_spmd.clone, body=%wide.region_3.4_spmd.clone.sunk | while | flops 249682 | bytes 499401 | solution.py:68
  84.0 4.4 %collective-permute-start.15 = (f32[3,8,1]{2,1,0:T(8,128)S(1)}, f32[3,8,1]{2,1,0:T(8,128)S(1)}, u32[]{:S(2)}, u32[]{:S(2)}) collective-permute-start(f32[3,8,1]{2,1,0:T(8,128)S(1)} %get-tuple-element.506), channel_id=1, source_target_pairs={{2,0},{4,2},{6,4},{8,6},{10,8},{12,10},{14,12},{16,14},{18,16},{20... | collective-permute-start | bytes 296 | tf_op jit(solution)/shard_map/ppermute | solution.py:25
  92.9 4.2 %collective-permute-done.17 = f32[3,1,514]{2,1,0:T(1,128)S(1)} collective-permute-done((f32[3,1,514]{2,1,0:T(1,128)S(1)}, f32[3,1,514]{2,1,0:T(1,128)S(1)}, u32[]{:S(2)}, u32[]{:S(2)}) %collective-permute-start.17) | collective-permute-done | bytes 6200 | tf_op jit(solution)/shard_map/ppermute | solution.py:25
  97.8 3.9 %reshape.72 = f32[3,4,2,256,2]{4,3,2,1,0:T(8,128)S(1)} reshape(f32[3,8,512]{2,1,0:T(8,128)} %fusion.78) | data formatting | bytes 98304 | tf_op jit(solution)/shard_map/reshape | solution.py:74
  102.3 4.4 %collective-permute-start.19 = (f32[6,4,4]{2,1,0:T(4,128)S(1)}, f32[6,4,4]{2,1,0:T(4,128)S(1)}, u32[]{:S(2)}, u32[]{:S(2)}) collective-permute-start(f32[6,4,4]{2,1,0:T(4,128)S(1)} %get-tuple-element.538), channel_id=1, source_target_pairs={{2,0},{4,2},{6,4},{8,6},{10,8},{12,10},{14,12},{16,14},{18,16},{20... | collective-permute-start | bytes 1160 | tf_op jit(solution)/shard_map/ppermute | solution.py:25
  111.5 4.2 %collective-permute-done.21 = f32[6,4,264]{2,1,0:T(4,128)S(1)} collective-permute-done((f32[6,4,264]{2,1,0:T(4,128)S(1)}, f32[6,4,264]{2,1,0:T(4,128)S(1)}, u32[]{:S(2)}, u32[]{:S(2)}) %collective-permute-start.21) | collective-permute-done | bytes 25376 | tf_op jit(solution)/shard_map/ppermute | solution.py:25
  115.9 2.2 %while.67 = (s32[]{:T(128)}, f32[3,12,264]{2,1,0:T(8,128)S(1)}, s32[]{:T(128)}, f32[3,12,264]{2,1,0:T(8,128)S(1)}, s32[]{:T(128)}, /*index=5*/s32[]{:T(128)}) while((s32[]{:T(128)}, f32[3,12,264]{2,1,0:T(8,128)S(1)}, s32[]{:T(128)}, f32[3,12,264]{2,1,0:T(8,128)S(1)}, s32[]{:T(128)}, /*index=5*/s32[]{:T(128)}) %tuple.168), condition=%wide.region_7.8_spmd.clone, body=%wide.region_6.7_spmd.clone.sunk | while | flops 95102 | bytes 190249 | solution.py:68
  118.2 4.4 %collective-permute-start.23 = (f32[3,4,1]{2,1,0:T(4,128)S(1)}, f32[3,4,1]{2,1,0:T(4,128)S(1)}, u32[]{:S(2)}, u32[]{:S(2)}) collective-permute-start(f32[3,4,1]{2,1,0:T(4,128)S(1)} %get-tuple-element.518), channel_id=1, source_target_pairs={{2,0},{4,2},{6,4},{8,6},{10,8},{12,10},{14,12},{16,14},{18,16},{20... | collective-permute-start | bytes 152 | tf_op jit(solution)/shard_map/ppermute | solution.py:25
  127.2 4.0 %collective-permute-done.25 = f32[3,1,258]{2,1,0:T(1,128)S(1)} collective-permute-done((f32[3,1,258]{2,1,0:T(1,128)S(1)}, f32[3,1,258]{2,1,0:T(1,128)S(1)}, u32[]{:S(2)}, u32[]{:S(2)}) %collective-permute-start.25) | collective-permute-done | bytes 3128 | tf_op jit(solution)/shard_map/ppermute | solution.py:25
  132.1 1.8 copy.8
  133.8 2.7 %reshape.73 = f32[3,8,512]{2,1,0:T(8,128)} reshape(f32[3,4,2,256,2]{4,3,2,1,0:T(8,128)S(1)} %copy.8) | data formatting | bytes 98304 | tf_op jit(solution)/shard_map/reshape | solution.py:89
  137.7 4.4 %collective-permute-start.27 = (f32[6,8,4]{2,1,0:T(8,128)S(1)}, f32[6,8,4]{2,1,0:T(8,128)S(1)}, u32[]{:S(2)}, u32[]{:S(2)}) collective-permute-start(f32[6,8,4]{2,1,0:T(8,128)S(1)} %get-tuple-element.510), channel_id=1, source_target_pairs={{2,0},{4,2},{6,4},{8,6},{10,8},{12,10},{14,12},{16,14},{18,16},{20... | collective-permute-start | bytes 2312 | tf_op jit(solution)/shard_map/ppermute | solution.py:25
  147.3 4.3 %collective-permute-done.29 = f32[6,4,520]{2,1,0:T(4,128)S(1)} collective-permute-done((f32[6,4,520]{2,1,0:T(4,128)S(1)}, f32[6,4,520]{2,1,0:T(4,128)S(1)}, u32[]{:S(2)}, u32[]{:S(2)}) %collective-permute-start.29) | collective-permute-done | bytes 49952 | tf_op jit(solution)/shard_map/ppermute | solution.py:25
  151.7 2.4 %while.68 = (s32[]{:T(128)}, f32[3,16,520]{2,1,0:T(8,128)S(1)}, s32[]{:T(128)}, f32[3,16,520]{2,1,0:T(8,128)S(1)}, s32[]{:T(128)}, /*index=5*/s32[]{:T(128)}) while((s32[]{:T(128)}, f32[3,16,520]{2,1,0:T(8,128)S(1)}, s32[]{:T(128)}, f32[3,16,520]{2,1,0:T(8,128)S(1)}, s32[]{:T(128)}, /*index=5*/s32[]{:T(128)}) %tuple.171), condition=%wide.region_9.10_spmd.clone, body=%wide.region_8.9_spmd.clone.sunk | while | flops 249682 | bytes 499401 | solution.py:68
  154.4 4.4 %collective-permute-start.31 = (f32[3,8,1]{2,1,0:T(8,128)S(1)}, f32[3,8,1]{2,1,0:T(8,128)S(1)}, u32[]{:S(2)}, u32[]{:S(2)}) collective-permute-start(f32[3,8,1]{2,1,0:T(8,128)S(1)} %get-tuple-element.502), channel_id=1, source_target_pairs={{2,0},{4,2},{6,4},{8,6},{10,8},{12,10},{14,12},{16,14},{18,16},{20... | collective-permute-start | bytes 296 | tf_op jit(solution)/shard_map/ppermute | solution.py:25
  163.2 4.2 %collective-permute-done.33 = f32[3,1,514]{2,1,0:T(1,128)S(1)} collective-permute-done((f32[3,1,514]{2,1,0:T(1,128)S(1)}, f32[3,1,514]{2,1,0:T(1,128)S(1)}, u32[]{:S(2)}, u32[]{:S(2)}) %collective-permute-start.33) | collective-permute-done | bytes 6200 | tf_op jit(solution)/shard_map/ppermute | solution.py:25
  167.8 6.7 %copy.9 = f32[3,8,2,512,2]{4,3,2,1,0:T(8,128)} copy(f32[3,8,2,512,2]{3,1,0,4,2:T(8,128)S(1)} %pad_maximum_fusion.10) | data formatting | bytes 393216 | tf_op jit(solution)/shard_map/stack | solution.py:87
  174.5 9.8 %reshape.74 = f32[3,16,1024]{2,1,0:T(8,128)S(1)} reshape(f32[3,8,2,512,2]{4,3,2,1,0:T(8,128)} %copy.9) | data formatting | bytes 393216 | tf_op jit(solution)/shard_map/reshape | solution.py:89
  184.6 4.4 %collective-permute-start.35 = (f32[6,16,4]{2,1,0:T(8,128)S(1)}, f32[6,16,4]{2,1,0:T(8,128)S(1)}, u32[]{:S(2)}, u32[]{:S(2)}) collective-permute-start(f32[6,16,4]{2,1,0:T(8,128)S(1)} %get-tuple-element.483), channel_id=1, source_target_pairs={{2,0},{4,2},{6,4},{8,6},{10,8},{12,10},{14,12},{16,14},{18,16},{20... | collective-permute-start | bytes 4616 | tf_op jit(solution)/shard_map/ppermute | solution.py:25
  195.1 4.3 %collective-permute-done.37 = f32[6,4,1032]{2,1,0:T(4,128)S(1)} collective-permute-done((f32[6,4,1032]{2,1,0:T(4,128)S(1)}, f32[6,4,1032]{2,1,0:T(4,128)S(1)}, u32[]{:S(2)}, u32[]{:S(2)}) %collective-permute-start.37) | collective-permute-done | bytes 99104 | tf_op jit(solution)/shard_map/ppermute | solution.py:25
  199.6 3.5 %while.69 = (s32[]{:T(128)}, f32[3,24,1032]{2,1,0:T(8,128)S(1)}, s32[]{:T(128)}, f32[3,24,1032]{2,1,0:T(8,128)S(1)}, s32[]{:T(128)}, /*index=5*/s32[]{:T(128)}) while((s32[]{:T(128)}, f32[3,24,1032]{2,1,0:T(8,128)S(1)}, s32[]{:T(128)}, f32[3,24,1032]{2,1,0:T(8,128)S(1)}, s32[]{:T(128)}, /*index=5*/s32[]{:T(128)}) %tuple.174), condition=%wide.region_11.12_spmd.clone, body=%wide.region_10.11_spmd.clone.sunk | while | flops 668858 | bytes 1486345 | solution.py:68
  (162 shorter events, 58.1 us)
Async XLA Ops:
  2.2 10.9 %collective-permute-start.1 = (f32[3,1,1024]{2,1,0:T(1,128)S(1)}, f32[3,1,1024]{2,1,0:T(1,128)S(1)}, u32[]{:S(2)}, u32[]{:S(2)}) collective-permute-start(f32[3,1,1024]{2,1,0:T(1,128)S(1)} %slice.515), channel_id=1, source_target_pairs={{0,1},{2,3},{4,5},{6,7},{8,9},{10,11},{12,13},{14,15},{16,17},{18,... | collective-permute-start | bytes 36872 | tf_op jit(solution)/shard_map/ppermute | solution.py:41
  7.1 6.0 %collective-permute-start = (f32[3,16,1]{2,1,0:T(8,128)S(1)}, f32[3,16,1]{2,1,0:T(8,128)S(1)}, u32[]{:S(2)}, u32[]{:S(2)}) collective-permute-start(f32[3,16,1]{2,1,0:T(8,128)S(1)} %slice.513), channel_id=1, source_target_pairs={{30,0},{0,2},{2,4},{4,6},{6,8},{8,10},{10,12},{12,14},{14,16},{16,... | collective-permute-start | bytes 584 | tf_op jit(solution)/shard_map/ppermute | solution.py:35
  15.0 6.2 %collective-permute-start.2 = (f32[6,16,4]{2,1,0:T(8,128)S(1)}, f32[6,16,4]{2,1,0:T(8,128)S(1)}, u32[]{:S(2)}, u32[]{:S(2)}) collective-permute-start(f32[6,16,4]{2,1,0:T(8,128)S(1)} %get-tuple-element.486), channel_id=1, source_target_pairs={{0,2},{2,4},{4,6},{6,8},{8,10},{10,12},{12,14},{14,16},{16,18},{18... | collective-permute-start | bytes 4616 | tf_op jit(solution)/shard_map/ppermute | solution.py:23
  15.0 6.2 %collective-permute-start.3 = (f32[6,16,4]{2,1,0:T(8,128)S(1)}, f32[6,16,4]{2,1,0:T(8,128)S(1)}, u32[]{:S(2)}, u32[]{:S(2)}) collective-permute-start(f32[6,16,4]{2,1,0:T(8,128)S(1)} %get-tuple-element.485), channel_id=1, source_target_pairs={{2,0},{4,2},{6,4},{8,6},{10,8},{12,10},{14,12},{16,14},{18,16},{20... | collective-permute-start | bytes 4616 | tf_op jit(solution)/shard_map/ppermute | solution.py:25
  21.6 4.0 %collective-permute-start.4 = (f32[6,4,1032]{2,1,0:T(4,128)S(1)}, f32[6,4,1032]{2,1,0:T(4,128)S(1)}, u32[]{:S(2)}, u32[]{:S(2)}) collective-permute-start(f32[6,4,1032]{2,1,0:T(4,128)S(1)} %get-tuple-element.481), channel_id=1, source_target_pairs={{0,1},{2,3},{4,5},{6,7},{8,9},{10,11},{12,13},{14,15},{16,17},{18,... | collective-permute-start | bytes 297224 | tf_op jit(solution)/shard_map/ppermute | solution.py:23
  22.9 6.6 %collective-permute-start.5 = (f32[6,4,1032]{2,1,0:T(4,128)S(1)}, f32[6,4,1032]{2,1,0:T(4,128)S(1)}, u32[]{:S(2)}, u32[]{:S(2)}) collective-permute-start(f32[6,4,1032]{2,1,0:T(4,128)S(1)} %get-tuple-element.482), channel_id=1, source_target_pairs={{1,0},{3,2},{5,4},{7,6},{9,8},{11,10},{13,12},{15,14},{17,16},{19,... | collective-permute-start | bytes 297224 | tf_op jit(solution)/shard_map/ppermute | solution.py:25
  33.2 6.0 %collective-permute-start.6 = (f32[3,16,1]{2,1,0:T(8,128)S(1)}, f32[3,16,1]{2,1,0:T(8,128)S(1)}, u32[]{:S(2)}, u32[]{:S(2)}) collective-permute-start(f32[3,16,1]{2,1,0:T(8,128)S(1)} %get-tuple-element.487), channel_id=1, source_target_pairs={{0,2},{2,4},{4,6},{6,8},{8,10},{10,12},{12,14},{14,16},{16,18},{18... | collective-permute-start | bytes 584 | tf_op jit(solution)/shard_map/ppermute | solution.py:23
  33.3 6.0 %collective-permute-start.7 = (f32[3,16,1]{2,1,0:T(8,128)S(1)}, f32[3,16,1]{2,1,0:T(8,128)S(1)}, u32[]{:S(2)}, u32[]{:S(2)}) collective-permute-start(f32[3,16,1]{2,1,0:T(8,128)S(1)} %get-tuple-element.488), channel_id=1, source_target_pairs={{2,0},{4,2},{6,4},{8,6},{10,8},{12,10},{14,12},{16,14},{18,16},{20... | collective-permute-start | bytes 584 | tf_op jit(solution)/shard_map/ppermute | solution.py:25
  41.0 5.6 %collective-permute-start.9 = (f32[3,1,1026]{2,1,0:T(1,128)S(1)}, f32[3,1,1026]{2,1,0:T(1,128)S(1)}, u32[]{:S(2)}, u32[]{:S(2)}) collective-permute-start(f32[3,1,1026]{2,1,0:T(1,128)S(1)} %get-tuple-element.494), channel_id=1, source_target_pairs={{1,0},{3,2},{5,4},{7,6},{9,8},{11,10},{13,12},{15,14},{17,16},{19,... | collective-permute-start | bytes 36944 | tf_op jit(solution)/shard_map/ppermute | solution.py:25
  67.3 6.0 %collective-permute-start.10 = (f32[6,8,4]{2,1,0:T(8,128)S(1)}, f32[6,8,4]{2,1,0:T(8,128)S(1)}, u32[]{:S(2)}, u32[]{:S(2)}) collective-permute-start(f32[6,8,4]{2,1,0:T(8,128)S(1)} %get-tuple-element.527), channel_id=1, source_target_pairs={{0,2},{2,4},{4,6},{6,8},{8,10},{10,12},{12,14},{14,16},{16,18},{18... | collective-permute-start | bytes 2312 | tf_op jit(solution)/shard_map/ppermute | solution.py:23
  67.3 6.0 %collective-permute-start.11 = (f32[6,8,4]{2,1,0:T(8,128)S(1)}, f32[6,8,4]{2,1,0:T(8,128)S(1)}, u32[]{:S(2)}, u32[]{:S(2)}) collective-permute-start(f32[6,8,4]{2,1,0:T(8,128)S(1)} %get-tuple-element.528), channel_id=1, source_target_pairs={{2,0},{4,2},{6,4},{8,6},{10,8},{12,10},{14,12},{16,14},{18,16},{20... | collective-permute-start | bytes 2312 | tf_op jit(solution)/shard_map/ppermute | solution.py:25
  75.0 6.1 %collective-permute-start.13 = (f32[6,4,520]{2,1,0:T(4,128)S(1)}, f32[6,4,520]{2,1,0:T(4,128)S(1)}, u32[]{:S(2)}, u32[]{:S(2)}) collective-permute-start(f32[6,4,520]{2,1,0:T(4,128)S(1)} %get-tuple-element.508), channel_id=1, source_target_pairs={{1,0},{3,2},{5,4},{7,6},{9,8},{11,10},{13,12},{15,14},{17,16},{19,... | collective-permute-start | bytes 149768 | tf_op jit(solution)/shard_map/ppermute | solution.py:25
  84.0 5.8 %collective-permute-start.14 = (f32[3,8,1]{2,1,0:T(8,128)S(1)}, f32[3,8,1]{2,1,0:T(8,128)S(1)}, u32[]{:S(2)}, u32[]{:S(2)}) collective-permute-start(f32[3,8,1]{2,1,0:T(8,128)S(1)} %get-tuple-element.505), channel_id=1, source_target_pairs={{0,2},{2,4},{4,6},{6,8},{8,10},{10,12},{12,14},{14,16},{16,18},{18... | collective-permute-start | bytes 296 | tf_op jit(solution)/shard_map/ppermute | solution.py:23
  84.0 5.8 %collective-permute-start.15 = (f32[3,8,1]{2,1,0:T(8,128)S(1)}, f32[3,8,1]{2,1,0:T(8,128)S(1)}, u32[]{:S(2)}, u32[]{:S(2)}) collective-permute-start(f32[3,8,1]{2,1,0:T(8,128)S(1)} %get-tuple-element.506), channel_id=1, source_target_pairs={{2,0},{4,2},{6,4},{8,6},{10,8},{12,10},{14,12},{16,14},{18,16},{20... | collective-permute-start | bytes 296 | tf_op jit(solution)/shard_map/ppermute | solution.py:25
  91.5 5.5 %collective-permute-start.17 = (f32[3,1,514]{2,1,0:T(1,128)S(1)}, f32[3,1,514]{2,1,0:T(1,128)S(1)}, u32[]{:S(2)}, u32[]{:S(2)}) collective-permute-start(f32[3,1,514]{2,1,0:T(1,128)S(1)} %get-tuple-element.520), channel_id=1, source_target_pairs={{1,0},{3,2},{5,4},{7,6},{9,8},{11,10},{13,12},{15,14},{17,16},{19,... | collective-permute-start | bytes 18512 | tf_op jit(solution)/shard_map/ppermute | solution.py:25
  102.3 5.8 %collective-permute-start.18 = (f32[6,4,4]{2,1,0:T(4,128)S(1)}, f32[6,4,4]{2,1,0:T(4,128)S(1)}, u32[]{:S(2)}, u32[]{:S(2)}) collective-permute-start(f32[6,4,4]{2,1,0:T(4,128)S(1)} %get-tuple-element.537), channel_id=1, source_target_pairs={{0,2},{2,4},{4,6},{6,8},{8,10},{10,12},{12,14},{14,16},{16,18},{18... | collective-permute-start | bytes 1160 | tf_op jit(solution)/shard_map/ppermute | solution.py:23
  102.3 5.8 %collective-permute-start.19 = (f32[6,4,4]{2,1,0:T(4,128)S(1)}, f32[6,4,4]{2,1,0:T(4,128)S(1)}, u32[]{:S(2)}, u32[]{:S(2)}) collective-permute-start(f32[6,4,4]{2,1,0:T(4,128)S(1)} %get-tuple-element.538), channel_id=1, source_target_pairs={{2,0},{4,2},{6,4},{8,6},{10,8},{12,10},{14,12},{16,14},{18,16},{20... | collective-permute-start | bytes 1160 | tf_op jit(solution)/shard_map/ppermute | solution.py:25
  109.9 5.9 %collective-permute-start.21 = (f32[6,4,264]{2,1,0:T(4,128)S(1)}, f32[6,4,264]{2,1,0:T(4,128)S(1)}, u32[]{:S(2)}, u32[]{:S(2)}) collective-permute-start(f32[6,4,264]{2,1,0:T(4,128)S(1)} %pad_maximum_fusion.26), channel_id=1, source_target_pairs={{1,0},{3,2},{5,4},{7,6},{9,8},{11,10},{13,12},{15,14},{17,16},{19,... | collective-permute-start | bytes 76040 | tf_op jit(solution)/shard_map/ppermute | solution.py:25
  118.2 5.8 %collective-permute-start.22 = (f32[3,4,1]{2,1,0:T(4,128)S(1)}, f32[3,4,1]{2,1,0:T(4,128)S(1)}, u32[]{:S(2)}, u32[]{:S(2)}) collective-permute-start(f32[3,4,1]{2,1,0:T(4,128)S(1)} %get-tuple-element.517), channel_id=1, source_target_pairs={{0,2},{2,4},{4,6},{6,8},{8,10},{10,12},{12,14},{14,16},{16,18},{18... | collective-permute-start | bytes 152 | tf_op jit(solution)/shard_map/ppermute | solution.py:23
  118.2 5.8 %collective-permute-start.23 = (f32[3,4,1]{2,1,0:T(4,128)S(1)}, f32[3,4,1]{2,1,0:T(4,128)S(1)}, u32[]{:S(2)}, u32[]{:S(2)}) collective-permute-start(f32[3,4,1]{2,1,0:T(4,128)S(1)} %get-tuple-element.518), channel_id=1, source_target_pairs={{2,0},{4,2},{6,4},{8,6},{10,8},{12,10},{14,12},{16,14},{18,16},{20... | collective-permute-start | bytes 152 | tf_op jit(solution)/shard_map/ppermute | solution.py:25
  125.7 5.5 %collective-permute-start.25 = (f32[3,1,258]{2,1,0:T(1,128)S(1)}, f32[3,1,258]{2,1,0:T(1,128)S(1)}, u32[]{:S(2)}, u32[]{:S(2)}) collective-permute-start(f32[3,1,258]{2,1,0:T(1,128)S(1)} %get-tuple-element.536), channel_id=1, source_target_pairs={{1,0},{3,2},{5,4},{7,6},{9,8},{11,10},{13,12},{15,14},{17,16},{19,... | collective-permute-start | bytes 9296 | tf_op jit(solution)/shard_map/ppermute | solution.py:25
  137.7 6.0 %collective-permute-start.26 = (f32[6,8,4]{2,1,0:T(8,128)S(1)}, f32[6,8,4]{2,1,0:T(8,128)S(1)}, u32[]{:S(2)}, u32[]{:S(2)}) collective-permute-start(f32[6,8,4]{2,1,0:T(8,128)S(1)} %get-tuple-element.509), channel_id=1, source_target_pairs={{0,2},{2,4},{4,6},{6,8},{8,10},{10,12},{12,14},{14,16},{16,18},{18... | collective-permute-start | bytes 2312 | tf_op jit(solution)/shard_map/ppermute | solution.py:23
  137.7 6.0 %collective-permute-start.27 = (f32[6,8,4]{2,1,0:T(8,128)S(1)}, f32[6,8,4]{2,1,0:T(8,128)S(1)}, u32[]{:S(2)}, u32[]{:S(2)}) collective-permute-start(f32[6,8,4]{2,1,0:T(8,128)S(1)} %get-tuple-element.510), channel_id=1, source_target_pairs={{2,0},{4,2},{6,4},{8,6},{10,8},{12,10},{14,12},{16,14},{18,16},{20... | collective-permute-start | bytes 2312 | tf_op jit(solution)/shard_map/ppermute | solution.py:25
  143.8 3.5 %collective-permute-start.28 = (f32[6,4,520]{2,1,0:T(4,128)S(1)}, f32[6,4,520]{2,1,0:T(4,128)S(1)}, u32[]{:S(2)}, u32[]{:S(2)}) collective-permute-start(f32[6,4,520]{2,1,0:T(4,128)S(1)} %get-tuple-element.503), channel_id=1, source_target_pairs={{0,1},{2,3},{4,5},{6,7},{8,9},{10,11},{12,13},{14,15},{16,17},{18,... | collective-permute-start | bytes 149768 | tf_op jit(solution)/shard_map/ppermute | solution.py:23
  145.4 6.1 %collective-permute-start.29 = (f32[6,4,520]{2,1,0:T(4,128)S(1)}, f32[6,4,520]{2,1,0:T(4,128)S(1)}, u32[]{:S(2)}, u32[]{:S(2)}) collective-permute-start(f32[6,4,520]{2,1,0:T(4,128)S(1)} %get-tuple-element.504), channel_id=1, source_target_pairs={{1,0},{3,2},{5,4},{7,6},{9,8},{11,10},{13,12},{15,14},{17,16},{19,... | collective-permute-start | bytes 149768 | tf_op jit(solution)/shard_map/ppermute | solution.py:25
  154.3 5.8 %collective-permute-start.30 = (f32[3,8,1]{2,1,0:T(8,128)S(1)}, f32[3,8,1]{2,1,0:T(8,128)S(1)}, u32[]{:S(2)}, u32[]{:S(2)}) collective-permute-start(f32[3,8,1]{2,1,0:T(8,128)S(1)} %get-tuple-element.501), channel_id=1, source_target_pairs={{0,2},{2,4},{4,6},{6,8},{8,10},{10,12},{12,14},{14,16},{16,18},{18... | collective-permute-start | bytes 296 | tf_op jit(solution)/shard_map/ppermute | solution.py:23
  154.4 5.8 %collective-permute-start.31 = (f32[3,8,1]{2,1,0:T(8,128)S(1)}, f32[3,8,1]{2,1,0:T(8,128)S(1)}, u32[]{:S(2)}, u32[]{:S(2)}) collective-permute-start(f32[3,8,1]{2,1,0:T(8,128)S(1)} %get-tuple-element.502), channel_id=1, source_target_pairs={{2,0},{4,2},{6,4},{8,6},{10,8},{12,10},{14,12},{16,14},{18,16},{20... | collective-permute-start | bytes 296 | tf_op jit(solution)/shard_map/ppermute | solution.py:25
  161.9 5.5 %collective-permute-start.33 = (f32[3,1,514]{2,1,0:T(1,128)S(1)}, f32[3,1,514]{2,1,0:T(1,128)S(1)}, u32[]{:S(2)}, u32[]{:S(2)}) collective-permute-start(f32[3,1,514]{2,1,0:T(1,128)S(1)} %get-tuple-element.516), channel_id=1, source_target_pairs={{1,0},{3,2},{5,4},{7,6},{9,8},{11,10},{13,12},{15,14},{17,16},{19,... | collective-permute-start | bytes 18512 | tf_op jit(solution)/shard_map/ppermute | solution.py:25
  184.6 6.2 %collective-permute-start.34 = (f32[6,16,4]{2,1,0:T(8,128)S(1)}, f32[6,16,4]{2,1,0:T(8,128)S(1)}, u32[]{:S(2)}, u32[]{:S(2)}) collective-permute-start(f32[6,16,4]{2,1,0:T(8,128)S(1)} %get-tuple-element.484), channel_id=1, source_target_pairs={{0,2},{2,4},{4,6},{6,8},{8,10},{10,12},{12,14},{14,16},{16,18},{18... | collective-permute-start | bytes 4616 | tf_op jit(solution)/shard_map/ppermute | solution.py:23
  184.6 6.2 %collective-permute-start.35 = (f32[6,16,4]{2,1,0:T(8,128)S(1)}, f32[6,16,4]{2,1,0:T(8,128)S(1)}, u32[]{:S(2)}, u32[]{:S(2)}) collective-permute-start(f32[6,16,4]{2,1,0:T(8,128)S(1)} %get-tuple-element.483), channel_id=1, source_target_pairs={{2,0},{4,2},{6,4},{8,6},{10,8},{12,10},{14,12},{16,14},{18,16},{20... | collective-permute-start | bytes 4616 | tf_op jit(solution)/shard_map/ppermute | solution.py:25
  191.1 4.0 %collective-permute-start.36 = (f32[6,4,1032]{2,1,0:T(4,128)S(1)}, f32[6,4,1032]{2,1,0:T(4,128)S(1)}, u32[]{:S(2)}, u32[]{:S(2)}) collective-permute-start(f32[6,4,1032]{2,1,0:T(4,128)S(1)} %get-tuple-element.479), channel_id=1, source_target_pairs={{0,1},{2,3},{4,5},{6,7},{8,9},{10,11},{12,13},{14,15},{16,17},{18,... | collective-permute-start | bytes 297224 | tf_op jit(solution)/shard_map/ppermute | solution.py:23
  192.8 6.6 %collective-permute-start.37 = (f32[6,4,1032]{2,1,0:T(4,128)S(1)}, f32[6,4,1032]{2,1,0:T(4,128)S(1)}, u32[]{:S(2)}, u32[]{:S(2)}) collective-permute-start(f32[6,4,1032]{2,1,0:T(4,128)S(1)} %get-tuple-element.480), channel_id=1, source_target_pairs={{1,0},{3,2},{5,4},{7,6},{9,8},{11,10},{13,12},{15,14},{17,16},{19,... | collective-permute-start | bytes 297224 | tf_op jit(solution)/shard_map/ppermute | solution.py:25
  (9 other events, 95.4 us)
where the time goes:
time: 208 us; the launch traced here: 204 us
  starting transfers between devices  70.8 us (34%)
  waiting for transfers between devices  58.7 us (28%)
  local copies, waits for them, and re-layouts  43.3 us (21%)
  other arithmetic  18.9 us (9%)
  loops' own time  11.5 us (6%)
    ppermute x18, starting transfers between devices, with_halo(): lax.ppermute(head, axis, [((i + 1) % count, i) for i in range(ends)])  51.7 us
    ppermute x18, waiting for transfers between devices, with_halo(): lax.ppermute(head, axis, [((i + 1) % count, i) for i in range(ends)])  37.8 us
    reshape x2, local copies, waits for them, and re-layouts, restrict(): return field.reshape(chans, rows // 2, 2, cols // 2, 2).mean(axis=(2, 4))  17.9 us
    ppermute x18, waiting for transfers between devices, with_halo(): lax.ppermute(tail, axis, [(i, (i + 1) % count) for i in range(ends)])  14.9 us
    ppermute x18, starting transfers between devices, with_halo(): lax.ppermute(tail, axis, [(i, (i + 1) % count) for i in range(ends)])  14.2 us
    reshape x2, local copies, waits for them, and re-layouts, prolong_from(): return stacked.reshape(chans, rows * 2, cols * 2)  12.6 us
    another operation x5, loops' own time, smooth(): value = lax.fori_loop(0, count, sweep_wide, value)  11.5 us
    another operation x2, local copies, waits for them, and re-layouts, prolong_from(): jnp.stack([jnp.stack([f00, f01], -1), jnp.stack([f10, f11], -1)], 2)  8.5 us
  transfers between devices with their start and end apart: 38, of which 24 were waited for; matrix products, arithmetic and copies ran while one was open for 1% of the time, Pallas kernels for 0%

commit v1 on v0

v1 whole, which is shorter than its diff:
```python
import functools

import jax
import jax.numpy as jnp
from jax import lax
from jax.experimental import pallas as pl
from jax.experimental.pallas import tpu as pltpu
from jax.sharding import PartitionSpec as P

SCREENING = 0.02
DAMPING = 0.8
LANES = 128
HALF = LANES // 2
VMEM = pl.BlockSpec(memory_space=pltpu.VMEM)
SMEM = pl.BlockSpec(memory_space=pltpu.SMEM)


def diagonal(scale):
    return SCREENING + 4.0 * scale


def rows_of(value):
    return lax.broadcasted_iota(jnp.int32, value.shape, 0)


def north_of(value):
    return jnp.where(rows_of(value) == 0, 0.0, pltpu.roll(value, 1, 0))


def south_of(value):
    last = value.shape[0] - 1
    return jnp.where(rows_of(value) == last, 0.0, pltpu.roll(value, last, 0))


def west_of(value):
    return pltpu.roll(value, 1, 1)


def east_of(value):
    return pltpu.roll(value, value.shape[1] - 1, 1)


def around(value):
    return (north_of(value) + south_of(value)) + (west_of(value) + east_of(value))


def sweep(value, right, scale, inside):
    diag = diagonal(scale)
    value = (1.0 - DAMPING) * value + (DAMPING / diag) * right + (DAMPING * scale / diag) * around(value)
    return value if inside is None else value * inside


def residual(value, right, scale):
    return right - diagonal(scale) * value + scale * around(value)


def two_parts(value):
    high = value.astype(jnp.bfloat16)
    return high, (value - high.astype(jnp.float32)).astype(jnp.bfloat16)


def moved(value, places):
    high, low = two_parts(value)
    dot = functools.partial(jnp.dot, preferred_element_type=jnp.float32)
    return dot(high, places) + dot(low, places)


def places_of(shape, wanted):
    source = lax.broadcasted_iota(jnp.int32, shape, 0)
    target = lax.broadcasted_iota(jnp.int32, shape, 1)
    return wanted(source, target).astype(jnp.float32).astype(jnp.bfloat16)


def halo_coarse(fine):
    return jnp.where(fine < HALF, fine // 2, HALF + fine // 2)


def pair_columns(fields):
    own = places_of((2 * LANES, LANES), lambda source, target: source // 2 == target)
    halo = places_of((LANES, LANES), lambda source, target: halo_coarse(source) == target)
    rows, cols = fields[0].shape
    blocks = (cols - LANES) // (2 * LANES)
    cut = [f[:, k * 2 * LANES:(k + 1) * 2 * LANES] for f in fields for k in range(blocks)]
    packed = moved(jnp.concatenate(cut, 0), own)
    edges = moved(jnp.concatenate([f[:, cols - LANES:] for f in fields], 0), halo)
    out = []
    for i in range(len(fields)):
        parts = [packed[(i * blocks + k) * rows:(i * blocks + k + 1) * rows] for k in range(blocks)]
        out.append(jnp.concatenate(parts + [edges[i * rows:(i + 1) * rows]], 1))
    return out


def spread_columns(fields):
    own = places_of((2 * LANES, 2 * LANES), lambda source, target: source == target // 2 + LANES * (target % 2))
    halo = places_of((2 * LANES, LANES), lambda source, target: source == halo_coarse(target) + LANES * (target % 2))
    rows, cols = fields[0].shape
    blocks = (cols - LANES) // LANES
    west = [0.75 * f + 0.25 * west_of(f) for f in fields]
    east = [0.75 * f + 0.25 * east_of(f) for f in fields]

    def cut(k):
        span = slice(k * LANES, (k + 1) * LANES)
        return [jnp.concatenate([w[:, span], e[:, span]], 1) for w, e in zip(west, east)]

    own_cut = [cut(k) for k in range(blocks)]
    packed = moved(jnp.concatenate([own_cut[k][i] for i in range(len(fields)) for k in range(blocks)], 0), own)
    edges = moved(jnp.concatenate(cut(blocks), 0), halo)
    out = []
    for i in range(len(fields)):
        parts = [packed[(i * blocks + k) * rows:(i * blocks + k + 1) * rows] for k in range(blocks)]
        out.append(jnp.concatenate(parts + [edges[i * rows:(i + 1) * rows]], 1))
    return out


def restrict(fields, paired_ref):
    rows = fields[0].shape[0]
    out = []
    for i, paired in enumerate(pair_columns(fields)):
        halves = []
        for k, tile in enumerate(tiles(paired)):
            paired_ref[i, k] = tile
            north = paired_ref[i, k, pl.ds(0, rows // 2, stride=2), :]
            south = paired_ref[i, k, pl.ds(1, rows // 2, stride=2), :]
            halves.append(0.25 * (north + south))
        out.append(jnp.concatenate(halves, 1))
    return out


def prolong(fields, fine_ref, first):
    rows = fields[0].shape[0]
    norths = [0.75 * f + 0.25 * north_of(f) for f in fields]
    souths = [0.75 * f + 0.25 * south_of(f) for f in fields]
    spread = spread_columns(norths + souths)
    for i in range(len(fields)):
        for k, (north, south) in enumerate(zip(tiles(spread[i]), tiles(spread[len(fields) + i]))):
            fine_ref[i, k, pl.ds(first, rows, stride=2), :] = north
            fine_ref[i, k, pl.ds(first + 1, rows, stride=2), :] = south


def wide_rows(fine_ref, chan, start, rows):
    return jnp.concatenate([fine_ref[chan, k, pl.ds(start, rows), :] for k in range(fine_ref.shape[1])], 1)


def selected(grad, labels):
    out = jnp.zeros(grad.shape[1:], jnp.float32)
    for source in range(grad.shape[0]):
        out = jnp.where((labels == source)[None], grad[source], out)
    return out


def edge_kernel(*refs):
    first, last, out_ref = refs[:4], refs[4:8], refs[8]
    inner = lax.broadcasted_iota(jnp.int32, (1, 1, LANES), 2) < HALF
    target, grad_x, grad_y, labels = (
        jnp.where(inner if f.ndim > 2 else inner[0], f[...], l[...]) for f, l in zip(first, last)
    )
    chans = target.shape[0]
    out_ref[:chans] = target
    out_ref[chans:2 * chans] = selected(grad_x, labels)
    out_ref[2 * chans:] = selected(grad_y, labels)


def edges(target, grad_x, grad_y, labels):
    chans, rows, cols = target.shape
    tile = cols // LANES - 1
    arrays = (target, grad_x, grad_y, labels)

    def spec(array, place):
        lead = (0,) * (array.ndim - 1)
        return pl.BlockSpec(array.shape[:-1] + (LANES,), lambda _: lead + (place,))

    return pl.pallas_call(
        edge_kernel,
        grid=(1,),
        in_specs=[spec(a, 0) for a in arrays] + [spec(a, tile) for a in arrays],
        out_specs=pl.BlockSpec((3 * chans, rows, LANES), lambda _: (0, 0, 0)),
        out_shape=jax.ShapeDtypeStruct((3 * chans, rows, LANES), jnp.float32),
        name="edges",
    )(*arrays, *arrays)


def window_of(rows, parts):
    spare = 8
    return rows + (2 * spare if parts > 2 else spare if parts == 2 else 0)


def own_start(parts, place):
    return 0 if parts == 1 else 8 * place if parts == 2 else 8


def band_mask(window, parts, place, rows):
    if parts <= 2:
        return None
    row = lax.broadcasted_iota(jnp.int32, (window, 1), 0) + place * rows - 8
    return ((row >= 0) & (row < parts * rows)).astype(jnp.float32)


def tiles(value):
    return [value[:, k * LANES:(k + 1) * LANES] for k in range(value.shape[1] // LANES)]


def pack(value8, right4, coarse12):
    out = tiles(value8)
    halves = tiles(right4) + tiles(coarse12[8:])
    if len(halves) % 2:
        halves.append(halves[-1])
    out += tiles(coarse12[:8])
    out += [jnp.concatenate([halves[k], halves[k + 1]], 0) for k in range(0, len(halves), 2)]
    return out


def packed_tiles(fine_tiles, coarse_tiles):
    return fine_tiles + coarse_tiles + (fine_tiles + coarse_tiles + 1) // 2


def unpack(tile, fine_tiles, coarse_tiles):
    value8 = jnp.concatenate([tile(k) for k in range(fine_tiles)], 1)
    top = jnp.concatenate([tile(fine_tiles + k) for k in range(coarse_tiles)], 1)
    halves = []
    for k in range(fine_tiles + coarse_tiles, packed_tiles(fine_tiles, coarse_tiles)):
        both = tile(k)
        halves += [both[:4], both[4:]]
    right4 = jnp.concatenate(halves[:fine_tiles], 1)
    bottom = jnp.concatenate(halves[fine_tiles:fine_tiles + coarse_tiles], 1)
    return value8, right4, jnp.concatenate([top, bottom], 0)


def down_kernel(parts, sweeps, target, grad_x, grad_y, labels, even, odd, *refs):
    if parts == 2:
        packed_ref, *refs = refs
    value_ref, right_ref, coarse_ref, v_ref, b_ref, paired_ref = refs
    chans, rows, cols = target.shape
    window = value_ref.shape[1]
    place = lax.axis_index("lat")
    second = lax.axis_index("lon") % 2 == 1
    start = own_start(parts, place)
    if parts == 2:
        start = pl.multiple_of(start, 8)
    inside = band_mask(window, parts, place, rows)
    inner = lax.broadcasted_iota(jnp.int32, (rows, LANES), 1) < HALF
    marks = labels[...]
    count = sweeps[0]
    scale = 1.0

    def halo(chan):
        a, b = even[chan], odd[chan]
        return jnp.where(inner != second, a, b)

    def chosen(grad, chan):
        out = jnp.zeros((rows, cols), jnp.float32)
        for source in range(grad.shape[0]):
            out = jnp.where(marks == source, grad[source, chan], out)
        return out

    if window > rows:
        v_ref[...] = jnp.zeros_like(v_ref)
        b_ref[...] = jnp.zeros_like(b_ref)
    resid = []
    for chan in range(chans):
        own = jnp.concatenate([target[chan], halo(chan)], 1)
        sel_x = jnp.concatenate([chosen(grad_x, chan), halo(chans + chan)], 1)
        sel_y = jnp.concatenate([chosen(grad_y, chan), halo(2 * chans + chan)], 1)
        right = SCREENING * own - ((sel_x - west_of(sel_x)) + (sel_y - north_of(sel_y)))
        v_ref[chan, pl.ds(start, rows), :] = own
        b_ref[chan, pl.ds(start, rows), :] = right
        if window > rows:
            below = pltpu.roll(sel_y[rows - 8:], 1, 0)
            b_ref[chan, pl.ds(start + rows, 8), :] = jnp.where(rows_of(below) == 0, below, 0.0)
        right = b_ref[chan, :window, :]
        if inside is not None:
            right = right * inside
        right_ref[chan] = right
        value = lax.fori_loop(
            0, count, lambda _, v, chan=chan: sweep(v, right_ref[chan], scale, inside), v_ref[chan, :window, :]
        )
        value_ref[chan] = value
        left = residual(value, right, scale)
        resid.append(left if inside is None else left * inside)
    coarse = restrict(resid, paired_ref)
    for chan in range(chans):
        coarse_ref[chan] = coarse[chan]
        if parts == 2:
            north = place == 0
            value8 = jnp.where(north, value_ref[chan, 12:20, :], value_ref[chan, 4:12, :])
            right4 = jnp.where(north, right_ref[chan, 13:17, :], right_ref[chan, 8:12, :])
            for k, tile in enumerate(pack(value8, right4, coarse[chan])):
                packed_ref[chan, k] = tile


def down(parts, sweeps, target, grad_x, grad_y, labels, even, odd):
    chans, rows, cols = target.shape
    window = window_of(rows, parts)
    wide, half = cols + LANES, cols // 2 + LANES
    f32 = functools.partial(jax.ShapeDtypeStruct, dtype=jnp.float32)
    outs = [f32((chans, window, wide)), f32((chans, window, wide)), f32((chans, window // 2, half))]
    if parts == 2:
        outs.insert(0, f32((chans, packed_tiles(wide // LANES, half // LANES), 8, LANES)))
    spare = 8 if window > rows else 0
    return pl.pallas_call(
        functools.partial(down_kernel, parts),
        in_specs=[SMEM] + [VMEM] * 6,
        out_specs=[VMEM] * len(outs),
        out_shape=outs,
        scratch_shapes=[
            pltpu.VMEM((chans, window + spare, wide), jnp.float32),
            pltpu.VMEM((chans, window + spare, wide), jnp.float32),
            pltpu.VMEM((chans, half // LANES, window, LANES), jnp.float32),
        ],
        compiler_params=pltpu.CompilerParams(vmem_limit_bytes=32 * 2**20),
        name="down",
    )(sweeps, target, grad_x, grad_y, labels, even, odd)


def joined(place, own, other, height):
    gap = jnp.zeros((height - own.shape[0], own.shape[1]), jnp.float32)
    top, bottom = (lambda v: jnp.concatenate([v, gap], 0)), (lambda v: jnp.concatenate([gap, v], 0))
    return jnp.where(place == 0, top(own) + bottom(other), bottom(own) + top(other))


def up_kernel(parts, sweeps, value_ref, right_ref, coarse_ref, *refs):
    if parts == 2:
        packed_ref, *refs = refs
    out_ref, b0_ref, b1_ref, b2_ref, pair_ref, fix1_ref, fix0_ref = refs
    chans, rows, cols = out_ref.shape
    window, wide = value_ref.shape[1:]
    half = b1_ref.shape[2]
    place = lax.axis_index("lat")
    inside = band_mask(window, parts, place, rows)
    north = place == 0

    def widened(value, upper, lower):
        def at(first):
            last = window - first - value.shape[0]
            pads = [jnp.zeros((n, wide), jnp.float32) for n in (first, last)]
            return jnp.concatenate([pads[0], value, pads[1]], 0)

        return jnp.where(north, at(upper), at(lower))

    def received(chan):
        return unpack(lambda k: packed_ref[chan, k], wide // LANES, half // LANES)

    for chan in range(chans):
        if parts == 2:
            b1_ref[chan] = joined(place, coarse_ref[chan], received(chan)[2], b1_ref.shape[1])
        else:
            b1_ref[chan] = coarse_ref[chan]

    def smoothed(values, right_ref, count, scale, inside=None):
        def step(_, values):
            return tuple(sweep(v, right_ref[i], scale, inside) for i, v in enumerate(values))

        return lax.fori_loop(0, count, step, tuple(values))

    def from_zero(right_ref, count, scale):
        first = [(DAMPING / diagonal(scale)) * right_ref[i] for i in range(chans)]
        return smoothed(first, right_ref, count - 1, scale)

    mid = from_zero(b1_ref, sweeps[1], 0.25)
    low = restrict([residual(mid[i], b1_ref[i], 0.25) for i in range(chans)], pair_ref)
    for i in range(chans):
        b2_ref[i] = low[i]
    fix2 = from_zero(b2_ref, sweeps[2], 0.0625)
    prolong(fix2, fix1_ref, 0)
    mid = smoothed([mid[i] + wide_rows(fix1_ref, i, 0, mid[i].shape[0]) for i in range(chans)], b1_ref, sweeps[1], 0.25)
    spare = 8 if parts > 2 else 0
    if spare:
        fix0_ref[...] = jnp.zeros_like(fix0_ref)
    prolong(mid, fix0_ref, spare)
    start = own_start(parts, place)
    shown = 0 if parts == 1 else pl.multiple_of((8 if parts == 2 else rows) * place, 8)
    for i in range(chans):
        value = value_ref[i] + wide_rows(fix0_ref, i, shown, window)
        if parts == 2:
            value8, right4, _ = received(i)
            value = value + widened(value8, 12, 4)
            b0_ref[i] = right_ref[i] + widened(right4, 16, 5)
        else:
            b0_ref[i] = right_ref[i]
        value = lax.fori_loop(0, sweeps[0], lambda _, v, i=i: sweep(v, b0_ref[i], 1.0, inside), value)
        if parts == 2:
            out_ref[i] = jnp.where(place == 0, value[:rows, :cols], value[8:8 + rows, :cols])
        else:
            out_ref[i] = value[start:start + rows, :cols]


def up(parts, shape, sweeps, value, right, coarse, *packed):
    chans, rows, cols = shape
    window, wide = value.shape[1:]
    full = parts * rows
    f32 = functools.partial(pltpu.VMEM, dtype=jnp.float32)
    spare = 16 if parts > 2 else 0
    return pl.pallas_call(
        functools.partial(up_kernel, parts),
        in_specs=[SMEM] + [VMEM] * (3 + len(packed)),
        out_specs=VMEM,
        out_shape=jax.ShapeDtypeStruct(shape, jnp.float32),
        scratch_shapes=[
            f32(value.shape),
            f32((chans, full // 2, cols // 2 + LANES)),
            f32((chans, full // 4, cols // 4 + LANES)),
            f32((chans, cols // 4 // LANES + 1, full // 2, LANES)),
            f32((chans, cols // 2 // LANES + 1, full // 2, LANES)),
            f32((chans, wide // LANES, full + spare, LANES)),
        ],
        compiler_params=pltpu.CompilerParams(vmem_limit_bytes=48 * 2**20),
        name="up",
    )(sweeps, value, right, coarse, *packed)


def local(target, grad_x, grad_y, labels, sweeps):
    parts, around_globe = lax.axis_size("lat"), lax.axis_size("lon")
    tile = edges(target, grad_x, grad_y, labels)
    swap_odd = [(i, (i + 1 if i % 2 else i - 1) % around_globe) for i in range(around_globe)]
    swap_even = [(i, i - 1 if i % 2 else i + 1) for i in range(around_globe)]
    odd = lax.ppermute(tile, "lon", swap_odd)
    even = lax.ppermute(tile, "lon", swap_even)
    found = down(parts, sweeps, target, grad_x, grad_y, labels, even, odd)
    if parts == 2:
        packed, value, right, coarse = found
        packed = lax.ppermute(packed, "lat", [(0, 1), (1, 0)])
        return up(parts, target.shape, sweeps, value, right, coarse, packed)
    value, right, coarse = found
    if parts > 2:
        rows = target.shape[1]
        southward = [(i, i + 1) for i in range(parts - 1)]
        northward = [(i + 1, i) for i in range(parts - 1)]

        def shared(field):
            north = lax.ppermute(field[:, rows:], "lat", southward)
            south = lax.ppermute(field[:, :16], "lat", northward)
            zeros = jnp.zeros_like(field[:, :16])
            return field + jnp.concatenate([north, zeros], 1) + jnp.concatenate([zeros, south], 1)

        value, right = shared(value), shared(right)
        every = lax.all_gather(coarse, "lat")
        step = rows // 2
        total = jnp.zeros((coarse.shape[0], parts * step + 8, coarse.shape[2]), jnp.float32)
        for i in range(parts):
            total = total.at[:, i * step:i * step + step + 8].add(every[i])
        coarse = total[:, 4:-4]
    return up(parts, target.shape, sweeps, value, right, coarse)


def solution(mesh):
    in_specs = (
        P(None, "lat", "lon"),
        P(None, None, "lat", "lon"),
        P(None, None, "lat", "lon"),
        P("lat", "lon"),
        P(),
    )
    out_specs = P(None, "lat", "lon")
    return jax.shard_map(local, mesh=mesh, in_specs=in_specs, out_specs=out_specs, check_vma=False)
```

time: 208 us -> 24.9 us (0.12); the launches traced: 204 us -> 24.5 us
  starting transfers between devices: 70.8 us -> 7.42 us
  waiting for transfers between devices: 58.7 us -> 7.86 us
  local copies, waits for them, and re-layouts: 43.3 us -> 0.02 us
  other arithmetic: 18.9 us -> 0 us
  loops' own time: 11.5 us -> 0 us
  Pallas kernels: 0 us -> 9.19 us
    ppermute x38 -> x3, starting transfers between devices: 70.8 us -> 7.42 us  [the longest x1 5.47 us: local(): odd = lax.ppermute(tile, 'lon', swap_odd)]
    ppermute x38 -> x3, waiting for transfers between devices: 58.7 us -> 7.86 us  [the longest x1 5.56 us: local(): packed = lax.ppermute(packed, 'lat', [(0, 1), (1, 0)])]
    reshape x4 -> x0, local copies, waits for them, and re-layouts: 30.5 us -> none  [the longest x2 17.9 us: restrict(): return field.reshape(chans, rows // 2, 2, cols // 2, 2).mean(axis=(2, 4))]
    another operation x5 -> x0, loops' own time: 11.5 us -> none  [smooth(): value = lax.fori_loop(0, count, sweep_wide, value)]
    pallas_call x0 -> x3, Pallas kernels: none -> 9.19 us  [the longest x1 4.5 us: up(): pl.pallas_call(functools.partial(up_kernel, parts), in_specs=[SMEM] + [VM...]
    another operation x2 -> x0, local copies, waits for them, and re-layouts: 8.5 us -> none  [prolong_from(): jnp.stack([jnp.stack([f00, f01], -1), jnp.stack([f10, f11], -1)], 2)]
    reduce_sum x2 -> x0, other arithmetic: 6.77 us -> none  [restrict(): return field.reshape(chans, rows // 2, 2, cols // 2, 2).mean(axis=(2, 4))]
    slice x24 -> x0, local copies, waits for them, and re-layouts: 3.41 us -> none  [the longest x1 1.43 us: cycle(): count = sweeps[level]]
  transfers between devices with their start and end apart: 38 -> 3, of which waited for: 24 -> 2; matrix products, arithmetic and copies ran while one was open for 1% -> 0% of each run, Pallas kernels for 0% -> 0%
where the time goes in v1:
time: 24.9 us; the launch traced here: 24.5 us
  Pallas kernels  9.19 us (37%)
  waiting for transfers between devices  7.86 us (32%)
  starting transfers between devices  7.42 us (30%)
    ppermute x1, waiting for transfers between devices, local(): packed = lax.ppermute(packed, 'lat', [(0, 1), (1, 0)])  5.56 us
    ppermute x1, starting transfers between devices, local(): odd = lax.ppermute(tile, 'lon', swap_odd)  5.47 us
    pallas_call x1, Pallas kernels, up(): pl.pallas_call(functools.partial(up_kernel, parts), in_specs=[SMEM] + [VM...  4.5 us
    pallas_call x1, Pallas kernels, down(): pl.pallas_call(functools.partial(down_kernel, parts), in_specs=[SMEM] + [...  3.05 us
    ppermute x1, waiting for transfers between devices, local(): odd = lax.ppermute(tile, 'lon', swap_odd)  2.3 us
    ppermute x1, starting transfers between devices, local(): packed = lax.ppermute(packed, 'lat', [(0, 1), (1, 0)])  1.95 us
    pallas_call x1, Pallas kernels, edges(): pl.pallas_call(edge_kernel, grid=(1,), in_specs=[spec(a, 0) for a in arra...  1.64 us
  transfers between devices with their start and end apart: 3, of which 2 were waited for; matrix products, arithmetic and copies ran while one was open for 0% of the time, Pallas kernels for 0%

profile of v1, /device:TPU:0, one launch (start us, length us, event | category | flops | bytes accessed | tf_op | source)
XLA Modules:
  0.0 24.5 jit_solution(3427622552799569330)
XLA Ops:
  0.0 0.0 copy-start.3
  0.0 0.0 copy-start.1
  0.0 0.0 copy-start
  0.0 0.0 copy-start.2
  0.0 0.0 copy-start.4
  0.0 1.6 %edges.1 = f32[9,16,128]{2,1,0:T(8,128)} custom-call(f32[3,16,1024]{2,1,0:T(8,128)} %target.1, f32[2,3,16,1024]{3,2,1,0:T(8,128)} %grad_x.1, f32[2,3,16,1024]{3,2,1,0:T(8,128)} %grad_y.1, s32[16,1024]{1,0:T(8,128)} %labels.1, f32[3,16,1024]{2,1,0:T(8,128)} %target.1, f32[2,3,16,1024]{3,2,1,0:T(8,128)} %grad_x.1, f32[2,3,16,1024]{3,2,1,0:T(8,128)} %grad_y.1, ...), custom_call_target="tpu_custom_call" | custom-call | tf_op jit(solution)/shard_map/edges/pallas_call | solution.py:172
  1.7 5.5 %collective-permute-start.1 = (f32[9,16,128]{2,1,0:T(8,128)}, f32[9,16,128]{2,1,0:T(8,128)S(1)}, u32[]{:S(2)}, u32[]{:S(2)}) collective-permute-start(f32[9,16,128]{2,1,0:T(8,128)} %edges.1), channel_id=1, source_target_pairs={{0,30},{2,4},{4,2},{6,8},{8,6},{10,12},{12,10},{14,16},{16,14},{18... | collective-permute-start | bytes 221192 | tf_op jit(solution)/shard_map/ppermute | solution.py:415
  7.1 0.0 collective-permute-start
  7.1 2.3 %collective-permute-done.1.odd = f32[9,16,128]{2,1,0:T(8,128)S(1)} collective-permute-done((f32[9,16,128]{2,1,0:T(8,128)}, f32[9,16,128]{2,1,0:T(8,128)S(1)}, u32[]{:S(2)}, u32[]{:S(2)}) %collective-permute-start.1) | collective-permute-done | bytes 73760 | tf_op jit(solution)/shard_map/ppermute | solution.py:415
  9.4 0.0 collective-permute-done.even
  9.4 0.0 copy-done.3
  9.4 0.0 copy-done.1
  9.4 0.0 copy-done
  9.4 0.0 copy-done.2
  9.4 0.0 copy-done.4
  9.5 3.1 %down.1 = (f32[3,21,8,128]{3,2,1,0:T(8,128)S(1)}, f32[3,24,1152]{2,1,0:T(8,128)S(1)}, f32[3,24,1152]{2,1,0:T(8,128)S(1)}, f32[3,12,640]{2,1,0:T(8,128)S(1)}) custom-call(s32[3]{0:T(128)S(1)} %copy-done.4, f32[3,16,1024]{2,1,0:T(8,128)S(1)} %copy-done.2, f32[2,3,16,1024]{3,2,1,0:T(8,128)S(1)} %copy-done, f32[2,3,16,1024]{3,2,1,0:T(8,128)S(1)} %copy-done.1, ...), custom_call_target="tpu_custom_call" | custom-call | tf_op jit(solution)/shard_map/down/pallas_call | solution.py:299
  12.5 2.0 %collective-permute-start.2 = (f32[3,21,8,128]{3,2,1,0:T(8,128)S(1)}, f32[3,21,8,128]{3,2,1,0:T(8,128)S(1)}, u32[]{:S(2)}, u32[]{:S(2)}) collective-permute-start(f32[3,21,8,128]{3,2,1,0:T(8,128)S(1)} %get-tuple-element.12), channel_id=1, source_target_pairs={{0,1},{1,0},{2,3},{3,2},{4,5},{5,4},{6,7},{7,6},{8,9},{9,8},{10,11... | collective-permute-start | bytes 774152 | tf_op jit(solution)/shard_map/ppermute | solution.py:420
  14.5 5.6 %collective-permute-done.2.refs_0_ = f32[3,21,8,128]{3,2,1,0:T(8,128)S(1)} collective-permute-done((f32[3,21,8,128]{3,2,1,0:T(8,128)S(1)}, f32[3,21,8,128]{3,2,1,0:T(8,128)S(1)}, u32[]{:S(2)}, u32[]{:S(2)}) %collective-permute-start.2) | collective-permute-done | bytes 258080 | tf_op jit(solution)/shard_map/ppermute | solution.py:420
  20.0 4.5 %up.1 = f32[3,16,1024]{2,1,0:T(8,128)} custom-call(s32[3]{0:T(128)S(1)} %copy-done.4, f32[3,24,1152]{2,1,0:T(8,128)S(1)} %get-tuple-element.9.value_ref, f32[3,24,1152]{2,1,0:T(8,128)S(1)} %get-tuple-element.10.right_ref, f32[3,12,640]{2,1,0:T(8,128)S(1)} %get-tuple-element.11.coarse_ref, f32[3,21,8,128]{3,2,1,0:T(8,128)S(1)} %collective-permute-done.2.refs_0_), custom_call_target="tpu_custom_call" | custom-call | tf_op jit(solution)/shard_map/up/pallas_call | solution.py:392
Async XLA Ops:
  0.0 9.4 %copy-start.3 = (s32[16,1024]{1,0:T(8,128)S(1)}, s32[16,1024]{1,0:T(8,128)}, u32[]{:S(2)}) copy-start(s32[16,1024]{1,0:T(8,128)} %labels.1) | copy-start | bytes 196612
  0.0 9.4 %copy-start.1 = (f32[2,3,16,1024]{3,2,1,0:T(8,128)S(1)}, f32[2,3,16,1024]{3,2,1,0:T(8,128)}, u32[]{:S(2)}) copy-start(f32[2,3,16,1024]{3,2,1,0:T(8,128)} %grad_y.1) | copy-start | bytes 1179652
  0.0 9.4 %copy-start = (f32[2,3,16,1024]{3,2,1,0:T(8,128)S(1)}, f32[2,3,16,1024]{3,2,1,0:T(8,128)}, u32[]{:S(2)}) copy-start(f32[2,3,16,1024]{3,2,1,0:T(8,128)} %grad_x.1) | copy-start | bytes 1179652
  0.0 9.4 %copy-start.2 = (f32[3,16,1024]{2,1,0:T(8,128)S(1)}, f32[3,16,1024]{2,1,0:T(8,128)}, u32[]{:S(2)}) copy-start(f32[3,16,1024]{2,1,0:T(8,128)} %target.1) | copy-start | bytes 589828
  0.0 9.4 %copy-start.4 = (s32[3]{0:T(128)S(1)}, s32[3]{0:T(128)}, u32[]{:S(2)}) copy-start(s32[3]{0:T(128)} %sweeps.3) | copy-start | bytes 40
  1.7 7.8 %collective-permute-start.1 = (f32[9,16,128]{2,1,0:T(8,128)}, f32[9,16,128]{2,1,0:T(8,128)S(1)}, u32[]{:S(2)}, u32[]{:S(2)}) collective-permute-start(f32[9,16,128]{2,1,0:T(8,128)} %edges.1), channel_id=1, source_target_pairs={{0,30},{2,4},{4,2},{6,8},{8,6},{10,12},{12,10},{14,16},{16,14},{18... | collective-permute-start | bytes 221192 | tf_op jit(solution)/shard_map/ppermute | solution.py:415
  7.1 2.3 %collective-permute-start = (f32[9,16,128]{2,1,0:T(8,128)}, f32[9,16,128]{2,1,0:T(8,128)S(1)}, u32[]{:S(2)}, u32[]{:S(2)}) collective-permute-start(f32[9,16,128]{2,1,0:T(8,128)} %edges.1), channel_id=1, source_target_pairs={{0,2},{2,0},{4,6},{6,4},{8,10},{10,8},{12,14},{14,12},{16,18},{18,... | collective-permute-start | bytes 221192 | tf_op jit(solution)/shard_map/ppermute | solution.py:416
  12.5 7.5 %collective-permute-start.2 = (f32[3,21,8,128]{3,2,1,0:T(8,128)S(1)}, f32[3,21,8,128]{3,2,1,0:T(8,128)S(1)}, u32[]{:S(2)}, u32[]{:S(2)}) collective-permute-start(f32[3,21,8,128]{3,2,1,0:T(8,128)S(1)} %get-tuple-element.12), channel_id=1, source_target_pairs={{0,1},{1,0},{2,3},{3,2},{4,5},{5,4},{6,7},{7,6},{8,9},{9,8},{10,11... | collective-permute-start | bytes 774152 | tf_op jit(solution)/shard_map/ppermute | solution.py:420

commit v2 on v1

--- a/solution.py
+++ b/solution.py
@@ -141,44 +141,6 @@
     return jnp.concatenate([fine_ref[chan, k, pl.ds(start, rows), :] for k in range(fine_ref.shape[1])], 1)
 
 
-def selected(grad, labels):
-    out = jnp.zeros(grad.shape[1:], jnp.float32)
-    for source in range(grad.shape[0]):
-        out = jnp.where((labels == source)[None], grad[source], out)
-    return out
-
-
-def edge_kernel(*refs):
-    first, last, out_ref = refs[:4], refs[4:8], refs[8]
-    inner = lax.broadcasted_iota(jnp.int32, (1, 1, LANES), 2) < HALF
-    target, grad_x, grad_y, labels = (
-        jnp.where(inner if f.ndim > 2 else inner[0], f[...], l[...]) for f, l in zip(first, last)
-    )
-    chans = target.shape[0]
-    out_ref[:chans] = target
-    out_ref[chans:2 * chans] = selected(grad_x, labels)
-    out_ref[2 * chans:] = selected(grad_y, labels)
-
-
-def edges(target, grad_x, grad_y, labels):
-    chans, rows, cols = target.shape
-    tile = cols // LANES - 1
-    arrays = (target, grad_x, grad_y, labels)
-
-    def spec(array, place):
-        lead = (0,) * (array.ndim - 1)
-        return pl.BlockSpec(array.shape[:-1] + (LANES,), lambda _: lead + (place,))
-
-    return pl.pallas_call(
-        edge_kernel,
-        grid=(1,),
-        in_specs=[spec(a, 0) for a in arrays] + [spec(a, tile) for a in arrays],
-        out_specs=pl.BlockSpec((3 * chans, rows, LANES), lambda _: (0, 0, 0)),
-        out_shape=jax.ShapeDtypeStruct((3 * chans, rows, LANES), jnp.float32),
-        name="edges",
-    )(*arrays, *arrays)
-
-
 def window_of(rows, parts):
     spare = 8
     return rows + (2 * spare if parts > 2 else spare if parts == 2 else 0)
@@ -197,6 +159,10 @@
 
 def tiles(value):
     return [value[:, k * LANES:(k + 1) * LANES] for k in range(value.shape[1] // LANES)]
+
+
+def lanes_of(tile):
+    return lax.broadcasted_iota(jnp.int32, tile.shape, len(tile.shape) - 1)
 
 
 def pack(value8, right4, coarse12):
@@ -225,10 +191,53 @@
     return value8, right4, jnp.concatenate([top, bottom], 0)
 
 
-def down_kernel(parts, sweeps, target, grad_x, grad_y, labels, even, odd, *refs):
-    if parts == 2:
-        packed_ref, *refs = refs
-    value_ref, right_ref, coarse_ref, v_ref, b_ref, paired_ref = refs
+def eastward(value):
+    own = value[..., -2 * LANES:-LANES]
+    return jnp.where(lanes_of(own) < HALF, value[..., -LANES:], own)
+
+
+def westward(value):
+    own = value[..., :LANES]
+    return jnp.where(lanes_of(own) < HALF, own, value[..., -LANES:])
+
+
+def with_edges(value, from_west, from_east):
+    inner = lanes_of(from_west) < HALF
+    first = value[..., :LANES] + jnp.where(inner, from_west, 0.0)
+    last = value[..., -2 * LANES:-LANES] + jnp.where(inner, 0.0, from_east)
+    halo = value[..., -LANES:] + jnp.where(inner, from_east, from_west)
+    return jnp.concatenate([first, value[..., LANES:-2 * LANES], last, halo], value.ndim - 1)
+
+
+VALUE_AT, RIGHT_AT = 48, 80
+
+
+def taller(value, rows):
+    missing = rows - value.shape[0]
+    return jnp.concatenate([value, jnp.zeros((missing, value.shape[1]), value.dtype)], 0) if missing else value
+
+
+def three_in_one(value, right, coarse, rows):
+    value, right, coarse = (taller(v, rows) for v in (value, right, coarse))
+    lane = lanes_of(value)
+    at = lambda first: (lane >= first) & (lane < first + 16)
+    out = jnp.where(at(VALUE_AT), pltpu.roll(value, VALUE_AT + 8, 1), coarse)
+    return jnp.where(at(RIGHT_AT), pltpu.roll(right, RIGHT_AT + 8, 1), out)
+
+
+def one_to_three(tile, value_rows, right_rows, coarse_rows):
+    lane = lanes_of(tile)
+    ends = lambda width: (lane < width) | (lane >= LANES - width)
+    value = jnp.where(ends(8), pltpu.roll(tile, LANES - VALUE_AT - 8, 1), 0.0)
+    right = jnp.where(ends(8), pltpu.roll(tile, LANES - RIGHT_AT - 8, 1), 0.0)
+    coarse = jnp.where(ends(32), tile, 0.0)
+    return value[:value_rows], right[:right_rows], coarse[:coarse_rows]
+
+
+def down_kernel(parts, sweeps, target, grad_x, grad_y, labels, *refs):
+    outs, scratch = refs[:8 if parts == 2 else 3], refs[8 if parts == 2 else 3:]
+    value_ref, right_ref, coarse_ref = outs[:3]
+    target_v, grad_x_v, grad_y_v, labels_v, v_ref, b_ref, paired_ref, sems = scratch
     chans, rows, cols = target.shape
     window = value_ref.shape[1]
     place = lax.axis_index("lat")
@@ -237,29 +246,40 @@
     if parts == 2:
         start = pl.multiple_of(start, 8)
     inside = band_mask(window, parts, place, rows)
-    inner = lax.broadcasted_iota(jnp.int32, (rows, LANES), 1) < HALF
-    marks = labels[...]
     count = sweeps[0]
     scale = 1.0
 
-    def halo(chan):
-        a, b = even[chan], odd[chan]
-        return jnp.where(inner != second, a, b)
+    marks_copy = pltpu.make_async_copy(labels, labels_v, sems.at[chans, 0])
+    marks_copy.start()
+    copies = []
+    for chan in range(chans):
+        copies.append([
+            pltpu.make_async_copy(target.at[chan], target_v.at[chan], sems.at[chan, 0]),
+            pltpu.make_async_copy(grad_x.at[:, chan], grad_x_v.at[:, chan], sems.at[chan, 1]),
+            pltpu.make_async_copy(grad_y.at[:, chan], grad_y_v.at[:, chan], sems.at[chan, 2]),
+        ])
+        for copy in copies[-1]:
+            copy.start()
+    if window > rows:
+        v_ref[...] = jnp.zeros_like(v_ref)
+        b_ref[...] = jnp.zeros_like(b_ref)
+    marks_copy.wait()
 
     def chosen(grad, chan):
+        marks = labels_v[...]
         out = jnp.zeros((rows, cols), jnp.float32)
         for source in range(grad.shape[0]):
             out = jnp.where(marks == source, grad[source, chan], out)
         return out
 
-    if window > rows:
-        v_ref[...] = jnp.zeros_like(v_ref)
-        b_ref[...] = jnp.zeros_like(b_ref)
+    blank = jnp.zeros((rows, LANES), jnp.float32)
     resid = []
     for chan in range(chans):
-        own = jnp.concatenate([target[chan], halo(chan)], 1)
-        sel_x = jnp.concatenate([chosen(grad_x, chan), halo(chans + chan)], 1)
-        sel_y = jnp.concatenate([chosen(grad_y, chan), halo(2 * chans + chan)], 1)
+        for copy in copies[chan]:
+            copy.wait()
+        own = jnp.concatenate([target_v[chan], blank], 1)
+        sel_x = jnp.concatenate([chosen(grad_x_v, chan), blank], 1)
+        sel_y = jnp.concatenate([chosen(grad_y_v, chan), blank], 1)
         right = SCREENING * own - ((sel_x - west_of(sel_x)) + (sel_y - north_of(sel_y)))
         v_ref[chan, pl.ds(start, rows), :] = own
         b_ref[chan, pl.ds(start, rows), :] = right
@@ -280,35 +300,51 @@
     for chan in range(chans):
         coarse_ref[chan] = coarse[chan]
         if parts == 2:
+            packed_ref, odd_ref, even_ref, odd_across, even_across = outs[3:]
             north = place == 0
-            value8 = jnp.where(north, value_ref[chan, 12:20, :], value_ref[chan, 4:12, :])
-            right4 = jnp.where(north, right_ref[chan, 13:17, :], right_ref[chan, 8:12, :])
+            value, right = value_ref[chan], right_ref[chan]
+            value8 = jnp.where(north, value[12:20], value[4:12])
+            right4 = jnp.where(north, right[13:17], right[8:12])
             for k, tile in enumerate(pack(value8, right4, coarse[chan])):
                 packed_ref[chan, k] = tile
-
-
-def down(parts, sweeps, target, grad_x, grad_y, labels, even, odd):
+            for height, odd, even, fields in (
+                (window, odd_ref, even_ref, (value, right, coarse[chan])),
+                (16, odd_across, even_across, (value8, right4, coarse[chan])),
+            ):
+                east = three_in_one(*[eastward(f) for f in fields], height)
+                west = three_in_one(*[westward(f) for f in fields], height)
+                odd[chan] = jnp.where(second, east, west)
+                even[chan] = jnp.where(second, west, east)
+
+
+def down(parts, sweeps, target, grad_x, grad_y, labels):
     chans, rows, cols = target.shape
     window = window_of(rows, parts)
     wide, half = cols + LANES, cols // 2 + LANES
     f32 = functools.partial(jax.ShapeDtypeStruct, dtype=jnp.float32)
     outs = [f32((chans, window, wide)), f32((chans, window, wide)), f32((chans, window // 2, half))]
     if parts == 2:
-        outs.insert(0, f32((chans, packed_tiles(wide // LANES, half // LANES), 8, LANES)))
+        outs.append(f32((chans, packed_tiles(wide // LANES, half // LANES), 8, LANES)))
+        outs += [f32((chans, window, LANES))] * 2 + [f32((chans, 16, LANES))] * 2
     spare = 8 if window > rows else 0
     return pl.pallas_call(
         functools.partial(down_kernel, parts),
-        in_specs=[SMEM] + [VMEM] * 6,
+        in_specs=[SMEM] + [pl.BlockSpec(memory_space=pl.ANY)] * 4,
         out_specs=[VMEM] * len(outs),
         out_shape=outs,
         scratch_shapes=[
+            pltpu.VMEM(target.shape, jnp.float32),
+            pltpu.VMEM(grad_x.shape, jnp.float32),
+            pltpu.VMEM(grad_y.shape, jnp.float32),
+            pltpu.VMEM(labels.shape, jnp.int32),
             pltpu.VMEM((chans, window + spare, wide), jnp.float32),
             pltpu.VMEM((chans, window + spare, wide), jnp.float32),
             pltpu.VMEM((chans, half // LANES, window, LANES), jnp.float32),
+            pltpu.SemaphoreType.DMA((chans + 1, 3)),
         ],
         compiler_params=pltpu.CompilerParams(vmem_limit_bytes=32 * 2**20),
         name="down",
-    )(sweeps, target, grad_x, grad_y, labels, even, odd)
+    )(sweeps, target, grad_x, grad_y, labels)
 
 
 def joined(place, own, other, height):
@@ -319,7 +355,8 @@
 
 def up_kernel(parts, sweeps, value_ref, right_ref, coarse_ref, *refs):
     if parts == 2:
-        packed_ref, *refs = refs
+        packed_ref, *edge_refs = refs[:5]
+        refs = refs[5:]
     out_ref, b0_ref, b1_ref, b2_ref, pair_ref, fix1_ref, fix0_ref = refs
     chans, rows, cols = out_ref.shape
     window, wide = value_ref.shape[1:]
@@ -336,12 +373,27 @@
 
         return jnp.where(north, at(upper), at(lower))
 
-    def received(chan):
-        return unpack(lambda k: packed_ref[chan, k], wide // LANES, half // LANES)
+    second = lax.axis_index("lon") % 2 == 1
+
+    def sides(odd_ref, even_ref, chan, *heights):
+        odd, even = odd_ref[chan], even_ref[chan]
+        west = one_to_three(jnp.where(second, even, odd), *heights)
+        east = one_to_three(jnp.where(second, odd, even), *heights)
+        return list(zip(west, east))
+
+    def own_part(chan, which):
+        field = (value_ref, right_ref, coarse_ref)[which][chan]
+        if parts != 2:
+            return field
+        return with_edges(field, *sides(*edge_refs[:2], chan, window, window, window // 2)[which])
+
+    def other_part(chan, which):
+        field = unpack(lambda k: packed_ref[chan, k], wide // LANES, half // LANES)[which]
+        return with_edges(field, *sides(*edge_refs[2:], chan, 8, 4, 12)[which])
 
     for chan in range(chans):
         if parts == 2:
-            b1_ref[chan] = joined(place, coarse_ref[chan], received(chan)[2], b1_ref.shape[1])
+            b1_ref[chan] = joined(place, own_part(chan, 2), other_part(chan, 2), b1_ref.shape[1])
         else:
             b1_ref[chan] = coarse_ref[chan]
 
@@ -369,13 +421,12 @@
     start = own_start(parts, place)
     shown = 0 if parts == 1 else pl.multiple_of((8 if parts == 2 else rows) * place, 8)
     for i in range(chans):
-        value = value_ref[i] + wide_rows(fix0_ref, i, shown, window)
+        value = own_part(i, 0) + wide_rows(fix0_ref, i, shown, window)
+        right = own_part(i, 1)
         if parts == 2:
-            value8, right4, _ = received(i)
-            value = value + widened(value8, 12, 4)
-            b0_ref[i] = right_ref[i] + widened(right4, 16, 5)
-        else:
-            b0_ref[i] = right_ref[i]
+            value = value + widened(other_part(i, 0), 12, 4)
+            right = right + widened(other_part(i, 1), 16, 5)
+        b0_ref[i] = right
         value = lax.fori_loop(0, sweeps[0], lambda _, v, i=i: sweep(v, b0_ref[i], 1.0, inside), value)
         if parts == 2:
             out_ref[i] = jnp.where(place == 0, value[:rows, :cols], value[8:8 + rows, :cols])
@@ -409,29 +460,41 @@
 
 def local(target, grad_x, grad_y, labels, sweeps):
     parts, around_globe = lax.axis_size("lat"), lax.axis_size("lon")
-    tile = edges(target, grad_x, grad_y, labels)
-    swap_odd = [(i, (i + 1 if i % 2 else i - 1) % around_globe) for i in range(around_globe)]
-    swap_even = [(i, i - 1 if i % 2 else i + 1) for i in range(around_globe)]
-    odd = lax.ppermute(tile, "lon", swap_odd)
-    even = lax.ppermute(tile, "lon", swap_even)
-    found = down(parts, sweeps, target, grad_x, grad_y, labels, even, odd)
+    value, right, coarse, *sent = down(parts, sweeps, target, grad_x, grad_y, labels)
     if parts == 2:
-        packed, value, right, coarse = found
+        odd = [(i, (i + 1 if i % 2 else i - 1) % around_globe) for i in range(around_globe)]
+        even = [(i, i - 1 if i % 2 else i + 1) for i in range(around_globe)]
+
+        def across(pairs):
+            return [(2 * i + k, 2 * j + 1 - k) for i, j in pairs for k in range(2)]
+
+        packed, odd_edge, even_edge, odd_across, even_across = sent
         packed = lax.ppermute(packed, "lat", [(0, 1), (1, 0)])
-        return up(parts, target.shape, sweeps, value, right, coarse, packed)
-    value, right, coarse = found
+        odd_edge = lax.ppermute(odd_edge, "lon", odd)
+        odd_across = lax.ppermute(odd_across, ("lon", "lat"), across(odd))
+        even_edge = lax.ppermute(even_edge, "lon", even)
+        even_across = lax.ppermute(even_across, ("lon", "lat"), across(even))
+        received = (packed, odd_edge, even_edge, odd_across, even_across)
+        return up(parts, target.shape, sweeps, value, right, coarse, *received)
+
+    def shared_lon(field):
+        from_west = lax.ppermute(eastward(field), "lon", [(i, (i + 1) % around_globe) for i in range(around_globe)])
+        from_east = lax.ppermute(westward(field), "lon", [((i + 1) % around_globe, i) for i in range(around_globe)])
+        return with_edges(field, from_west, from_east)
+
+    value, right, coarse = (shared_lon(f) for f in (value, right, coarse))
     if parts > 2:
         rows = target.shape[1]
         southward = [(i, i + 1) for i in range(parts - 1)]
         northward = [(i + 1, i) for i in range(parts - 1)]
 
-        def shared(field):
+        def shared_lat(field):
             north = lax.ppermute(field[:, rows:], "lat", southward)
             south = lax.ppermute(field[:, :16], "lat", northward)
             zeros = jnp.zeros_like(field[:, :16])
             return field + jnp.concatenate([north, zeros], 1) + jnp.concatenate([zeros, south], 1)
 
-        value, right = shared(value), shared(right)
+        value, right = shared_lat(value), shared_lat(right)
         every = lax.all_gather(coarse, "lat")
         step = rows // 2
         total = jnp.zeros((coarse.shape[0], parts * step + 8, coarse.shape[2]), jnp.float32)

time: 24.9 us -> 28 us (1.12); the launches traced: 24.5 us -> 28 us
  local copies, waits for them, and re-layouts: 0.02 us -> 5.06 us
  waiting for transfers between devices: 7.86 us -> 5.93 us
    ppermute x1, waiting for transfers between devices: 5.56 us -> 0.01 us  [local(): packed = lax.ppermute(packed, 'lat', [(0, 1), (1, 0)])]
    unnamed x10 -> x12, local copies, waits for them, and re-layouts: 0.02 us -> 5.06 us
    ppermute x2 -> x4, waiting for transfers between devices: 2.3 us -> 5.92 us  [the longest x1 5.92 us: local(): odd_across = lax.ppermute(odd_across, ('lon', 'lat'), across(odd))]
    pallas_call x1 -> x0, Pallas kernels: 1.64 us -> none  [edges(): pl.pallas_call(edge_kernel, grid=(1,), in_specs=[spec(a, 0) for a in arra...]
    pallas_call x1, Pallas kernels: 3.05 us -> 4.16 us  [down(): pl.pallas_call(functools.partial(down_kernel, parts), in_specs=[SMEM] + [...]
    ppermute x1, starting transfers between devices: 1.95 us -> 3 us  [local(): packed = lax.ppermute(packed, 'lat', [(0, 1), (1, 0)])]
    ppermute x2 -> x4, starting transfers between devices: 5.47 us -> 4.65 us  [the longest x1 3.71 us: local(): odd_edge = lax.ppermute(odd_edge, 'lon', odd)]
    pallas_call x1, Pallas kernels: 4.5 us -> 5.16 us  [up(): pl.pallas_call(functools.partial(up_kernel, parts), in_specs=[SMEM] + [VM...]
  transfers between devices with their start and end apart: 3 -> 5, of which waited for: 2 -> 1; matrix products, arithmetic and copies ran while one was open for 0% -> 0% of each run, Pallas kernels for 0% -> 0%
where the time goes in v2:
time: 28 us
  Pallas kernels  9.32 us (33%)
  starting transfers between devices  7.65 us (27%)
  waiting for transfers between devices  5.93 us (21%)
  local copies, waits for them, and re-layouts  5.06 us (18%)
    ppermute x1, waiting for transfers between devices, local(): odd_across = lax.ppermute(odd_across, ('lon', 'lat'), across(odd))  5.92 us
    pallas_call x1, Pallas kernels, up(): pl.pallas_call(functools.partial(up_kernel, parts), in_specs=[SMEM] + [VM...  5.16 us
    unnamed x12, local copies, waits for them, and re-layouts  5.06 us
    pallas_call x1, Pallas kernels, down(): pl.pallas_call(functools.partial(down_kernel, parts), in_specs=[SMEM] + [...  4.16 us
    ppermute x1, starting transfers between devices, local(): odd_edge = lax.ppermute(odd_edge, 'lon', odd)  3.71 us
    ppermute x1, starting transfers between devices, local(): packed = lax.ppermute(packed, 'lat', [(0, 1), (1, 0)])  3 us
    ppermute x1, starting transfers between devices, local(): odd_across = lax.ppermute(odd_across, ('lon', 'lat'), across(odd))  0.93 us
  transfers between devices with their start and end apart: 5, of which 1 were waited for; matrix products, arithmetic and copies ran while one was open for 0% of the time, Pallas kernels for 0%

profile of v2, /device:TPU:0, one launch (start us, length us, event | category | flops | bytes accessed | tf_op | source)
XLA Modules:
  0.0 28.0 jit_solution(8470821598073238983)
XLA Ops:
  0.0 0.0 copy-start
  0.0 1.0 %copy-done = f32[2,3,16,1024]{3,2,1,0:T(8,128)S(1)} copy-done((f32[2,3,16,1024]{3,2,1,0:T(8,128)S(1)}, f32[2,3,16,1024]{3,2,1,0:T(8,128)}, u32[]{:S(2)}) %copy-start) | copy-done | bytes 393240
  1.0 0.0 copy-start.1
  1.0 1.0 %copy-done.1 = f32[2,3,16,1024]{3,2,1,0:T(8,128)S(1)} copy-done((f32[2,3,16,1024]{3,2,1,0:T(8,128)S(1)}, f32[2,3,16,1024]{3,2,1,0:T(8,128)}, u32[]{:S(2)}) %copy-start.1) | copy-done | bytes 393240
  2.0 0.0 copy-start.2
  2.0 0.9 %copy-done.2 = f32[3,16,1024]{2,1,0:T(8,128)S(1)} copy-done((f32[3,16,1024]{2,1,0:T(8,128)S(1)}, f32[3,16,1024]{2,1,0:T(8,128)}, u32[]{:S(2)}) %copy-start.2) | copy-done | bytes 196632
  2.9 0.0 copy-start.3
  2.9 0.8 %copy-done.3 = s32[16,1024]{1,0:T(8,128)S(1)} copy-done((s32[16,1024]{1,0:T(8,128)S(1)}, s32[16,1024]{1,0:T(8,128)}, u32[]{:S(2)}) %copy-start.3) | copy-done | bytes 65560
  3.8 0.0 copy-start.4
  3.8 0.7 %copy-done.4 = s32[3]{0:T(128)S(1)} copy-done((s32[3]{0:T(128)S(1)}, s32[3]{0:T(128)}, u32[]{:S(2)}) %copy-start.4) | copy-done | bytes 36
  4.4 4.2 %down.1 = (f32[3,24,1152]{2,1,0:T(8,128)S(1)}, f32[3,24,1152]{2,1,0:T(8,128)S(1)}, f32[3,12,640]{2,1,0:T(8,128)S(1)}, f32[3,21,8,128]{3,2,1,0:T(8,128)S(1)}, f32...) custom-call(s32[3]{0:T(128)S(1)} %copy-done.4, ...), custom_call_target="tpu_custom_call" | custom-call | tf_op jit(solution)/shard_map/down/pallas_call | solution.py:330
  8.6 3.0 %collective-permute-start = (f32[3,21,8,128]{3,2,1,0:T(8,128)S(1)}, f32[3,21,8,128]{3,2,1,0:T(8,128)S(1)}, u32[]{:S(2)}, u32[]{:S(2)}) collective-permute-start(f32[3,21,8,128]{3,2,1,0:T(8,128)S(1)} %get-tuple-element.16), channel_id=1, source_target_pairs={{0,1},{1,0},{2,3},{3,2},{4,5},{5,4},{6,7},{7,6},{8,9},{9,8},{10,11... | collective-permute-start | bytes 774152 | tf_op jit(solution)/shard_map/ppermute | solution.py:472
  11.6 3.7 %collective-permute-start.1 = (f32[3,24,128]{2,1,0:T(8,128)S(1)}, f32[3,24,128]{2,1,0:T(8,128)S(1)}, u32[]{:S(2)}, u32[]{:S(2)}) collective-permute-start(f32[3,24,128]{2,1,0:T(8,128)S(1)} %get-tuple-element.17), channel_id=1, source_target_pairs={{0,30},{2,4},{4,2},{6,8},{8,6},{10,12},{12,10},{14,16},{16,14},{18... | collective-permute-start | bytes 110600 | tf_op jit(solution)/shard_map/ppermute | solution.py:473
  15.3 0.0 collective-permute-start.2
  15.3 0.9 %collective-permute-start.3 = (f32[3,16,128]{2,1,0:T(8,128)S(1)}, f32[3,16,128]{2,1,0:T(8,128)S(1)}, u32[]{:S(2)}, u32[]{:S(2)}) collective-permute-start(f32[3,16,128]{2,1,0:T(8,128)S(1)} %get-tuple-element.19), channel_id=1, source_target_pairs={{0,31},{1,30},{2,5},{3,4},{4,3},{5,2},{6,9},{7,8},{8,7},{9,6},{10,... | collective-permute-start | bytes 73736 | tf_op jit(solution)/shard_map/ppermute | solution.py:474
  16.2 0.0 collective-permute-start.4
  16.2 5.9 %collective-permute-done.3.refs_3_ = f32[3,16,128]{2,1,0:T(8,128)S(1)} collective-permute-done((f32[3,16,128]{2,1,0:T(8,128)S(1)}, f32[3,16,128]{2,1,0:T(8,128)S(1)}, u32[]{:S(2)}, u32[]{:S(2)}) %collective-permute-start.3) | collective-permute-done | bytes 24608 | tf_op jit(solution)/shard_map/ppermute | solution.py:474
  22.2 0.0 collective-permute-done.4.refs_4_
  22.2 0.0 collective-permute-done.1.refs_1_
  22.2 0.0 collective-permute-done.2.refs_2_
  22.2 0.0 collective-permute-done.refs_0_
  22.2 0.0 copy-start.5
  22.2 0.6 %copy-done.5 = s32[3]{0:T(128)S(1)} copy-done((s32[3]{0:T(128)S(1)}, s32[3]{0:T(128)}, u32[]{:S(2)}) %copy-start.5) | copy-done | bytes 36
  22.8 5.2 %up.1 = f32[3,16,1024]{2,1,0:T(8,128)} custom-call(s32[3]{0:T(128)S(1)} %copy-done.5, f32[3,24,1152]{2,1,0:T(8,128)S(1)} %get-tuple-element.13.value_ref, f32[3,24,1152]{2,1,0:T(8,128)S(1)} %get-tuple-element.14.right_ref, f32[3,12,640]{2,1,0:T(8,128)S(1)} %get-tuple-element.15.coarse_ref, f32[3,21,8,128]{3,2,1,0:T(8,128)S(1)} %collective-permute-done.refs_0_, ...), custom_call_target="tpu_custom_call" | custom-call | tf_op jit(solution)/shard_map/up/pallas_call | solution.py:443
Async XLA Ops:
  0.0 1.0 %copy-start = (f32[2,3,16,1024]{3,2,1,0:T(8,128)S(1)}, f32[2,3,16,1024]{3,2,1,0:T(8,128)}, u32[]{:S(2)}) copy-start(f32[2,3,16,1024]{3,2,1,0:T(8,128)} %grad_x.1) | copy-start | bytes 1179652
  1.0 1.0 %copy-start.1 = (f32[2,3,16,1024]{3,2,1,0:T(8,128)S(1)}, f32[2,3,16,1024]{3,2,1,0:T(8,128)}, u32[]{:S(2)}) copy-start(f32[2,3,16,1024]{3,2,1,0:T(8,128)} %grad_y.1) | copy-start | bytes 1179652
  2.0 0.9 %copy-start.2 = (f32[3,16,1024]{2,1,0:T(8,128)S(1)}, f32[3,16,1024]{2,1,0:T(8,128)}, u32[]{:S(2)}) copy-start(f32[3,16,1024]{2,1,0:T(8,128)} %target.1) | copy-start | bytes 589828
  2.9 0.8 %copy-start.3 = (s32[16,1024]{1,0:T(8,128)S(1)}, s32[16,1024]{1,0:T(8,128)}, u32[]{:S(2)}) copy-start(s32[16,1024]{1,0:T(8,128)} %labels.1) | copy-start | bytes 196612
  3.8 0.7 %copy-start.4 = (s32[3]{0:T(128)S(1)}, s32[3]{0:T(128)}, u32[]{:S(2)}) copy-start(s32[3]{0:T(128)} %sweeps.3) | copy-start | bytes 40
  8.6 13.6 %collective-permute-start = (f32[3,21,8,128]{3,2,1,0:T(8,128)S(1)}, f32[3,21,8,128]{3,2,1,0:T(8,128)S(1)}, u32[]{:S(2)}, u32[]{:S(2)}) collective-permute-start(f32[3,21,8,128]{3,2,1,0:T(8,128)S(1)} %get-tuple-element.16), channel_id=1, source_target_pairs={{0,1},{1,0},{2,3},{3,2},{4,5},{5,4},{6,7},{7,6},{8,9},{9,8},{10,11... | collective-permute-start | bytes 774152 | tf_op jit(solution)/shard_map/ppermute | solution.py:472
  11.6 10.6 %collective-permute-start.1 = (f32[3,24,128]{2,1,0:T(8,128)S(1)}, f32[3,24,128]{2,1,0:T(8,128)S(1)}, u32[]{:S(2)}, u32[]{:S(2)}) collective-permute-start(f32[3,24,128]{2,1,0:T(8,128)S(1)} %get-tuple-element.17), channel_id=1, source_target_pairs={{0,30},{2,4},{4,2},{6,8},{8,6},{10,12},{12,10},{14,16},{16,14},{18... | collective-permute-start | bytes 110600 | tf_op jit(solution)/shard_map/ppermute | solution.py:473
  15.3 6.9 %collective-permute-start.2 = (f32[3,24,128]{2,1,0:T(8,128)S(1)}, f32[3,24,128]{2,1,0:T(8,128)S(1)}, u32[]{:S(2)}, u32[]{:S(2)}) collective-permute-start(f32[3,24,128]{2,1,0:T(8,128)S(1)} %get-tuple-element.18), channel_id=1, source_target_pairs={{0,2},{2,0},{4,6},{6,4},{8,10},{10,8},{12,14},{14,12},{16,18},{18,... | collective-permute-start | bytes 110600 | tf_op jit(solution)/shard_map/ppermute | solution.py:475
  15.3 6.8 %collective-permute-start.3 = (f32[3,16,128]{2,1,0:T(8,128)S(1)}, f32[3,16,128]{2,1,0:T(8,128)S(1)}, u32[]{:S(2)}, u32[]{:S(2)}) collective-permute-start(f32[3,16,128]{2,1,0:T(8,128)S(1)} %get-tuple-element.19), channel_id=1, source_target_pairs={{0,31},{1,30},{2,5},{3,4},{4,3},{5,2},{6,9},{7,8},{8,7},{9,6},{10,... | collective-permute-start | bytes 73736 | tf_op jit(solution)/shard_map/ppermute | solution.py:474
  16.2 5.9 %collective-permute-start.4 = (f32[3,16,128]{2,1,0:T(8,128)S(1)}, f32[3,16,128]{2,1,0:T(8,128)S(1)}, u32[]{:S(2)}, u32[]{:S(2)}) collective-permute-start(f32[3,16,128]{2,1,0:T(8,128)S(1)} %get-tuple-element.20), channel_id=1, source_target_pairs={{0,3},{1,2},{2,1},{3,0},{4,7},{5,6},{6,5},{7,4},{8,11},{9,10},{10,... | collective-permute-start | bytes 73736 | tf_op jit(solution)/shard_map/ppermute | solution.py:476
  22.2 0.7 %copy-start.5 = (s32[3]{0:T(128)S(1)}, s32[3]{0:T(128)}, u32[]{:S(2)}) copy-start(s32[3]{0:T(128)} %sweeps.3) | copy-start | bytes 40

commit v3 on v2

--- a/solution.py
+++ b/solution.py
@@ -12,7 +12,7 @@
 LANES = 128
 HALF = LANES // 2
 VMEM = pl.BlockSpec(memory_space=pltpu.VMEM)
-SMEM = pl.BlockSpec(memory_space=pltpu.SMEM)
+HBM = pl.BlockSpec(memory_space=pltpu.HBM)
 
 
 def diagonal(scale):
@@ -234,10 +234,10 @@
     return value[:value_rows], right[:right_rows], coarse[:coarse_rows]
 
 
-def down_kernel(parts, sweeps, target, grad_x, grad_y, labels, *refs):
+def down_kernel(parts, sweeps_hbm, target, grad_x, grad_y, labels, *refs):
     outs, scratch = refs[:8 if parts == 2 else 3], refs[8 if parts == 2 else 3:]
     value_ref, right_ref, coarse_ref = outs[:3]
-    target_v, grad_x_v, grad_y_v, labels_v, v_ref, b_ref, paired_ref, sems = scratch
+    sweeps, target_v, grad_x_v, grad_y_v, labels_v, v_ref, b_ref, paired_ref, sems = scratch
     chans, rows, cols = target.shape
     window = value_ref.shape[1]
     place = lax.axis_index("lat")
@@ -246,11 +246,14 @@
     if parts == 2:
         start = pl.multiple_of(start, 8)
     inside = band_mask(window, parts, place, rows)
-    count = sweeps[0]
     scale = 1.0
 
-    marks_copy = pltpu.make_async_copy(labels, labels_v, sems.at[chans, 0])
-    marks_copy.start()
+    first_copies = [
+        pltpu.make_async_copy(labels, labels_v, sems.at[chans, 0]),
+        pltpu.make_async_copy(sweeps_hbm, sweeps, sems.at[chans, 1]),
+    ]
+    for copy in first_copies:
+        copy.start()
     copies = []
     for chan in range(chans):
         copies.append([
@@ -263,7 +266,9 @@
     if window > rows:
         v_ref[...] = jnp.zeros_like(v_ref)
         b_ref[...] = jnp.zeros_like(b_ref)
-    marks_copy.wait()
+    for copy in first_copies:
+        copy.wait()
+    count = sweeps[0]
 
     def chosen(grad, chan):
         marks = labels_v[...]
@@ -329,10 +334,11 @@
     spare = 8 if window > rows else 0
     return pl.pallas_call(
         functools.partial(down_kernel, parts),
-        in_specs=[SMEM] + [pl.BlockSpec(memory_space=pl.ANY)] * 4,
+        in_specs=[HBM] * 5,
         out_specs=[VMEM] * len(outs),
         out_shape=outs,
         scratch_shapes=[
+            pltpu.SMEM(sweeps.shape, jnp.int32),
             pltpu.VMEM(target.shape, jnp.float32),
             pltpu.VMEM(grad_x.shape, jnp.float32),
             pltpu.VMEM(grad_y.shape, jnp.float32),
@@ -353,11 +359,13 @@
     return jnp.where(place == 0, top(own) + bottom(other), bottom(own) + top(other))
 
 
-def up_kernel(parts, sweeps, value_ref, right_ref, coarse_ref, *refs):
+def up_kernel(parts, sweeps_hbm, value_ref, right_ref, coarse_ref, *refs):
     if parts == 2:
         packed_ref, *edge_refs = refs[:5]
         refs = refs[5:]
-    out_ref, b0_ref, b1_ref, b2_ref, pair_ref, fix1_ref, fix0_ref = refs
+    out_ref, sweeps, b0_ref, b1_ref, b2_ref, pair_ref, fix1_ref, fix0_ref, sem = refs
+    sweeps_copy = pltpu.make_async_copy(sweeps_hbm, sweeps, sem)
+    sweeps_copy.start()
     chans, rows, cols = out_ref.shape
     window, wide = value_ref.shape[1:]
     half = b1_ref.shape[2]
@@ -407,6 +415,7 @@
         first = [(DAMPING / diagonal(scale)) * right_ref[i] for i in range(chans)]
         return smoothed(first, right_ref, count - 1, scale)
 
+    sweeps_copy.wait()
     mid = from_zero(b1_ref, sweeps[1], 0.25)
     low = restrict([residual(mid[i], b1_ref[i], 0.25) for i in range(chans)], pair_ref)
     for i in range(chans):
@@ -442,16 +451,18 @@
     spare = 16 if parts > 2 else 0
     return pl.pallas_call(
         functools.partial(up_kernel, parts),
-        in_specs=[SMEM] + [VMEM] * (3 + len(packed)),
+        in_specs=[HBM] + [VMEM] * (3 + len(packed)),
         out_specs=VMEM,
         out_shape=jax.ShapeDtypeStruct(shape, jnp.float32),
         scratch_shapes=[
+            pltpu.SMEM(sweeps.shape, jnp.int32),
             f32(value.shape),
             f32((chans, full // 2, cols // 2 + LANES)),
             f32((chans, full // 4, cols // 4 + LANES)),
             f32((chans, cols // 4 // LANES + 1, full // 2, LANES)),
             f32((chans, cols // 2 // LANES + 1, full // 2, LANES)),
             f32((chans, wide // LANES, full + spare, LANES)),
+            pltpu.SemaphoreType.DMA,
         ],
         compiler_params=pltpu.CompilerParams(vmem_limit_bytes=48 * 2**20),
         name="up",

time: 28 us -> 26.9 us (0.961)
  Pallas kernels: 9.32 us -> 8.43 us
    pallas_call x2, Pallas kernels: 9.32 us -> 8.43 us  [the longest x1 4.85 us: up(): pl.pallas_call(functools.partial(up_kernel, parts), in_specs=[HBM] + [VME...]
where the time goes in v3:
time: 26.9 us; the launch traced here: 27.1 us
  Pallas kernels  8.43 us (31%)
  starting transfers between devices  7.65 us (28%)
  waiting for transfers between devices  5.93 us (22%)
  local copies, waits for them, and re-layouts  5.06 us (19%)
    ppermute x1, waiting for transfers between devices, local(): odd_across = lax.ppermute(odd_across, ('lon', 'lat'), across(odd))  5.92 us
    unnamed x12, local copies, waits for them, and re-layouts  5.06 us
    pallas_call x1, Pallas kernels, up(): pl.pallas_call(functools.partial(up_kernel, parts), in_specs=[HBM] + [VME...  4.85 us
    ppermute x1, starting transfers between devices, local(): odd_edge = lax.ppermute(odd_edge, 'lon', odd)  3.72 us
    pallas_call x1, Pallas kernels, down(): pl.pallas_call(functools.partial(down_kernel, parts), in_specs=[HBM] * 5,...  3.58 us
    ppermute x1, starting transfers between devices, local(): packed = lax.ppermute(packed, 'lat', [(0, 1), (1, 0)])  3 us
    ppermute x1, starting transfers between devices, local(): odd_across = lax.ppermute(odd_across, ('lon', 'lat'), across(odd))  0.93 us
  transfers between devices with their start and end apart: 5, of which 1 were waited for; matrix products, arithmetic and copies ran while one was open for 0% of the time, Pallas kernels for 0%

profile of v3, /device:TPU:0, one launch (start us, length us, event | category | flops | bytes accessed | tf_op | source)
XLA Modules:
  0.0 27.1 jit_solution(15579720553168014397)
XLA Ops:
  0.0 0.0 copy-start
  0.0 1.0 %copy-done = f32[2,3,16,1024]{3,2,1,0:T(8,128)S(1)} copy-done((f32[2,3,16,1024]{3,2,1,0:T(8,128)S(1)}, f32[2,3,16,1024]{3,2,1,0:T(8,128)}, u32[]{:S(2)}) %copy-start) | copy-done | bytes 393240
  1.0 0.0 copy-start.1
  1.0 1.0 %copy-done.1 = f32[2,3,16,1024]{3,2,1,0:T(8,128)S(1)} copy-done((f32[2,3,16,1024]{3,2,1,0:T(8,128)S(1)}, f32[2,3,16,1024]{3,2,1,0:T(8,128)}, u32[]{:S(2)}) %copy-start.1) | copy-done | bytes 393240
  2.0 0.0 copy-start.2
  2.0 0.9 %copy-done.2 = f32[3,16,1024]{2,1,0:T(8,128)S(1)} copy-done((f32[3,16,1024]{2,1,0:T(8,128)S(1)}, f32[3,16,1024]{2,1,0:T(8,128)}, u32[]{:S(2)}) %copy-start.2) | copy-done | bytes 196632
  2.9 0.0 copy-start.3
  2.9 0.8 %copy-done.3 = s32[16,1024]{1,0:T(8,128)S(1)} copy-done((s32[16,1024]{1,0:T(8,128)S(1)}, s32[16,1024]{1,0:T(8,128)}, u32[]{:S(2)}) %copy-start.3) | copy-done | bytes 65560
  3.8 0.0 copy-start.4
  3.8 0.7 %copy-done.4 = s32[3]{0:T(128)S(1)} copy-done((s32[3]{0:T(128)S(1)}, s32[3]{0:T(128)}, u32[]{:S(2)}) %copy-start.4) | copy-done | bytes 36
  4.4 3.6 %down.1 = (f32[3,24,1152]{2,1,0:T(8,128)S(1)}, f32[3,24,1152]{2,1,0:T(8,128)S(1)}, f32[3,12,640]{2,1,0:T(8,128)S(1)}, f32[3,21,8,128]{3,2,1,0:T(8,128)S(1)}, f32...) custom-call(s32[3]{0:T(128)S(1)} %copy-done.4, ...), custom_call_target="tpu_custom_call" | custom-call | tf_op jit(solution)/shard_map/down/pallas_call | solution.py:335
  8.0 3.0 %collective-permute-start = (f32[3,21,8,128]{3,2,1,0:T(8,128)S(1)}, f32[3,21,8,128]{3,2,1,0:T(8,128)S(1)}, u32[]{:S(2)}, u32[]{:S(2)}) collective-permute-start(f32[3,21,8,128]{3,2,1,0:T(8,128)S(1)} %get-tuple-element.16), channel_id=1, source_target_pairs={{0,1},{1,0},{2,3},{3,2},{4,5},{5,4},{6,7},{7,6},{8,9},{9,8},{10,11... | collective-permute-start | bytes 774152 | tf_op jit(solution)/shard_map/ppermute | solution.py:483
  11.0 3.7 %collective-permute-start.1 = (f32[3,24,128]{2,1,0:T(8,128)S(1)}, f32[3,24,128]{2,1,0:T(8,128)S(1)}, u32[]{:S(2)}, u32[]{:S(2)}) collective-permute-start(f32[3,24,128]{2,1,0:T(8,128)S(1)} %get-tuple-element.17), channel_id=1, source_target_pairs={{0,30},{2,4},{4,2},{6,8},{8,6},{10,12},{12,10},{14,16},{16,14},{18... | collective-permute-start | bytes 110600 | tf_op jit(solution)/shard_map/ppermute | solution.py:484
  14.7 0.0 collective-permute-start.2
  14.7 0.9 %collective-permute-start.3 = (f32[3,16,128]{2,1,0:T(8,128)S(1)}, f32[3,16,128]{2,1,0:T(8,128)S(1)}, u32[]{:S(2)}, u32[]{:S(2)}) collective-permute-start(f32[3,16,128]{2,1,0:T(8,128)S(1)} %get-tuple-element.19), channel_id=1, source_target_pairs={{0,31},{1,30},{2,5},{3,4},{4,3},{5,2},{6,9},{7,8},{8,7},{9,6},{10,... | collective-permute-start | bytes 73736 | tf_op jit(solution)/shard_map/ppermute | solution.py:485
  15.7 0.0 collective-permute-start.4
  15.7 5.9 %collective-permute-done.3.refs_3_ = f32[3,16,128]{2,1,0:T(8,128)S(1)} collective-permute-done((f32[3,16,128]{2,1,0:T(8,128)S(1)}, f32[3,16,128]{2,1,0:T(8,128)S(1)}, u32[]{:S(2)}, u32[]{:S(2)}) %collective-permute-start.3) | collective-permute-done | bytes 24608 | tf_op jit(solution)/shard_map/ppermute | solution.py:485
  21.6 0.0 collective-permute-done.4.refs_4_
  21.6 0.0 collective-permute-done.1.refs_1_
  21.6 0.0 collective-permute-done.2.refs_2_
  21.6 0.0 collective-permute-done.refs_0_
  21.6 0.0 copy-start.5
  21.6 0.6 %copy-done.5 = s32[3]{0:T(128)S(1)} copy-done((s32[3]{0:T(128)S(1)}, s32[3]{0:T(128)}, u32[]{:S(2)}) %copy-start.5) | copy-done | bytes 36
  22.3 4.8 %up.1 = f32[3,16,1024]{2,1,0:T(8,128)} custom-call(s32[3]{0:T(128)S(1)} %copy-done.5, f32[3,24,1152]{2,1,0:T(8,128)S(1)} %get-tuple-element.13.value_ref, f32[3,24,1152]{2,1,0:T(8,128)S(1)} %get-tuple-element.14.right_ref, f32[3,12,640]{2,1,0:T(8,128)S(1)} %get-tuple-element.15.coarse_ref, f32[3,21,8,128]{3,2,1,0:T(8,128)S(1)} %collective-permute-done.refs_0_, ...), custom_call_target="tpu_custom_call" | custom-call | tf_op jit(solution)/shard_map/up/pallas_call | solution.py:452
Async XLA Ops:
  0.0 1.0 %copy-start = (f32[2,3,16,1024]{3,2,1,0:T(8,128)S(1)}, f32[2,3,16,1024]{3,2,1,0:T(8,128)}, u32[]{:S(2)}) copy-start(f32[2,3,16,1024]{3,2,1,0:T(8,128)} %grad_x.1) | copy-start | bytes 1179652
  1.0 1.0 %copy-start.1 = (f32[2,3,16,1024]{3,2,1,0:T(8,128)S(1)}, f32[2,3,16,1024]{3,2,1,0:T(8,128)}, u32[]{:S(2)}) copy-start(f32[2,3,16,1024]{3,2,1,0:T(8,128)} %grad_y.1) | copy-start | bytes 1179652
  2.0 0.9 %copy-start.2 = (f32[3,16,1024]{2,1,0:T(8,128)S(1)}, f32[3,16,1024]{2,1,0:T(8,128)}, u32[]{:S(2)}) copy-start(f32[3,16,1024]{2,1,0:T(8,128)} %target.1) | copy-start | bytes 589828
  2.9 0.8 %copy-start.3 = (s32[16,1024]{1,0:T(8,128)S(1)}, s32[16,1024]{1,0:T(8,128)}, u32[]{:S(2)}) copy-start(s32[16,1024]{1,0:T(8,128)} %labels.1) | copy-start | bytes 196612
  3.8 0.7 %copy-start.4 = (s32[3]{0:T(128)S(1)}, s32[3]{0:T(128)}, u32[]{:S(2)}) copy-start(s32[3]{0:T(128)} %sweeps_hbm.3) | copy-start | bytes 40
  8.0 13.6 %collective-permute-start = (f32[3,21,8,128]{3,2,1,0:T(8,128)S(1)}, f32[3,21,8,128]{3,2,1,0:T(8,128)S(1)}, u32[]{:S(2)}, u32[]{:S(2)}) collective-permute-start(f32[3,21,8,128]{3,2,1,0:T(8,128)S(1)} %get-tuple-element.16), channel_id=1, source_target_pairs={{0,1},{1,0},{2,3},{3,2},{4,5},{5,4},{6,7},{7,6},{8,9},{9,8},{10,11... | collective-permute-start | bytes 774152 | tf_op jit(solution)/shard_map/ppermute | solution.py:483
  11.0 10.6 %collective-permute-start.1 = (f32[3,24,128]{2,1,0:T(8,128)S(1)}, f32[3,24,128]{2,1,0:T(8,128)S(1)}, u32[]{:S(2)}, u32[]{:S(2)}) collective-permute-start(f32[3,24,128]{2,1,0:T(8,128)S(1)} %get-tuple-element.17), channel_id=1, source_target_pairs={{0,30},{2,4},{4,2},{6,8},{8,6},{10,12},{12,10},{14,16},{16,14},{18... | collective-permute-start | bytes 110600 | tf_op jit(solution)/shard_map/ppermute | solution.py:484
  14.7 6.9 %collective-permute-start.2 = (f32[3,24,128]{2,1,0:T(8,128)S(1)}, f32[3,24,128]{2,1,0:T(8,128)S(1)}, u32[]{:S(2)}, u32[]{:S(2)}) collective-permute-start(f32[3,24,128]{2,1,0:T(8,128)S(1)} %get-tuple-element.18), channel_id=1, source_target_pairs={{0,2},{2,0},{4,6},{6,4},{8,10},{10,8},{12,14},{14,12},{16,18},{18,... | collective-permute-start | bytes 110600 | tf_op jit(solution)/shard_map/ppermute | solution.py:486
  14.7 6.8 %collective-permute-start.3 = (f32[3,16,128]{2,1,0:T(8,128)S(1)}, f32[3,16,128]{2,1,0:T(8,128)S(1)}, u32[]{:S(2)}, u32[]{:S(2)}) collective-permute-start(f32[3,16,128]{2,1,0:T(8,128)S(1)} %get-tuple-element.19), channel_id=1, source_target_pairs={{0,31},{1,30},{2,5},{3,4},{4,3},{5,2},{6,9},{7,8},{8,7},{9,6},{10,... | collective-permute-start | bytes 73736 | tf_op jit(solution)/shard_map/ppermute | solution.py:485
  15.7 5.9 %collective-permute-start.4 = (f32[3,16,128]{2,1,0:T(8,128)S(1)}, f32[3,16,128]{2,1,0:T(8,128)S(1)}, u32[]{:S(2)}, u32[]{:S(2)}) collective-permute-start(f32[3,16,128]{2,1,0:T(8,128)S(1)} %get-tuple-element.20), channel_id=1, source_target_pairs={{0,3},{1,2},{2,1},{3,0},{4,7},{5,6},{6,5},{7,4},{8,11},{9,10},{10,... | collective-permute-start | bytes 73736 | tf_op jit(solution)/shard_map/ppermute | solution.py:487
  21.6 0.7 %copy-start.5 = (s32[3]{0:T(128)S(1)}, s32[3]{0:T(128)}, u32[]{:S(2)}) copy-start(s32[3]{0:T(128)} %sweeps_hbm.3) | copy-start | bytes 40

commit v4 on v3

--- a/solution.py
+++ b/solution.py
@@ -13,6 +13,10 @@
 HALF = LANES // 2
 VMEM = pl.BlockSpec(memory_space=pltpu.VMEM)
 HBM = pl.BlockSpec(memory_space=pltpu.HBM)
+
+
+def in_hbm(array):
+    return pltpu.with_memory_space_constraint(array, pltpu.HBM)
 
 
 def diagonal(scale):
@@ -350,7 +354,7 @@
         ],
         compiler_params=pltpu.CompilerParams(vmem_limit_bytes=32 * 2**20),
         name="down",
-    )(sweeps, target, grad_x, grad_y, labels)
+    )(*(in_hbm(a) for a in (sweeps, target, grad_x, grad_y, labels)))
 
 
 def joined(place, own, other, height):
@@ -466,7 +470,7 @@
         ],
         compiler_params=pltpu.CompilerParams(vmem_limit_bytes=48 * 2**20),
         name="up",
-    )(sweeps, value, right, coarse, *packed)
+    )(in_hbm(sweeps), value, right, coarse, *packed)
 
 
 def local(target, grad_x, grad_y, labels, sweeps):

time: 26.9 us -> 22.4 us (0.83); the launches traced: 27.1 us -> 22.1 us
  local copies, waits for them, and re-layouts: 5.06 us -> 0 us
    unnamed x12 -> x0, local copies, waits for them, and re-layouts: 5.06 us -> none
where the time goes in v4:
time: 22.4 us; the launch traced here: 22.1 us
  Pallas kernels  8.45 us (38%)
  starting transfers between devices  7.65 us (34%)
  waiting for transfers between devices  5.93 us (26%)
    ppermute x1, waiting for transfers between devices, local(): odd_across = lax.ppermute(odd_across, ('lon', 'lat'), across(odd))  5.92 us
    pallas_call x1, Pallas kernels, up(): pl.pallas_call(functools.partial(up_kernel, parts), in_specs=[HBM] + [VME...  4.7 us
    pallas_call x1, Pallas kernels, down(): pl.pallas_call(functools.partial(down_kernel, parts), in_specs=[HBM] * 5,...  3.75 us
    ppermute x1, starting transfers between devices, local(): odd_edge = lax.ppermute(odd_edge, 'lon', odd)  3.72 us
    ppermute x1, starting transfers between devices, local(): packed = lax.ppermute(packed, 'lat', [(0, 1), (1, 0)])  3 us
    ppermute x1, starting transfers between devices, local(): odd_across = lax.ppermute(odd_across, ('lon', 'lat'), across(odd))  0.93 us
  transfers between devices with their start and end apart: 5, of which 1 were waited for; matrix products, arithmetic and copies ran while one was open for 0% of the time, Pallas kernels for 0%

profile of v4, /device:TPU:0, one launch (start us, length us, event | category | flops | bytes accessed | tf_op | source)
XLA Modules:
  0.0 22.1 jit_solution(16808837824306943213)
XLA Ops:
  0.0 3.8 %down.1 = (f32[3,24,1152]{2,1,0:T(8,128)S(1)}, f32[3,24,1152]{2,1,0:T(8,128)S(1)}, f32[3,12,640]{2,1,0:T(8,128)S(1)}, f32[3,21,8,128]{3,2,1,0:T(8,128)S(1)}, f32...) custom-call(s32[3]{0:T(128)} %sweeps_hbm.3, ...), custom_call_target="tpu_custom_call" | custom-call | tf_op jit(solution)/shard_map/down/pallas_call | solution.py:339
  3.8 3.0 %collective-permute-start = (f32[3,21,8,128]{3,2,1,0:T(8,128)S(1)}, f32[3,21,8,128]{3,2,1,0:T(8,128)S(1)}, u32[]{:S(2)}, u32[]{:S(2)}) collective-permute-start(f32[3,21,8,128]{3,2,1,0:T(8,128)S(1)} %get-tuple-element.16), channel_id=1, source_target_pairs={{0,1},{1,0},{2,3},{3,2},{4,5},{5,4},{6,7},{7,6},{8,9},{9,8},{10,11... | collective-permute-start | bytes 774152 | tf_op jit(solution)/shard_map/ppermute | solution.py:487
  6.8 3.7 %collective-permute-start.1 = (f32[3,24,128]{2,1,0:T(8,128)S(1)}, f32[3,24,128]{2,1,0:T(8,128)S(1)}, u32[]{:S(2)}, u32[]{:S(2)}) collective-permute-start(f32[3,24,128]{2,1,0:T(8,128)S(1)} %get-tuple-element.17), channel_id=1, source_target_pairs={{0,30},{2,4},{4,2},{6,8},{8,6},{10,12},{12,10},{14,16},{16,14},{18... | collective-permute-start | bytes 110600 | tf_op jit(solution)/shard_map/ppermute | solution.py:488
  10.5 0.0 collective-permute-start.2
  10.5 0.9 %collective-permute-start.3 = (f32[3,16,128]{2,1,0:T(8,128)S(1)}, f32[3,16,128]{2,1,0:T(8,128)S(1)}, u32[]{:S(2)}, u32[]{:S(2)}) collective-permute-start(f32[3,16,128]{2,1,0:T(8,128)S(1)} %get-tuple-element.19), channel_id=1, source_target_pairs={{0,31},{1,30},{2,5},{3,4},{4,3},{5,2},{6,9},{7,8},{8,7},{9,6},{10,... | collective-permute-start | bytes 73736 | tf_op jit(solution)/shard_map/ppermute | solution.py:489
  11.4 0.0 collective-permute-start.4
  11.4 5.9 %collective-permute-done.3.refs_3_ = f32[3,16,128]{2,1,0:T(8,128)S(1)} collective-permute-done((f32[3,16,128]{2,1,0:T(8,128)S(1)}, f32[3,16,128]{2,1,0:T(8,128)S(1)}, u32[]{:S(2)}, u32[]{:S(2)}) %collective-permute-start.3) | collective-permute-done | bytes 24608 | tf_op jit(solution)/shard_map/ppermute | solution.py:489
  17.3 0.0 collective-permute-done.4.refs_4_
  17.3 0.0 collective-permute-done.1.refs_1_
  17.3 0.0 collective-permute-done.2.refs_2_
  17.3 0.0 collective-permute-done.refs_0_
  17.4 4.7 %up.1 = f32[3,16,1024]{2,1,0:T(8,128)} custom-call(s32[3]{0:T(128)} %sweeps_hbm.3, f32[3,24,1152]{2,1,0:T(8,128)S(1)} %get-tuple-element.13.value_ref, f32[3,24,1152]{2,1,0:T(8,128)S(1)} %get-tuple-element.14.right_ref, f32[3,12,640]{2,1,0:T(8,128)S(1)} %get-tuple-element.15.coarse_ref, f32[3,21,8,128]{3,2,1,0:T(8,128)S(1)} %collective-permute-done.refs_0_, ...), custom_call_target="tpu_custom_call" | custom-call | tf_op jit(solution)/shard_map/up/pallas_call | solution.py:456
Async XLA Ops:
  3.8 13.6 %collective-permute-start = (f32[3,21,8,128]{3,2,1,0:T(8,128)S(1)}, f32[3,21,8,128]{3,2,1,0:T(8,128)S(1)}, u32[]{:S(2)}, u32[]{:S(2)}) collective-permute-start(f32[3,21,8,128]{3,2,1,0:T(8,128)S(1)} %get-tuple-element.16), channel_id=1, source_target_pairs={{0,1},{1,0},{2,3},{3,2},{4,5},{5,4},{6,7},{7,6},{8,9},{9,8},{10,11... | collective-permute-start | bytes 774152 | tf_op jit(solution)/shard_map/ppermute | solution.py:487
  6.8 10.6 %collective-permute-start.1 = (f32[3,24,128]{2,1,0:T(8,128)S(1)}, f32[3,24,128]{2,1,0:T(8,128)S(1)}, u32[]{:S(2)}, u32[]{:S(2)}) collective-permute-start(f32[3,24,128]{2,1,0:T(8,128)S(1)} %get-tuple-element.17), channel_id=1, source_target_pairs={{0,30},{2,4},{4,2},{6,8},{8,6},{10,12},{12,10},{14,16},{16,14},{18... | collective-permute-start | bytes 110600 | tf_op jit(solution)/shard_map/ppermute | solution.py:488
  10.5 6.9 %collective-permute-start.2 = (f32[3,24,128]{2,1,0:T(8,128)S(1)}, f32[3,24,128]{2,1,0:T(8,128)S(1)}, u32[]{:S(2)}, u32[]{:S(2)}) collective-permute-start(f32[3,24,128]{2,1,0:T(8,128)S(1)} %get-tuple-element.18), channel_id=1, source_target_pairs={{0,2},{2,0},{4,6},{6,4},{8,10},{10,8},{12,14},{14,12},{16,18},{18,... | collective-permute-start | bytes 110600 | tf_op jit(solution)/shard_map/ppermute | solution.py:490
  10.5 6.8 %collective-permute-start.3 = (f32[3,16,128]{2,1,0:T(8,128)S(1)}, f32[3,16,128]{2,1,0:T(8,128)S(1)}, u32[]{:S(2)}, u32[]{:S(2)}) collective-permute-start(f32[3,16,128]{2,1,0:T(8,128)S(1)} %get-tuple-element.19), channel_id=1, source_target_pairs={{0,31},{1,30},{2,5},{3,4},{4,3},{5,2},{6,9},{7,8},{8,7},{9,6},{10,... | collective-permute-start | bytes 73736 | tf_op jit(solution)/shard_map/ppermute | solution.py:489
  11.4 5.9 %collective-permute-start.4 = (f32[3,16,128]{2,1,0:T(8,128)S(1)}, f32[3,16,128]{2,1,0:T(8,128)S(1)}, u32[]{:S(2)}, u32[]{:S(2)}) collective-permute-start(f32[3,16,128]{2,1,0:T(8,128)S(1)} %get-tuple-element.20), channel_id=1, source_target_pairs={{0,3},{1,2},{2,1},{3,0},{4,7},{5,6},{6,5},{7,4},{8,11},{9,10},{10,... | collective-permute-start | bytes 73736 | tf_op jit(solution)/shard_map/ppermute | solution.py:491

commit v5 on v0

v5 whole, which is shorter than its diff:
```python
import functools

import jax
import jax.numpy as jnp
from jax import lax
from jax.experimental import pallas as pl
from jax.experimental.pallas import tpu as pltpu
from jax.sharding import PartitionSpec as P

SCREENING = 0.02
DAMPING = 0.8
LANES = 128
HALF = LANES // 2
SUBLANES = 8
VMEM = pl.BlockSpec(memory_space=pltpu.VMEM)
HBM = pl.BlockSpec(memory_space=pltpu.HBM)
F32 = functools.partial(jax.ShapeDtypeStruct, dtype=jnp.float32)
SCRATCH = functools.partial(pltpu.VMEM, dtype=jnp.float32)


def in_hbm(array):
    return pltpu.with_memory_space_constraint(array, pltpu.HBM)


def diagonal(scale):
    return SCREENING + 4.0 * scale


def rows_of(value):
    return lax.broadcasted_iota(jnp.int32, value.shape, 0)


def lanes_of(tile):
    return lax.broadcasted_iota(jnp.int32, tile.shape, len(tile.shape) - 1)


def tiles(value):
    return [value[:, k * LANES:(k + 1) * LANES] for k in range(value.shape[1] // LANES)]


def row_before(value):
    return jnp.where(rows_of(value) == 0, 0.0, pltpu.roll(value, 1, 0))


def row_after(value):
    last = value.shape[0] - 1
    return jnp.where(rows_of(value) == last, 0.0, pltpu.roll(value, last, 0))


def norths(planes):
    return [row_before(planes[-1])] + list(planes[:-1])


def souths(planes):
    return list(planes[1:]) + [row_after(planes[0])]


def west_of(value):
    return pltpu.roll(value, 1, 1)


def east_of(value):
    return pltpu.roll(value, value.shape[1] - 1, 1)


def around(planes):
    return [
        (north + south) + (west_of(value) + east_of(value))
        for value, north, south in zip(planes, norths(planes), souths(planes))
    ]


def sweep(planes, scaled, scale, inside=None):
    beside = DAMPING * scale / diagonal(scale)
    planes = [
        (1.0 - DAMPING) * value + (right + beside * total) for value, right, total in zip(planes, scaled, around(planes))
    ]
    return tuple(planes if inside is None else [value * mask for value, mask in zip(planes, inside)])


def residual(planes, right, scale):
    return [b - diagonal(scale) * value + scale * total for value, b, total in zip(planes, right, around(planes))]


def load_planes(ref, start, count, height):
    def plane(first):
        rows = pl.ds(first, height, stride=count) if count > 1 else pl.ds(first, height)
        return jnp.concatenate([ref[k, rows, :] for k in range(ref.shape[0])], 1)

    return [plane(start + t) for t in range(count)]


def store_planes(ref, start, planes):
    count, height = len(planes), planes[0].shape[0]
    for t, plane in enumerate(planes):
        rows = pl.ds(start + t, height, stride=count) if count > 1 else pl.ds(start + t, height)
        for k, tile in enumerate(tiles(plane)):
            ref[k, rows, :] = tile


def places_of(shape, wanted):
    source = lax.broadcasted_iota(jnp.int32, shape, 0)
    target = lax.broadcasted_iota(jnp.int32, shape, 1)
    return wanted(source, target).astype(jnp.float32).astype(jnp.bfloat16)


def halo_coarse(fine):
    return jnp.where(fine < HALF, fine // 2, HALF + fine // 2)


def pairing():
    own = places_of((2 * LANES, LANES), lambda source, target: source // 2 == target)
    halo = places_of((LANES, LANES), lambda source, target: halo_coarse(source) == target)
    return own, halo


def spreading():
    own = places_of((2 * LANES, 2 * LANES), lambda source, target: source == target // 2 + LANES * (target % 2))
    halo = places_of((2 * LANES, LANES), lambda source, target: source == halo_coarse(target) + LANES * (target % 2))
    return own, halo


def moved(value, places):
    high = value.astype(jnp.bfloat16)
    low = (value - high.astype(jnp.float32)).astype(jnp.bfloat16)
    dot = functools.partial(jnp.dot, preferred_element_type=jnp.float32)
    return dot(high, places) + dot(low, places)


def moved_blocks(own_blocks, halo_blocks, places):
    rows, count = halo_blocks[0].shape[0], len(own_blocks[0])
    packed = moved(jnp.concatenate([block for blocks in own_blocks for block in blocks], 0), places[0])
    edges = moved(jnp.concatenate(halo_blocks, 0), places[1])
    out = []
    for i in range(len(own_blocks)):
        parts = [packed[(i * count + k) * rows:(i * count + k + 1) * rows] for k in range(count)]
        out.append(jnp.concatenate(parts + [edges[i * rows:(i + 1) * rows]], 1))
    return out


def pair_columns(fields, places):
    cols = fields[0].shape[1] - LANES
    width = 2 * LANES
    own = [[f[:, k * width:(k + 1) * width] for k in range(cols // width)] for f in fields]
    return moved_blocks(own, [f[:, cols:] for f in fields], places)


def spread_columns(fields, places):
    cut = [list(zip(tiles(0.75 * f + 0.25 * west_of(f)), tiles(0.75 * f + 0.25 * east_of(f)))) for f in fields]
    blocks = [[jnp.concatenate(both, 1) for both in field] for field in cut]
    return moved_blocks([b[:-1] for b in blocks], [b[-1] for b in blocks], places)


def prolong(fields, places):
    halves = [
        half
        for planes in fields
        for value, north, south in zip(planes, norths(planes), souths(planes))
        for half in (0.75 * value + 0.25 * north, 0.75 * value + 0.25 * south)
    ]
    spread = spread_columns(halves, places)
    count = 2 * len(fields[0])
    return [spread[i * count:(i + 1) * count] for i in range(len(fields))]


def window_of(rows, parts):
    return rows + (2 * SUBLANES if parts > 2 else SUBLANES if parts == 2 else 0)


def own_start(parts, place):
    return 0 if parts == 1 else pl.multiple_of(SUBLANES * place, SUBLANES) if parts == 2 else SUBLANES


def band_masks(window, parts, place, rows):
    if parts <= 2:
        return None
    count = window // SUBLANES
    first = place * rows - SUBLANES
    row = [first + t + count * lax.broadcasted_iota(jnp.int32, (SUBLANES, 1), 0) for t in range(count)]
    return [((r >= 0) & (r < parts * rows)).astype(jnp.float32) for r in row]


def eastward(own_last, halo):
    return jnp.where(lanes_of(halo) < HALF, halo, own_last)


def westward(own_first, halo):
    return jnp.where(lanes_of(halo) < HALF, own_first, halo)


def with_edges(parts, from_west, from_east):
    inner = lanes_of(from_west) < HALF
    first = parts[0] + jnp.where(inner, from_west, 0.0)
    last = parts[-2] + jnp.where(inner, 0.0, from_east)
    halo = parts[-1] + jnp.where(inner, from_east, from_west)
    return [first] + list(parts[1:-2]) + [last, halo]


COARSE_WIDTH, FINE_WIDTH, REACH = 32, 8, 4
TO_EAST, TO_WEST = -24, -8


def in_window(lane, start, width):
    start = start % LANES
    end = start + width
    return (lane >= start) & (lane < end) if end <= LANES else (lane >= start) | (lane < end - LANES)


def slots(value_rows, right_rows, coarse_rows, coarse_start):
    out, at = [], 0
    for which, rows, start, width in (
        (2, coarse_rows, coarse_start, COARSE_WIDTH),
        (0, value_rows, -REACH, FINE_WIDTH),
        (1, right_rows, -REACH, FINE_WIDTH),
    ):
        for first in range(0, rows, SUBLANES):
            out.append((which, first, min(SUBLANES, rows - first), start, width, at))
            at += width
    assert at <= LANES
    return out


def bundle(fields, coarse_start):
    out = jnp.zeros((SUBLANES, LANES), jnp.float32)
    lane = lanes_of(out)
    for which, first, rows, start, width, at in slots(*(f.shape[0] for f in fields), coarse_start):
        piece = fields[which][first:first + rows]
        if rows < SUBLANES:
            piece = jnp.concatenate([piece, jnp.zeros((SUBLANES - rows, LANES), jnp.float32)], 0)
        out = jnp.where(in_window(lane, at, width), pltpu.roll(piece, (at - start) % LANES, 1), out)
    return out


def unbundle(tile, heights, coarse_start):
    lane = lanes_of(tile)
    pieces = ([], [], [])
    for which, first, rows, start, width, at in slots(*heights, coarse_start):
        piece = jnp.where(in_window(lane, start, width), pltpu.roll(tile, (start - at) % LANES, 1), 0.0)
        pieces[which].append(piece[:rows])
    return [jnp.concatenate(p, 0) if len(p) > 1 else p[0] for p in pieces]


VALUE_ROWS, RIGHT_ROWS, COARSE_ROWS = 8, 4, 12
ACROSS = (VALUE_ROWS, RIGHT_ROWS, COARSE_ROWS)


def pack(value, right, coarse):
    halves = right[:-1] + [c[SUBLANES:] for c in coarse[:-1]]
    joined = [jnp.concatenate(halves[k:k + 2], 0) for k in range(0, len(halves), 2)]
    return value[:-1] + [c[:SUBLANES] for c in coarse[:-1]] + joined + [bundle([value[-1], right[-1], coarse[-1]], TO_WEST)]


def packed_tiles(fine, coarse):
    return fine + coarse + (fine + coarse) // 2 + 1


def unpack(tile, fine, coarse):
    halves = []
    for k in range(fine + coarse, fine + coarse + (fine + coarse) // 2):
        both = tile(k)
        halves += [both[:4], both[4:]]
    value = [tile(k) for k in range(fine)]
    right = halves[:fine]
    low = [jnp.concatenate([tile(fine + k), halves[fine + k]], 0) for k in range(coarse)]
    ends = unbundle(tile(packed_tiles(fine, coarse) - 1), ACROSS, TO_WEST)
    return [field + [end] for field, end in zip((value, right, low), ends)]


def down_kernel(parts, sweeps_hbm, target, grad_x, grad_y, labels, *refs):
    sent = 5 if parts == 2 else 0
    value_ref, right_ref, coarse_ref = refs[:3]
    sent_refs = refs[3:3 + sent]
    sweeps, target_v, grad_x_v, grad_y_v, labels_v, v_ref, b_ref, scaled_ref, resid_ref, sems = refs[3 + sent:]
    chans, rows, cols = target.shape
    window = value_ref.shape[2]
    count = window // SUBLANES
    place = lax.axis_index("lat")
    start = own_start(parts, place)
    inside = band_masks(window, parts, place, rows)
    scale = 1.0

    first_copies = [
        pltpu.make_async_copy(labels, labels_v, sems.at[chans, 0]),
        pltpu.make_async_copy(sweeps_hbm, sweeps, sems.at[chans, 1]),
    ]
    for copy in first_copies:
        copy.start()
    copies = []
    for chan in range(chans):
        copies.append([
            pltpu.make_async_copy(target.at[chan], target_v.at[chan], sems.at[chan, 0]),
            pltpu.make_async_copy(grad_x.at[:, chan], grad_x_v.at[:, chan], sems.at[chan, 1]),
            pltpu.make_async_copy(grad_y.at[:, chan], grad_y_v.at[:, chan], sems.at[chan, 2]),
        ])
        for copy in copies[-1]:
            copy.start()
    if window > rows:
        v_ref[...] = jnp.zeros_like(v_ref)
        b_ref[...] = jnp.zeros_like(b_ref)
    places = pairing()
    for copy in first_copies:
        copy.wait()

    def chosen(grad, chan):
        marks = labels_v[...]
        out = jnp.zeros((rows, cols), jnp.float32)
        for source in range(grad.shape[0]):
            out = jnp.where(marks == source, grad[source, chan], out)
        return out

    blank = jnp.zeros((rows, LANES), jnp.float32)
    paired = []
    for chan in range(chans):
        for copy in copies[chan]:
            copy.wait()
        own = jnp.concatenate([target_v[chan], blank], 1)
        sel_x = jnp.concatenate([chosen(grad_x_v, chan), blank], 1)
        sel_y = jnp.concatenate([chosen(grad_y_v, chan), blank], 1)
        right = SCREENING * own - ((sel_x - west_of(sel_x)) + (sel_y - row_before(sel_y)))
        below = pltpu.roll(sel_y[rows - SUBLANES:], 1, 0)
        below = jnp.where(rows_of(below) == 0, below, 0.0)
        for k, (v, b, s) in enumerate(zip(tiles(own), tiles(right), tiles(below))):
            v_ref[chan, k, pl.ds(start, rows), :] = v
            b_ref[chan, k, pl.ds(start, rows), :] = b
            if window > rows:
                b_ref[chan, k, pl.ds(start + rows, SUBLANES), :] = s
        planes = load_planes(v_ref.at[chan], 0, count, SUBLANES)
        right = load_planes(b_ref.at[chan], 0, count, SUBLANES)
        if inside is not None:
            right = [b * mask for b, mask in zip(right, inside)]
        store_planes(right_ref.at[chan], 0, right)
        for t in range(count):
            scaled_ref[t] = (DAMPING / diagonal(scale)) * right[t]

        def step(_, planes):
            return sweep(planes, [scaled_ref[t] for t in range(count)], scale, inside)

        planes = lax.fori_loop(0, sweeps[0], step, tuple(planes))
        store_planes(value_ref.at[chan], 0, planes)
        left = residual(planes, [(diagonal(scale) / DAMPING) * scaled_ref[t] for t in range(count)], scale)
        if inside is not None:
            left = [r * mask for r, mask in zip(left, inside)]
        store_planes(resid_ref.at[chan], 0, left)
        north, south = load_planes(resid_ref.at[chan], 0, 2, window // 2)
        paired.append(north + south)
    coarse = pair_columns(paired, places)
    for chan in range(chans):
        low = 0.25 * coarse[chan]
        coarse_ref[chan] = low
        if parts != 2:
            continue
        packed_ref, east_ref, east_across, west_ref, west_across = sent_refs
        wide = value_ref.shape[1]
        value = [value_ref[chan, k] for k in range(wide)]
        right = [right_ref[chan, k] for k in range(wide)]
        low = tiles(low)
        north = place == 0
        value_border = [jnp.where(north, v[12:20], v[4:12]) for v in value]
        right_border = [jnp.where(north, b[13:17], b[8:12]) for b in right]
        for k, tile in enumerate(pack(value_border, right_border, low)):
            packed_ref[chan, k] = tile
        for east, west, fields in (
            (east_ref, west_ref, (value, right, low)),
            (east_across, west_across, (value_border, right_border, low)),
        ):
            east[chan] = bundle([eastward(f[-2], f[-1]) for f in fields], TO_EAST)
            west[chan] = bundle([westward(f[0], f[-1]) for f in fields], TO_WEST)


def down(parts, sweeps, target, grad_x, grad_y, labels):
    chans, rows, cols = target.shape
    window = window_of(rows, parts)
    wide, half = cols // LANES + 1, cols // 2 // LANES + 1
    spare = SUBLANES if window > rows else 0
    outs = [F32((chans, wide, window, LANES))] * 2 + [F32((chans, window // 2, half * LANES))]
    if parts == 2:
        outs.append(F32((chans, packed_tiles(wide - 1, half - 1), SUBLANES, LANES)))
        outs += [F32((chans, SUBLANES, LANES))] * 4
    return pl.pallas_call(
        functools.partial(down_kernel, parts),
        in_specs=[HBM] * 5,
        out_specs=[VMEM] * len(outs),
        out_shape=outs,
        scratch_shapes=[
            pltpu.SMEM(sweeps.shape, jnp.int32),
            SCRATCH(target.shape),
            SCRATCH(grad_x.shape),
            SCRATCH(grad_y.shape),
            pltpu.VMEM(labels.shape, jnp.int32),
            SCRATCH((chans, wide, window + spare, LANES)),
            SCRATCH((chans, wide, window + spare, LANES)),
            SCRATCH((window // SUBLANES, SUBLANES, wide * LANES)),
            SCRATCH((chans, wide, window, LANES)),
            pltpu.SemaphoreType.DMA((chans + 1, 3)),
        ],
        compiler_params=pltpu.CompilerParams(vmem_limit_bytes=32 * 2**20),
        name="down",
    )(*(in_hbm(a) for a in (sweeps, target, grad_x, grad_y, labels)))


def joined(place, own, other, height):
    gap = jnp.zeros((height - own.shape[0], own.shape[1]), jnp.float32)
    top, bottom = (lambda v: jnp.concatenate([v, gap], 0)), (lambda v: jnp.concatenate([gap, v], 0))
    return jnp.where(place == 0, top(own) + bottom(other), bottom(own) + top(other))


def up_kernel(parts, sweeps_hbm, value_ref, right_ref, coarse_ref, *refs):
    received = 5 if parts == 2 else 0
    packed_ref, *edge_refs = refs[:received] or [None]
    out_hbm, sweeps, v0_ref, b0_ref, k0_ref, b1_ref, k1_ref, k2_ref, fix_ref, out_ref, sems = refs[received:]
    sweeps_copy = pltpu.make_async_copy(sweeps_hbm, sweeps, sems.at[0])
    sweeps_copy.start()
    chans, rows, cols = out_ref.shape
    wide, window = value_ref.shape[1:3]
    half = coarse_ref.shape[2] // LANES
    full = parts * rows
    count0, count1, count2 = window // SUBLANES, max(1, full // 2 // SUBLANES), max(1, full // 4 // SUBLANES)
    place = lax.axis_index("lat")
    inside = band_masks(window, parts, place, rows)
    own_heights = (window, window, window // 2)

    def sides(chan, across):
        heights = ACROSS if across else own_heights
        from_west = unbundle(edge_refs[across][chan], heights, TO_EAST)
        from_east = unbundle(edge_refs[2 + across][chan], heights, TO_WEST)
        return list(zip(from_west, from_east))

    from_partner = []
    for chan in range(chans):
        low = coarse_ref[chan]
        if parts == 2:
            here, there = sides(chan, 0), sides(chan, 1)
            other = unpack(lambda k: packed_ref[chan, k], wide - 1, half - 1)
            value, right, other_low = (with_edges(f, *s) for f, s in zip(other, there))
            low = jnp.concatenate(with_edges(tiles(low), *here[2]), 1)
            low = joined(place, low, jnp.concatenate(other_low, 1), full // 2)
            for ref, own, side in ((v0_ref, value_ref, here[0]), (b0_ref, right_ref, here[1])):
                for k, tile in enumerate(with_edges([own[chan, k] for k in range(wide)], *side)):
                    ref[chan, k] = tile
            from_partner.append((value, right))
        else:
            v0_ref[chan] = value_ref[chan]
            b0_ref[chan] = right_ref[chan]
        for k, tile in enumerate(tiles(low)):
            b1_ref[chan, k] = tile

    def add_rows(value_at, right_at):
        for chan, (value, right) in enumerate(from_partner):
            for k in range(wide):
                v0_ref[chan, k, pl.ds(value_at, VALUE_ROWS), :] += value[k]
                b0_ref[chan, k, pl.ds(right_at, RIGHT_ROWS), :] += right[k]

    if parts == 2:
        pl.when(place == 0)(lambda: add_rows(12, 16))
        pl.when(place == 1)(lambda: add_rows(4, 5))

    def smoothed(fields, scaled_ref, count, scale):
        def step(_, fields):
            scaled = [[scaled_ref[i, t] for t in range(len(f))] for i, f in enumerate(fields)]
            return tuple(sweep(f, k, scale) for f, k in zip(fields, scaled))

        return lax.fori_loop(0, count, step, tuple(tuple(f) for f in fields))

    def from_zero(rights, scaled_ref, count, scale):
        first = [[(DAMPING / diagonal(scale)) * b for b in planes] for planes in rights]
        for i, planes in enumerate(first):
            for t, plane in enumerate(planes):
                scaled_ref[i, t] = plane
        return smoothed(first, scaled_ref, count - 1, scale)

    pair_places, spread_places = pairing(), spreading()
    height1 = full // 2 // count1
    right1 = [load_planes(b1_ref.at[i], 0, count1, height1) for i in range(chans)]
    sweeps_copy.wait()
    mid = from_zero(right1, k1_ref, sweeps[1], 0.25)
    left = [residual(f, load_planes(b1_ref.at[i], 0, count1, height1), 0.25) for i, f in enumerate(mid)]
    if count1 > 1:
        pairs = [f[t] + f[t + 1] for f in left for t in range(0, count1, 2)]
        low = [0.25 * v for v in pair_columns(pairs, pair_places)]
        right2 = [low[i * count2:(i + 1) * count2] for i in range(chans)]
    else:
        raise NotImplementedError("one part")
    fix2 = from_zero(right2, k2_ref, sweeps[2], 0.0625)
    mid = [[v + f for v, f in zip(planes, fix)] for planes, fix in zip(mid, prolong(fix2, spread_places))]
    mid = smoothed(mid, k1_ref, sweeps[1], 0.25)
    spare = (fix_ref.shape[2] - full) // 2
    for i, fix in enumerate(prolong(mid, spread_places)):
        store_planes(fix_ref.at[i], spare, fix)
    shown = pl.multiple_of((SUBLANES if parts == 2 else rows) * place, SUBLANES)
    start = own_start(parts, place)
    out_copies = []
    for i in range(chans):
        planes = load_planes(v0_ref.at[i], 0, count0, SUBLANES)
        fix = load_planes(fix_ref.at[i], shown, count0, SUBLANES)
        planes = tuple(v + f for v, f in zip(planes, fix))
        for t, b in enumerate(load_planes(b0_ref.at[i], 0, count0, SUBLANES)):
            k0_ref[t] = (DAMPING / diagonal(1.0)) * b

        def step(_, planes):
            return sweep(planes, [k0_ref[t] for t in range(count0)], 1.0, inside)

        planes = lax.fori_loop(0, sweeps[0], step, planes)
        store_planes(v0_ref.at[i], 0, planes)
        for k in range(cols // LANES):
            out_ref[i, :, k * LANES:(k + 1) * LANES] = v0_ref[i, k, pl.ds(start, rows), :]
        out_copies.append(pltpu.make_async_copy(out_ref.at[i], out_hbm.at[i], sems.at[1 + i]))
        out_copies[-1].start()
    for copy in out_copies:
        copy.wait()


def up(parts, shape, sweeps, value, right, coarse, *received):
    chans, rows, cols = shape
    wide, window = value.shape[1:3]
    full = parts * rows
    half, quarter = cols // 2 // LANES + 1, cols // 4 // LANES + 1
    count1, count2 = max(1, full // 2 // SUBLANES), max(1, full // 4 // SUBLANES)
    spare = 2 * SUBLANES if parts > 2 else 0
    return pl.pallas_call(
        functools.partial(up_kernel, parts),
        in_specs=[HBM] + [VMEM] * (3 + len(received)),
        out_specs=HBM,
        out_shape=F32(shape),
        scratch_shapes=[
            pltpu.SMEM(sweeps.shape, jnp.int32),
            SCRATCH(value.shape),
            SCRATCH(value.shape),
            SCRATCH((window // SUBLANES, SUBLANES, wide * LANES)),
            SCRATCH((chans, half, full // 2, LANES)),
            SCRATCH((chans, count1, full // 2 // count1, half * LANES)),
            SCRATCH((chans, count2, full // 4 // count2, quarter * LANES)),
            SCRATCH((chans, wide, full + spare, LANES)),
            SCRATCH(shape),
            pltpu.SemaphoreType.DMA((1 + chans,)),
        ],
        compiler_params=pltpu.CompilerParams(vmem_limit_bytes=48 * 2**20),
        name="up",
    )(in_hbm(sweeps), value, right, coarse, *received)


def local(target, grad_x, grad_y, labels, sweeps):
    parts, around_globe = lax.axis_size("lat"), lax.axis_size("lon")
    value, right, coarse, *sent = down(parts, sweeps, target, grad_x, grad_y, labels)
    eastward_pairs = [(i, (i + 1) % around_globe) for i in range(around_globe)]
    westward_pairs = [(j, i) for i, j in eastward_pairs]
    if parts == 2:
        def across(pairs):
            return [(2 * i + k, 2 * j + 1 - k) for i, j in pairs for k in range(2)]

        packed, east, east_across, west, west_across = sent
        packed = lax.ppermute(packed, "lat", [(0, 1), (1, 0)])
        from_west = lax.ppermute(east, "lon", eastward_pairs)
        across_west = lax.ppermute(east_across, ("lon", "lat"), across(eastward_pairs))
        from_east = lax.ppermute(west, "lon", westward_pairs)
        across_east = lax.ppermute(west_across, ("lon", "lat"), across(westward_pairs))
        received = (packed, from_west, across_west, from_east, across_east)
        return up(parts, target.shape, sweeps, value, right, coarse, *received)

    chans, half_rows = coarse.shape[:2]
    coarse = coarse.reshape(chans, half_rows, -1, LANES).transpose(0, 2, 1, 3)

    def shared_lon(field):
        parts_of = [field[:, k] for k in range(field.shape[1])]
        from_west = lax.ppermute(eastward(parts_of[-2], parts_of[-1]), "lon", eastward_pairs)
        from_east = lax.ppermute(westward(parts_of[0], parts_of[-1]), "lon", westward_pairs)
        return jnp.stack(with_edges(parts_of, from_west, from_east), 1)

    value, right, coarse = (shared_lon(f) for f in (value, right, coarse))
    if parts > 2:
        rows = target.shape[1]
        spare = 2 * SUBLANES
        southward = [(i, i + 1) for i in range(parts - 1)]
        northward = [(i + 1, i) for i in range(parts - 1)]

        def shared_lat(field):
            north = lax.ppermute(field[:, :, rows:], "lat", southward)
            south = lax.ppermute(field[:, :, :spare], "lat", northward)
            zeros = jnp.zeros_like(south)
            return field + jnp.concatenate([north, zeros], 2) + jnp.concatenate([zeros, south], 2)

        value, right = shared_lat(value), shared_lat(right)
        every = lax.all_gather(coarse, "lat")
        step = rows // 2
        total = jnp.zeros((chans, coarse.shape[1], parts * step + SUBLANES, LANES), jnp.float32)
        for i in range(parts):
            total = total.at[:, :, i * step:i * step + step + SUBLANES].add(every[i])
        coarse = total[:, :, 4:-4]
    coarse = coarse.transpose(0, 2, 1, 3).reshape(chans, coarse.shape[2], -1)
    return up(parts, target.shape, sweeps, value, right, coarse)


def solution(mesh):
    in_specs = (
        P(None, "lat", "lon"),
        P(None, None, "lat", "lon"),
        P(None, None, "lat", "lon"),
        P("lat", "lon"),
        P(),
    )
    out_specs = P(None, "lat", "lon")
    return jax.shard_map(local, mesh=mesh, in_specs=in_specs, out_specs=out_specs, check_vma=False)
```

time: 208 us -> 18.3 us (0.09); the launches traced: 204 us -> 18.7 us
  starting transfers between devices: 70.8 us -> 9.02 us
  waiting for transfers between devices: 58.7 us -> 1.56 us
  local copies, waits for them, and re-layouts: 43.3 us -> 0 us
  other arithmetic: 18.9 us -> 0 us
  loops' own time: 11.5 us -> 0 us
  Pallas kernels: 0 us -> 8.08 us
    ppermute x38 -> x5, starting transfers between devices: 70.8 us -> 9.02 us  [the longest x1 3 us: local(): packed = lax.ppermute(packed, 'lat', [(0, 1), (1, 0)])]
    ppermute x38 -> x5, waiting for transfers between devices: 58.7 us -> 1.56 us  [the longest x1 0.8 us: local(): lax.ppermute(east_across, ('lon', 'lat'), across(eastward_pairs))]
    reshape x4 -> x0, local copies, waits for them, and re-layouts: 30.5 us -> none  [the longest x2 17.9 us: restrict(): return field.reshape(chans, rows // 2, 2, cols // 2, 2).mean(axis=(2, 4))]
    another operation x5 -> x0, loops' own time: 11.5 us -> none  [smooth(): value = lax.fori_loop(0, count, sweep_wide, value)]
    another operation x2 -> x0, local copies, waits for them, and re-layouts: 8.5 us -> none  [prolong_from(): jnp.stack([jnp.stack([f00, f01], -1), jnp.stack([f10, f11], -1)], 2)]
    pallas_call x0 -> x2, Pallas kernels: none -> 8.08 us  [the longest x1 4.71 us: up(): pl.pallas_call(functools.partial(up_kernel, parts), in_specs=[HBM] + [VME...]
    reduce_sum x2 -> x0, other arithmetic: 6.77 us -> none  [restrict(): return field.reshape(chans, rows // 2, 2, cols // 2, 2).mean(axis=(2, 4))]
    slice x24 -> x0, local copies, waits for them, and re-layouts: 3.41 us -> none  [the longest x1 1.43 us: cycle(): count = sweeps[level]]
  transfers between devices with their start and end apart: 38 -> 5, of which waited for: 24 -> 2; matrix products, arithmetic and copies ran while one was open for 1% -> 0% of each run, Pallas kernels for 0% -> 0%
where the time goes in v5:
time: 18.3 us; the launch traced here: 18.7 us
  starting transfers between devices  9.02 us (49%)
  Pallas kernels  8.08 us (44%)
  waiting for transfers between devices  1.56 us (9%)
    pallas_call x1, Pallas kernels, up(): pl.pallas_call(functools.partial(up_kernel, parts), in_specs=[HBM] + [VME...  4.71 us
    pallas_call x1, Pallas kernels, down(): pl.pallas_call(functools.partial(down_kernel, parts), in_specs=[HBM] * 5,...  3.37 us
    ppermute x1, starting transfers between devices, local(): packed = lax.ppermute(packed, 'lat', [(0, 1), (1, 0)])  3 us
    ppermute x1, starting transfers between devices, local(): from_east = lax.ppermute(west, 'lon', westward_pairs)  2.66 us
    ppermute x1, starting transfers between devices, local(): lax.ppermute(east_across, ('lon', 'lat'), across(eastward_pairs))  1.78 us
    ppermute x1, starting transfers between devices, local(): lax.ppermute(west_across, ('lon', 'lat'), across(westward_pairs))  1.57 us
    ppermute x1, waiting for transfers between devices, local(): lax.ppermute(east_across, ('lon', 'lat'), across(eastward_pairs))  0.8 us
    ppermute x1, waiting for transfers between devices, local(): lax.ppermute(west_across, ('lon', 'lat'), across(westward_pairs))  0.75 us
  transfers between devices with their start and end apart: 5, of which 2 were waited for; matrix products, arithmetic and copies ran while one was open for 0% of the time, Pallas kernels for 0%

profile of v5, /device:TPU:0, one launch (start us, length us, event | category | flops | bytes accessed | tf_op | source)
XLA Modules:
  0.0 18.7 jit_solution(5964427584509320197)
XLA Ops:
  0.0 3.4 %down.1 = (f32[3,9,24,128]{3,2,1,0:T(8,128)S(1)}, f32[3,9,24,128]{3,2,1,0:T(8,128)S(1)}, f32[3,12,640]{2,1,0:T(8,128)S(1)}, f32[3,19,8,128]{3,2,1,0:T(8,128)S(1)...) custom-call(s32[3]{0:T(128)} %sweeps_hbm.3, ...), custom_call_target="tpu_custom_call" | custom-call | tf_op jit(solution)/shard_map/down/pallas_call | solution.py:379
  3.4 3.0 %collective-permute-start = (f32[3,19,8,128]{3,2,1,0:T(8,128)S(1)}, f32[3,19,8,128]{3,2,1,0:T(8,128)S(1)}, u32[]{:S(2)}, u32[]{:S(2)}) collective-permute-start(f32[3,19,8,128]{3,2,1,0:T(8,128)S(1)} %get-tuple-element.16), channel_id=1, source_target_pairs={{0,1},{1,0},{2,3},{3,2},{4,5},{5,4},{6,7},{7,6},{8,9},{9,8},{10,11... | collective-permute-start | bytes 700424 | tf_op jit(solution)/shard_map/ppermute | solution.py:551
  6.4 0.0 collective-permute-start.1
  6.4 1.8 %collective-permute-start.2 = (f32[3,8,128]{2,1,0:T(8,128)S(1)}, f32[3,8,128]{2,1,0:T(8,128)S(1)}, u32[]{:S(2)}, u32[]{:S(2)}) collective-permute-start(f32[3,8,128]{2,1,0:T(8,128)S(1)} %get-tuple-element.18), channel_id=1, source_target_pairs={{0,3},{1,2},{2,5},{3,4},{4,7},{5,6},{6,9},{7,8},{8,11},{9,10},{10,... | collective-permute-start | bytes 36872 | tf_op jit(solution)/shard_map/ppermute | solution.py:553
  8.2 2.7 %collective-permute-start.3 = (f32[3,8,128]{2,1,0:T(8,128)S(1)}, f32[3,8,128]{2,1,0:T(8,128)S(1)}, u32[]{:S(2)}, u32[]{:S(2)}) collective-permute-start(f32[3,8,128]{2,1,0:T(8,128)S(1)} %get-tuple-element.19), channel_id=1, source_target_pairs={{2,0},{4,2},{6,4},{8,6},{10,8},{12,10},{14,12},{16,14},{18,16},{20... | collective-permute-start | bytes 36872 | tf_op jit(solution)/shard_map/ppermute | solution.py:554
  10.8 1.6 %collective-permute-start.4 = (f32[3,8,128]{2,1,0:T(8,128)S(1)}, f32[3,8,128]{2,1,0:T(8,128)S(1)}, u32[]{:S(2)}, u32[]{:S(2)}) collective-permute-start(f32[3,8,128]{2,1,0:T(8,128)S(1)} %get-tuple-element.20), channel_id=1, source_target_pairs={{2,1},{3,0},{4,3},{5,2},{6,5},{7,4},{8,7},{9,6},{10,9},{11,8},{12,... | collective-permute-start | bytes 36872 | tf_op jit(solution)/shard_map/ppermute | solution.py:555
  12.4 0.0 collective-permute-done.1.refs_1_
  12.4 0.8 %collective-permute-done.2.refs_2_ = f32[3,8,128]{2,1,0:T(8,128)S(1)} collective-permute-done((f32[3,8,128]{2,1,0:T(8,128)S(1)}, f32[3,8,128]{2,1,0:T(8,128)S(1)}, u32[]{:S(2)}, u32[]{:S(2)}) %collective-permute-start.2) | collective-permute-done | bytes 12320 | tf_op jit(solution)/shard_map/ppermute | solution.py:553
  13.2 0.0 collective-permute-done.3.refs_3_
  13.2 0.7 %collective-permute-done.4.refs_4_ = f32[3,8,128]{2,1,0:T(8,128)S(1)} collective-permute-done((f32[3,8,128]{2,1,0:T(8,128)S(1)}, f32[3,8,128]{2,1,0:T(8,128)S(1)}, u32[]{:S(2)}, u32[]{:S(2)}) %collective-permute-start.4) | collective-permute-done | bytes 12320 | tf_op jit(solution)/shard_map/ppermute | solution.py:555
  14.0 0.0 collective-permute-done.refs_0_
  14.0 4.7 %up.1 = f32[3,16,1024]{2,1,0:T(8,128)} custom-call(s32[3]{0:T(128)} %sweeps_hbm.3, f32[3,9,24,128]{3,2,1,0:T(8,128)S(1)} %get-tuple-element.13.value_ref, f32[3,9,24,128]{3,2,1,0:T(8,128)S(1)} %get-tuple-element.14.right_ref, f32[3,12,640]{2,1,0:T(8,128)S(1)} %get-tuple-element.15.coarse_ref, f32[3,19,8,128]{3,2,1,0:T(8,128)S(1)} %collective-permute-done.refs_0_, ...), custom_call_target="tpu_custom_call" | custom-call | tf_op jit(solution)/shard_map/up/pallas_call | solution.py:519
Async XLA Ops:
  3.4 10.6 %collective-permute-start = (f32[3,19,8,128]{3,2,1,0:T(8,128)S(1)}, f32[3,19,8,128]{3,2,1,0:T(8,128)S(1)}, u32[]{:S(2)}, u32[]{:S(2)}) collective-permute-start(f32[3,19,8,128]{3,2,1,0:T(8,128)S(1)} %get-tuple-element.16), channel_id=1, source_target_pairs={{0,1},{1,0},{2,3},{3,2},{4,5},{5,4},{6,7},{7,6},{8,9},{9,8},{10,11... | collective-permute-start | bytes 700424 | tf_op jit(solution)/shard_map/ppermute | solution.py:551
  6.4 6.0 %collective-permute-start.1 = (f32[3,8,128]{2,1,0:T(8,128)S(1)}, f32[3,8,128]{2,1,0:T(8,128)S(1)}, u32[]{:S(2)}, u32[]{:S(2)}) collective-permute-start(f32[3,8,128]{2,1,0:T(8,128)S(1)} %get-tuple-element.17), channel_id=1, source_target_pairs={{0,2},{2,4},{4,6},{6,8},{8,10},{10,12},{12,14},{14,16},{16,18},{18... | collective-permute-start | bytes 36872 | tf_op jit(solution)/shard_map/ppermute | solution.py:552
  6.4 6.8 %collective-permute-start.2 = (f32[3,8,128]{2,1,0:T(8,128)S(1)}, f32[3,8,128]{2,1,0:T(8,128)S(1)}, u32[]{:S(2)}, u32[]{:S(2)}) collective-permute-start(f32[3,8,128]{2,1,0:T(8,128)S(1)} %get-tuple-element.18), channel_id=1, source_target_pairs={{0,3},{1,2},{2,5},{3,4},{4,7},{5,6},{6,9},{7,8},{8,11},{9,10},{10,... | collective-permute-start | bytes 36872 | tf_op jit(solution)/shard_map/ppermute | solution.py:553
  8.2 5.0 %collective-permute-start.3 = (f32[3,8,128]{2,1,0:T(8,128)S(1)}, f32[3,8,128]{2,1,0:T(8,128)S(1)}, u32[]{:S(2)}, u32[]{:S(2)}) collective-permute-start(f32[3,8,128]{2,1,0:T(8,128)S(1)} %get-tuple-element.19), channel_id=1, source_target_pairs={{2,0},{4,2},{6,4},{8,6},{10,8},{12,10},{14,12},{16,14},{18,16},{20... | collective-permute-start | bytes 36872 | tf_op jit(solution)/shard_map/ppermute | solution.py:554
  10.8 3.1 %collective-permute-start.4 = (f32[3,8,128]{2,1,0:T(8,128)S(1)}, f32[3,8,128]{2,1,0:T(8,128)S(1)}, u32[]{:S(2)}, u32[]{:S(2)}) collective-permute-start(f32[3,8,128]{2,1,0:T(8,128)S(1)} %get-tuple-element.20), channel_id=1, source_target_pairs={{2,1},{3,0},{4,3},{5,2},{6,5},{7,4},{8,7},{9,6},{10,9},{11,8},{12,... | collective-permute-start | bytes 36872 | tf_op jit(solution)/shard_map/ppermute | solution.py:555

commit v6 on v5

--- a/solution.py
+++ b/solution.py
@@ -309,10 +309,11 @@
         return out
 
     blank = jnp.zeros((rows, LANES), jnp.float32)
-    paired = []
+    fields = []
     for chan in range(chans):
         for copy in copies[chan]:
             copy.wait()
+    for chan in range(chans):
         own = jnp.concatenate([target_v[chan], blank], 1)
         sel_x = jnp.concatenate([chosen(grad_x_v, chan), blank], 1)
         sel_y = jnp.concatenate([chosen(grad_y_v, chan), blank], 1)
@@ -324,23 +325,29 @@
             b_ref[chan, k, pl.ds(start, rows), :] = b
             if window > rows:
                 b_ref[chan, k, pl.ds(start + rows, SUBLANES), :] = s
-        planes = load_planes(v_ref.at[chan], 0, count, SUBLANES)
+    for chan in range(chans):
+        fields.append(tuple(load_planes(v_ref.at[chan], 0, count, SUBLANES)))
         right = load_planes(b_ref.at[chan], 0, count, SUBLANES)
         if inside is not None:
             right = [b * mask for b, mask in zip(right, inside)]
         store_planes(right_ref.at[chan], 0, right)
         for t in range(count):
-            scaled_ref[t] = (DAMPING / diagonal(scale)) * right[t]
-
-        def step(_, planes):
-            return sweep(planes, [scaled_ref[t] for t in range(count)], scale, inside)
-
-        planes = lax.fori_loop(0, sweeps[0], step, tuple(planes))
+            scaled_ref[chan, t] = (DAMPING / diagonal(scale)) * right[t]
+
+    def step(_, fields):
+        return tuple(
+            sweep(planes, [scaled_ref[chan, t] for t in range(count)], scale, inside) for chan, planes in enumerate(fields)
+        )
+
+    fields = lax.fori_loop(0, sweeps[0], step, tuple(fields))
+    paired = []
+    for chan, planes in enumerate(fields):
         store_planes(value_ref.at[chan], 0, planes)
-        left = residual(planes, [(diagonal(scale) / DAMPING) * scaled_ref[t] for t in range(count)], scale)
+        left = residual(planes, [(diagonal(scale) / DAMPING) * scaled_ref[chan, t] for t in range(count)], scale)
         if inside is not None:
             left = [r * mask for r, mask in zip(left, inside)]
         store_planes(resid_ref.at[chan], 0, left)
+    for chan in range(chans):
         north, south = load_planes(resid_ref.at[chan], 0, 2, window // 2)
         paired.append(north + south)
     coarse = pair_columns(paired, places)
@@ -389,7 +396,7 @@
             pltpu.VMEM(labels.shape, jnp.int32),
             SCRATCH((chans, wide, window + spare, LANES)),
             SCRATCH((chans, wide, window + spare, LANES)),
-            SCRATCH((window // SUBLANES, SUBLANES, wide * LANES)),
+            SCRATCH((chans, window // SUBLANES, SUBLANES, wide * LANES)),
             SCRATCH((chans, wide, window, LANES)),
             pltpu.SemaphoreType.DMA((chans + 1, 3)),
         ],
@@ -484,22 +491,28 @@
     mid = [[v + f for v, f in zip(planes, fix)] for planes, fix in zip(mid, prolong(fix2, spread_places))]
     mid = smoothed(mid, k1_ref, sweeps[1], 0.25)
     spare = (fix_ref.shape[2] - full) // 2
+    if spare:
+        fix_ref[...] = jnp.zeros_like(fix_ref)
     for i, fix in enumerate(prolong(mid, spread_places)):
         store_planes(fix_ref.at[i], spare, fix)
     shown = pl.multiple_of((SUBLANES if parts == 2 else rows) * place, SUBLANES)
     start = own_start(parts, place)
-    out_copies = []
+    fields = []
     for i in range(chans):
         planes = load_planes(v0_ref.at[i], 0, count0, SUBLANES)
         fix = load_planes(fix_ref.at[i], shown, count0, SUBLANES)
-        planes = tuple(v + f for v, f in zip(planes, fix))
+        fields.append(tuple(v + f for v, f in zip(planes, fix)))
         for t, b in enumerate(load_planes(b0_ref.at[i], 0, count0, SUBLANES)):
-            k0_ref[t] = (DAMPING / diagonal(1.0)) * b
-
-        def step(_, planes):
-            return sweep(planes, [k0_ref[t] for t in range(count0)], 1.0, inside)
-
-        planes = lax.fori_loop(0, sweeps[0], step, planes)
+            k0_ref[i, t] = (DAMPING / diagonal(1.0)) * b
+
+    def step(_, fields):
+        return tuple(
+            sweep(planes, [k0_ref[i, t] for t in range(count0)], 1.0, inside) for i, planes in enumerate(fields)
+        )
+
+    fields = lax.fori_loop(0, sweeps[0], step, tuple(fields))
+    out_copies = []
+    for i, planes in enumerate(fields):
         store_planes(v0_ref.at[i], 0, planes)
         for k in range(cols // LANES):
             out_ref[i, :, k * LANES:(k + 1) * LANES] = v0_ref[i, k, pl.ds(start, rows), :]
@@ -525,7 +538,7 @@
             pltpu.SMEM(sweeps.shape, jnp.int32),
             SCRATCH(value.shape),
             SCRATCH(value.shape),
-            SCRATCH((window // SUBLANES, SUBLANES, wide * LANES)),
+            SCRATCH((chans, window // SUBLANES, SUBLANES, wide * LANES)),
             SCRATCH((chans, half, full // 2, LANES)),
             SCRATCH((chans, count1, full // 2 // count1, half * LANES)),
             SCRATCH((chans, count2, full // 4 // count2, quarter * LANES)),

time: 18.3 us -> 17.3 us (0.945); the launches traced: 18.7 us -> 17.1 us
  Pallas kernels: 8.08 us -> 6.55 us
    pallas_call x1, Pallas kernels: 4.71 us -> 3.82 us  [up(): pl.pallas_call(functools.partial(up_kernel, parts), in_specs=[HBM] + [VME...]
    pallas_call x1, Pallas kernels: 3.37 us -> 2.72 us  [down(): pl.pallas_call(functools.partial(down_kernel, parts), in_specs=[HBM] * 5,...]
where the time goes in v6:
time: 17.3 us; the launch traced here: 17.1 us
  starting transfers between devices  9.02 us (52%)
  Pallas kernels  6.55 us (38%)
  waiting for transfers between devices  1.55 us (9%)
    pallas_call x1, Pallas kernels, up(): pl.pallas_call(functools.partial(up_kernel, parts), in_specs=[HBM] + [VME...  3.82 us
    ppermute x1, starting transfers between devices, local(): packed = lax.ppermute(packed, 'lat', [(0, 1), (1, 0)])  3 us
    pallas_call x1, Pallas kernels, down(): pl.pallas_call(functools.partial(down_kernel, parts), in_specs=[HBM] * 5,...  2.72 us
    ppermute x1, starting transfers between devices, local(): from_east = lax.ppermute(west, 'lon', westward_pairs)  2.67 us
    ppermute x1, starting transfers between devices, local(): lax.ppermute(east_across, ('lon', 'lat'), across(eastward_pairs))  1.77 us
    ppermute x1, starting transfers between devices, local(): lax.ppermute(west_across, ('lon', 'lat'), across(westward_pairs))  1.57 us
    ppermute x1, waiting for transfers between devices, local(): lax.ppermute(east_across, ('lon', 'lat'), across(eastward_pairs))  0.8 us
    ppermute x1, waiting for transfers between devices, local(): lax.ppermute(west_across, ('lon', 'lat'), across(westward_pairs))  0.74 us
  transfers between devices with their start and end apart: 5, of which 2 were waited for; matrix products, arithmetic and copies ran while one was open for 0% of the time, Pallas kernels for 0%

profile of v6, /device:TPU:0, one launch (start us, length us, event | category | flops | bytes accessed | tf_op | source)
XLA Modules:
  0.0 17.1 jit_solution(18166595257274960393)
XLA Ops:
  0.0 2.7 %down.1 = (f32[3,9,24,128]{3,2,1,0:T(8,128)S(1)}, f32[3,9,24,128]{3,2,1,0:T(8,128)S(1)}, f32[3,12,640]{2,1,0:T(8,128)S(1)}, f32[3,19,8,128]{3,2,1,0:T(8,128)S(1)...) custom-call(s32[3]{0:T(128)} %sweeps_hbm.3, ...), custom_call_target="tpu_custom_call" | custom-call | tf_op jit(solution)/shard_map/down/pallas_call | solution.py:386
  2.7 3.0 %collective-permute-start = (f32[3,19,8,128]{3,2,1,0:T(8,128)S(1)}, f32[3,19,8,128]{3,2,1,0:T(8,128)S(1)}, u32[]{:S(2)}, u32[]{:S(2)}) collective-permute-start(f32[3,19,8,128]{3,2,1,0:T(8,128)S(1)} %get-tuple-element.16), channel_id=1, source_target_pairs={{0,1},{1,0},{2,3},{3,2},{4,5},{5,4},{6,7},{7,6},{8,9},{9,8},{10,11... | collective-permute-start | bytes 700424 | tf_op jit(solution)/shard_map/ppermute | solution.py:564
  5.7 0.0 collective-permute-start.1
  5.7 1.8 %collective-permute-start.2 = (f32[3,8,128]{2,1,0:T(8,128)S(1)}, f32[3,8,128]{2,1,0:T(8,128)S(1)}, u32[]{:S(2)}, u32[]{:S(2)}) collective-permute-start(f32[3,8,128]{2,1,0:T(8,128)S(1)} %get-tuple-element.18), channel_id=1, source_target_pairs={{0,3},{1,2},{2,5},{3,4},{4,7},{5,6},{6,9},{7,8},{8,11},{9,10},{10,... | collective-permute-start | bytes 36872 | tf_op jit(solution)/shard_map/ppermute | solution.py:566
  7.5 2.7 %collective-permute-start.3 = (f32[3,8,128]{2,1,0:T(8,128)S(1)}, f32[3,8,128]{2,1,0:T(8,128)S(1)}, u32[]{:S(2)}, u32[]{:S(2)}) collective-permute-start(f32[3,8,128]{2,1,0:T(8,128)S(1)} %get-tuple-element.19), channel_id=1, source_target_pairs={{2,0},{4,2},{6,4},{8,6},{10,8},{12,10},{14,12},{16,14},{18,16},{20... | collective-permute-start | bytes 36872 | tf_op jit(solution)/shard_map/ppermute | solution.py:567
  10.2 1.6 %collective-permute-start.4 = (f32[3,8,128]{2,1,0:T(8,128)S(1)}, f32[3,8,128]{2,1,0:T(8,128)S(1)}, u32[]{:S(2)}, u32[]{:S(2)}) collective-permute-start(f32[3,8,128]{2,1,0:T(8,128)S(1)} %get-tuple-element.20), channel_id=1, source_target_pairs={{2,1},{3,0},{4,3},{5,2},{6,5},{7,4},{8,7},{9,6},{10,9},{11,8},{12,... | collective-permute-start | bytes 36872 | tf_op jit(solution)/shard_map/ppermute | solution.py:568
  11.8 0.0 collective-permute-done.1.refs_1_
  11.8 0.8 %collective-permute-done.2.refs_2_ = f32[3,8,128]{2,1,0:T(8,128)S(1)} collective-permute-done((f32[3,8,128]{2,1,0:T(8,128)S(1)}, f32[3,8,128]{2,1,0:T(8,128)S(1)}, u32[]{:S(2)}, u32[]{:S(2)}) %collective-permute-start.2) | collective-permute-done | bytes 12320 | tf_op jit(solution)/shard_map/ppermute | solution.py:566
  12.6 0.0 collective-permute-done.3.refs_3_
  12.6 0.7 %collective-permute-done.4.refs_4_ = f32[3,8,128]{2,1,0:T(8,128)S(1)} collective-permute-done((f32[3,8,128]{2,1,0:T(8,128)S(1)}, f32[3,8,128]{2,1,0:T(8,128)S(1)}, u32[]{:S(2)}, u32[]{:S(2)}) %collective-permute-start.4) | collective-permute-done | bytes 12320 | tf_op jit(solution)/shard_map/ppermute | solution.py:568
  13.3 0.0 collective-permute-done.refs_0_
  13.3 3.8 %up.1 = f32[3,16,1024]{2,1,0:T(8,128)} custom-call(s32[3]{0:T(128)} %sweeps_hbm.3, f32[3,9,24,128]{3,2,1,0:T(8,128)S(1)} %get-tuple-element.13.value_ref, f32[3,9,24,128]{3,2,1,0:T(8,128)S(1)} %get-tuple-element.14.right_ref, f32[3,12,640]{2,1,0:T(8,128)S(1)} %get-tuple-element.15.coarse_ref, f32[3,19,8,128]{3,2,1,0:T(8,128)S(1)} %collective-permute-done.refs_0_, ...), custom_call_target="tpu_custom_call" | custom-call | tf_op jit(solution)/shard_map/up/pallas_call | solution.py:532
Async XLA Ops:
  2.7 10.6 %collective-permute-start = (f32[3,19,8,128]{3,2,1,0:T(8,128)S(1)}, f32[3,19,8,128]{3,2,1,0:T(8,128)S(1)}, u32[]{:S(2)}, u32[]{:S(2)}) collective-permute-start(f32[3,19,8,128]{3,2,1,0:T(8,128)S(1)} %get-tuple-element.16), channel_id=1, source_target_pairs={{0,1},{1,0},{2,3},{3,2},{4,5},{5,4},{6,7},{7,6},{8,9},{9,8},{10,11... | collective-permute-start | bytes 700424 | tf_op jit(solution)/shard_map/ppermute | solution.py:564
  5.7 6.0 %collective-permute-start.1 = (f32[3,8,128]{2,1,0:T(8,128)S(1)}, f32[3,8,128]{2,1,0:T(8,128)S(1)}, u32[]{:S(2)}, u32[]{:S(2)}) collective-permute-start(f32[3,8,128]{2,1,0:T(8,128)S(1)} %get-tuple-element.17), channel_id=1, source_target_pairs={{0,2},{2,4},{4,6},{6,8},{8,10},{10,12},{12,14},{14,16},{16,18},{18... | collective-permute-start | bytes 36872 | tf_op jit(solution)/shard_map/ppermute | solution.py:565
  5.7 6.8 %collective-permute-start.2 = (f32[3,8,128]{2,1,0:T(8,128)S(1)}, f32[3,8,128]{2,1,0:T(8,128)S(1)}, u32[]{:S(2)}, u32[]{:S(2)}) collective-permute-start(f32[3,8,128]{2,1,0:T(8,128)S(1)} %get-tuple-element.18), channel_id=1, source_target_pairs={{0,3},{1,2},{2,5},{3,4},{4,7},{5,6},{6,9},{7,8},{8,11},{9,10},{10,... | collective-permute-start | bytes 36872 | tf_op jit(solution)/shard_map/ppermute | solution.py:566
  7.5 5.1 %collective-permute-start.3 = (f32[3,8,128]{2,1,0:T(8,128)S(1)}, f32[3,8,128]{2,1,0:T(8,128)S(1)}, u32[]{:S(2)}, u32[]{:S(2)}) collective-permute-start(f32[3,8,128]{2,1,0:T(8,128)S(1)} %get-tuple-element.19), channel_id=1, source_target_pairs={{2,0},{4,2},{6,4},{8,6},{10,8},{12,10},{14,12},{16,14},{18,16},{20... | collective-permute-start | bytes 36872 | tf_op jit(solution)/shard_map/ppermute | solution.py:567
  10.2 3.1 %collective-permute-start.4 = (f32[3,8,128]{2,1,0:T(8,128)S(1)}, f32[3,8,128]{2,1,0:T(8,128)S(1)}, u32[]{:S(2)}, u32[]{:S(2)}) collective-permute-start(f32[3,8,128]{2,1,0:T(8,128)S(1)} %get-tuple-element.20), channel_id=1, source_target_pairs={{2,1},{3,0},{4,3},{5,2},{6,5},{7,4},{8,7},{9,6},{10,9},{11,8},{12,... | collective-permute-start | bytes 36872 | tf_op jit(solution)/shard_map/ppermute | solution.py:568

commit v7 on v6

--- a/solution.py
+++ b/solution.py
@@ -72,9 +72,10 @@
 
 def sweep(planes, scaled, scale, inside=None):
     beside = DAMPING * scale / diagonal(scale)
-    planes = [
-        (1.0 - DAMPING) * value + (right + beside * total) for value, right, total in zip(planes, scaled, around(planes))
-    ]
+    totals = [beside * total for total in around(planes)]
+    if scaled is not None:
+        totals = [right + total for right, total in zip(scaled, totals)]
+    planes = [(1.0 - DAMPING) * value + total for value, total in zip(planes, totals)]
     return tuple(planes if inside is None else [value * mask for value, mask in zip(planes, inside)])
 
 
@@ -196,8 +197,8 @@
     return [first] + list(parts[1:-2]) + [last, halo]
 
 
-COARSE_WIDTH, FINE_WIDTH, REACH = 32, 8, 4
-TO_EAST, TO_WEST = -24, -8
+COARSE_WIDTH, FINE_WIDTH = 32, 8
+TO_EAST, TO_WEST = (-24, 0), (-8, -8)
 
 
 def in_window(lane, start, width):
@@ -206,13 +207,9 @@
     return (lane >= start) & (lane < end) if end <= LANES else (lane >= start) | (lane < end - LANES)
 
 
-def slots(value_rows, right_rows, coarse_rows, coarse_start):
+def slots(heights, starts):
     out, at = [], 0
-    for which, rows, start, width in (
-        (2, coarse_rows, coarse_start, COARSE_WIDTH),
-        (0, value_rows, -REACH, FINE_WIDTH),
-        (1, right_rows, -REACH, FINE_WIDTH),
-    ):
+    for which, (rows, start, width) in enumerate(zip(heights, starts, (COARSE_WIDTH, FINE_WIDTH))):
         for first in range(0, rows, SUBLANES):
             out.append((which, first, min(SUBLANES, rows - first), start, width, at))
             at += width
@@ -220,10 +217,10 @@
     return out
 
 
-def bundle(fields, coarse_start):
+def bundle(fields, starts):
     out = jnp.zeros((SUBLANES, LANES), jnp.float32)
     lane = lanes_of(out)
-    for which, first, rows, start, width, at in slots(*(f.shape[0] for f in fields), coarse_start):
+    for which, first, rows, start, width, at in slots([f.shape[0] for f in fields], starts):
         piece = fields[which][first:first + rows]
         if rows < SUBLANES:
             piece = jnp.concatenate([piece, jnp.zeros((SUBLANES - rows, LANES), jnp.float32)], 0)
@@ -231,48 +228,44 @@
     return out
 
 
-def unbundle(tile, heights, coarse_start):
+def unbundle(tile, heights, starts):
     lane = lanes_of(tile)
-    pieces = ([], [], [])
-    for which, first, rows, start, width, at in slots(*heights, coarse_start):
+    pieces = [[] for _ in heights]
+    for which, first, rows, start, width, at in slots(heights, starts):
         piece = jnp.where(in_window(lane, start, width), pltpu.roll(tile, (start - at) % LANES, 1), 0.0)
         pieces[which].append(piece[:rows])
     return [jnp.concatenate(p, 0) if len(p) > 1 else p[0] for p in pieces]
 
 
-VALUE_ROWS, RIGHT_ROWS, COARSE_ROWS = 8, 4, 12
-ACROSS = (VALUE_ROWS, RIGHT_ROWS, COARSE_ROWS)
-
-
-def pack(value, right, coarse):
-    halves = right[:-1] + [c[SUBLANES:] for c in coarse[:-1]]
+COARSE_ROWS, FINE_ROWS = 12, 8
+
+
+def pack(coarse, fine):
+    halves = [c[SUBLANES:] for c in coarse[:-1]]
     joined = [jnp.concatenate(halves[k:k + 2], 0) for k in range(0, len(halves), 2)]
-    return value[:-1] + [c[:SUBLANES] for c in coarse[:-1]] + joined + [bundle([value[-1], right[-1], coarse[-1]], TO_WEST)]
-
-
-def packed_tiles(fine, coarse):
-    return fine + coarse + (fine + coarse) // 2 + 1
-
-
-def unpack(tile, fine, coarse):
+    return fine + [c[:SUBLANES] for c in coarse[:-1]] + joined + [bundle([coarse[-1]], TO_WEST)]
+
+
+def packed_tiles(coarse, fine):
+    return fine + coarse + coarse // 2 + 1
+
+
+def unpack_coarse(tile, coarse, fine):
     halves = []
-    for k in range(fine + coarse, fine + coarse + (fine + coarse) // 2):
+    for k in range(fine + coarse, fine + coarse + coarse // 2):
         both = tile(k)
         halves += [both[:4], both[4:]]
-    value = [tile(k) for k in range(fine)]
-    right = halves[:fine]
-    low = [jnp.concatenate([tile(fine + k), halves[fine + k]], 0) for k in range(coarse)]
-    ends = unbundle(tile(packed_tiles(fine, coarse) - 1), ACROSS, TO_WEST)
-    return [field + [end] for field, end in zip((value, right, low), ends)]
+    low = [jnp.concatenate([tile(fine + k), halves[k]], 0) for k in range(coarse)]
+    return low + unbundle(tile(packed_tiles(coarse, fine) - 1), [COARSE_ROWS], TO_WEST)
 
 
 def down_kernel(parts, sweeps_hbm, target, grad_x, grad_y, labels, *refs):
     sent = 5 if parts == 2 else 0
-    value_ref, right_ref, coarse_ref = refs[:3]
-    sent_refs = refs[3:3 + sent]
-    sweeps, target_v, grad_x_v, grad_y_v, labels_v, v_ref, b_ref, scaled_ref, resid_ref, sems = refs[3 + sent:]
+    fine_ref, coarse_ref = refs[:2]
+    sent_refs = refs[2:2 + sent]
+    sweeps, target_v, grad_x_v, grad_y_v, labels_v, v_ref, b_ref, scaled_ref, resid_ref, sems = refs[2 + sent:]
     chans, rows, cols = target.shape
-    window = value_ref.shape[2]
+    window = fine_ref.shape[2]
     count = window // SUBLANES
     place = lax.axis_index("lat")
     start = own_start(parts, place)
@@ -313,7 +306,6 @@
     for chan in range(chans):
         for copy in copies[chan]:
             copy.wait()
-    for chan in range(chans):
         own = jnp.concatenate([target_v[chan], blank], 1)
         sel_x = jnp.concatenate([chosen(grad_x_v, chan), blank], 1)
         sel_y = jnp.concatenate([chosen(grad_y_v, chan), blank], 1)
@@ -330,7 +322,6 @@
         right = load_planes(b_ref.at[chan], 0, count, SUBLANES)
         if inside is not None:
             right = [b * mask for b, mask in zip(right, inside)]
-        store_planes(right_ref.at[chan], 0, right)
         for t in range(count):
             scaled_ref[chan, t] = (DAMPING / diagonal(scale)) * right[t]
 
@@ -342,7 +333,6 @@
     fields = lax.fori_loop(0, sweeps[0], step, tuple(fields))
     paired = []
     for chan, planes in enumerate(fields):
-        store_planes(value_ref.at[chan], 0, planes)
         left = residual(planes, [(diagonal(scale) / DAMPING) * scaled_ref[chan, t] for t in range(count)], scale)
         if inside is not None:
             left = [r * mask for r, mask in zip(left, inside)]
@@ -350,28 +340,30 @@
     for chan in range(chans):
         north, south = load_planes(resid_ref.at[chan], 0, 2, window // 2)
         paired.append(north + south)
-    coarse = pair_columns(paired, places)
-    for chan in range(chans):
-        low = 0.25 * coarse[chan]
-        coarse_ref[chan] = low
-        if parts != 2:
-            continue
-        packed_ref, east_ref, east_across, west_ref, west_across = sent_refs
-        wide = value_ref.shape[1]
-        value = [value_ref[chan, k] for k in range(wide)]
-        right = [right_ref[chan, k] for k in range(wide)]
-        low = tiles(low)
-        north = place == 0
-        value_border = [jnp.where(north, v[12:20], v[4:12]) for v in value]
-        right_border = [jnp.where(north, b[13:17], b[8:12]) for b in right]
-        for k, tile in enumerate(pack(value_border, right_border, low)):
+    coarse = [0.25 * low for low in pair_columns(paired, places)]
+    for chan in range(chans):
+        coarse_ref[chan] = coarse[chan]
+    fields = lax.fori_loop(0, sweeps[0], step, fields)
+    for chan, planes in enumerate(fields):
+        store_planes(fine_ref.at[chan], 0, planes)
+    if parts != 2:
+        return
+    packed_ref, east_ref, east_across, west_ref, west_across = sent_refs
+    wide = fine_ref.shape[1]
+    for chan in range(chans):
+        low = tiles(coarse[chan])
+        over = [jnp.where(place == 0, fine_ref[chan, k, rows:], fine_ref[chan, k, :SUBLANES]) for k in range(wide)]
+        for k, tile in enumerate(pack(low, over[:-1])):
             packed_ref[chan, k] = tile
-        for east, west, fields in (
-            (east_ref, west_ref, (value, right, low)),
-            (east_across, west_across, (value_border, right_border, low)),
+        to_east, to_west = eastward(low[-2], low[-1]), westward(low[0], low[-1])
+        beside = fine_ref[chan, wide - 1, pl.ds(start, rows), :]
+        for ref, low_edge, fine_edge, starts in (
+            (east_ref, to_east, beside, TO_EAST),
+            (west_ref, to_west, beside, TO_WEST),
+            (east_across, to_east, over[-1], TO_EAST),
+            (west_across, to_west, over[-1], TO_WEST),
         ):
-            east[chan] = bundle([eastward(f[-2], f[-1]) for f in fields], TO_EAST)
-            west[chan] = bundle([westward(f[0], f[-1]) for f in fields], TO_WEST)
+            ref[chan] = bundle([low_edge, fine_edge], starts)
 
 
 def down(parts, sweeps, target, grad_x, grad_y, labels):
@@ -379,9 +371,9 @@
     window = window_of(rows, parts)
     wide, half = cols // LANES + 1, cols // 2 // LANES + 1
     spare = SUBLANES if window > rows else 0
-    outs = [F32((chans, wide, window, LANES))] * 2 + [F32((chans, window // 2, half * LANES))]
+    outs = [F32((chans, wide, window, LANES)), F32((chans, window // 2, half * LANES))]
     if parts == 2:
-        outs.append(F32((chans, packed_tiles(wide - 1, half - 1), SUBLANES, LANES)))
+        outs.append(F32((chans, packed_tiles(half - 1, wide - 1), SUBLANES, LANES)))
         outs += [F32((chans, SUBLANES, LANES))] * 4
     return pl.pallas_call(
         functools.partial(down_kernel, parts),
@@ -411,55 +403,47 @@
     return jnp.where(place == 0, top(own) + bottom(other), bottom(own) + top(other))
 
 
-def up_kernel(parts, sweeps_hbm, value_ref, right_ref, coarse_ref, *refs):
+def up_kernel(parts, sweeps_hbm, fine_ref, coarse_ref, *refs):
     received = 5 if parts == 2 else 0
     packed_ref, *edge_refs = refs[:received] or [None]
-    out_hbm, sweeps, v0_ref, b0_ref, k0_ref, b1_ref, k1_ref, k2_ref, fix_ref, out_ref, sems = refs[received:]
+    out_hbm, sweeps, b1_ref, k1_ref, k2_ref, fix_ref, out_ref, sems = refs[received:]
     sweeps_copy = pltpu.make_async_copy(sweeps_hbm, sweeps, sems.at[0])
     sweeps_copy.start()
     chans, rows, cols = out_ref.shape
-    wide, window = value_ref.shape[1:3]
-    half = coarse_ref.shape[2] // LANES
+    wide, half = cols // LANES, coarse_ref.shape[2] // LANES
+    window = window_of(rows, parts)
     full = parts * rows
-    count0, count1, count2 = window // SUBLANES, max(1, full // 2 // SUBLANES), max(1, full // 4 // SUBLANES)
+    count0, count1, count2 = window // SUBLANES, full // 2 // SUBLANES, full // 4 // SUBLANES
     place = lax.axis_index("lat")
+    start = own_start(parts, place)
     inside = band_masks(window, parts, place, rows)
-    own_heights = (window, window, window // 2)
 
     def sides(chan, across):
-        heights = ACROSS if across else own_heights
+        heights = (COARSE_ROWS, FINE_ROWS if across else rows)
         from_west = unbundle(edge_refs[across][chan], heights, TO_EAST)
         from_east = unbundle(edge_refs[2 + across][chan], heights, TO_WEST)
         return list(zip(from_west, from_east))
 
-    from_partner = []
+    def beside(parts_of, from_west, from_east):
+        return [parts_of[0] + from_west] + parts_of[1:-1] + [parts_of[-1] + from_east]
+
     for chan in range(chans):
         low = coarse_ref[chan]
+        fine = [fine_ref[chan, k, pl.ds(start, rows), :] for k in range(wide)]
         if parts == 2:
             here, there = sides(chan, 0), sides(chan, 1)
-            other = unpack(lambda k: packed_ref[chan, k], wide - 1, half - 1)
-            value, right, other_low = (with_edges(f, *s) for f, s in zip(other, there))
-            low = jnp.concatenate(with_edges(tiles(low), *here[2]), 1)
+            other_low = with_edges(unpack_coarse(lambda k: packed_ref[chan, k], half - 1, wide), *there[0])
+            low = jnp.concatenate(with_edges(tiles(low), *here[0]), 1)
             low = joined(place, low, jnp.concatenate(other_low, 1), full // 2)
-            for ref, own, side in ((v0_ref, value_ref, here[0]), (b0_ref, right_ref, here[1])):
-                for k, tile in enumerate(with_edges([own[chan, k] for k in range(wide)], *side)):
-                    ref[chan, k] = tile
-            from_partner.append((value, right))
-        else:
-            v0_ref[chan] = value_ref[chan]
-            b0_ref[chan] = right_ref[chan]
+            fine = beside(fine, *here[1])
+            other = beside([packed_ref[chan, k] for k in range(wide)], *there[1])
         for k, tile in enumerate(tiles(low)):
             b1_ref[chan, k] = tile
-
-    def add_rows(value_at, right_at):
-        for chan, (value, right) in enumerate(from_partner):
-            for k in range(wide):
-                v0_ref[chan, k, pl.ds(value_at, VALUE_ROWS), :] += value[k]
-                b0_ref[chan, k, pl.ds(right_at, RIGHT_ROWS), :] += right[k]
-
-    if parts == 2:
-        pl.when(place == 0)(lambda: add_rows(12, 16))
-        pl.when(place == 1)(lambda: add_rows(4, 5))
+        for k in range(wide):
+            span = slice(k * LANES, (k + 1) * LANES)
+            out_ref[chan, :, span] = fine[k]
+            if parts == 2:
+                out_ref[chan, pl.ds(SUBLANES - start, SUBLANES), span] += other[k]
 
     def smoothed(fields, scaled_ref, count, scale):
         def step(_, fields):
@@ -476,17 +460,13 @@
         return smoothed(first, scaled_ref, count - 1, scale)
 
     pair_places, spread_places = pairing(), spreading()
-    height1 = full // 2 // count1
-    right1 = [load_planes(b1_ref.at[i], 0, count1, height1) for i in range(chans)]
+    right1 = [load_planes(b1_ref.at[i], 0, count1, SUBLANES) for i in range(chans)]
     sweeps_copy.wait()
     mid = from_zero(right1, k1_ref, sweeps[1], 0.25)
-    left = [residual(f, load_planes(b1_ref.at[i], 0, count1, height1), 0.25) for i, f in enumerate(mid)]
-    if count1 > 1:
-        pairs = [f[t] + f[t + 1] for f in left for t in range(0, count1, 2)]
-        low = [0.25 * v for v in pair_columns(pairs, pair_places)]
-        right2 = [low[i * count2:(i + 1) * count2] for i in range(chans)]
-    else:
-        raise NotImplementedError("one part")
+    left = [residual(f, load_planes(b1_ref.at[i], 0, count1, SUBLANES), 0.25) for i, f in enumerate(mid)]
+    pairs = [f[t] + f[t + 1] for f in left for t in range(0, count1, 2)]
+    low = [0.25 * v for v in pair_columns(pairs, pair_places)]
+    right2 = [low[i * count2:(i + 1) * count2] for i in range(chans)]
     fix2 = from_zero(right2, k2_ref, sweeps[2], 0.0625)
     mid = [[v + f for v, f in zip(planes, fix)] for planes, fix in zip(mid, prolong(fix2, spread_places))]
     mid = smoothed(mid, k1_ref, sweeps[1], 0.25)
@@ -497,63 +477,53 @@
         store_planes(fix_ref.at[i], spare, fix)
     shown = pl.multiple_of((SUBLANES if parts == 2 else rows) * place, SUBLANES)
     start = own_start(parts, place)
-    fields = []
-    for i in range(chans):
-        planes = load_planes(v0_ref.at[i], 0, count0, SUBLANES)
-        fix = load_planes(fix_ref.at[i], shown, count0, SUBLANES)
-        fields.append(tuple(v + f for v, f in zip(planes, fix)))
-        for t, b in enumerate(load_planes(b0_ref.at[i], 0, count0, SUBLANES)):
-            k0_ref[i, t] = (DAMPING / diagonal(1.0)) * b
+    fields = [tuple(load_planes(fix_ref.at[i], shown, count0, SUBLANES)) for i in range(chans)]
 
     def step(_, fields):
-        return tuple(
-            sweep(planes, [k0_ref[i, t] for t in range(count0)], 1.0, inside) for i, planes in enumerate(fields)
-        )
+        return tuple(sweep(planes, None, 1.0, inside) for planes in fields)
 
     fields = lax.fori_loop(0, sweeps[0], step, tuple(fields))
     out_copies = []
     for i, planes in enumerate(fields):
-        store_planes(v0_ref.at[i], 0, planes)
-        for k in range(cols // LANES):
-            out_ref[i, :, k * LANES:(k + 1) * LANES] = v0_ref[i, k, pl.ds(start, rows), :]
+        store_planes(fix_ref.at[i], 0, planes)
+        for k in range(wide):
+            out_ref[i, :, k * LANES:(k + 1) * LANES] += fix_ref[i, k, pl.ds(start, rows), :]
         out_copies.append(pltpu.make_async_copy(out_ref.at[i], out_hbm.at[i], sems.at[1 + i]))
         out_copies[-1].start()
     for copy in out_copies:
         copy.wait()
 
 
-def up(parts, shape, sweeps, value, right, coarse, *received):
+def up(parts, shape, sweeps, fine, coarse, *received):
     chans, rows, cols = shape
-    wide, window = value.shape[1:3]
     full = parts * rows
-    half, quarter = cols // 2 // LANES + 1, cols // 4 // LANES + 1
-    count1, count2 = max(1, full // 2 // SUBLANES), max(1, full // 4 // SUBLANES)
+    wide, half, quarter = cols // LANES + 1, cols // 2 // LANES + 1, cols // 4 // LANES + 1
+    count1, count2 = full // 2 // SUBLANES, full // 4 // SUBLANES
     spare = 2 * SUBLANES if parts > 2 else 0
     return pl.pallas_call(
         functools.partial(up_kernel, parts),
-        in_specs=[HBM] + [VMEM] * (3 + len(received)),
+        in_specs=[HBM] + [VMEM] * (2 + len(received)),
         out_specs=HBM,
         out_shape=F32(shape),
         scratch_shapes=[
             pltpu.SMEM(sweeps.shape, jnp.int32),
-            SCRATCH(value.shape),
-            SCRATCH(value.shape),
-            SCRATCH((chans, window // SUBLANES, SUBLANES, wide * LANES)),
             SCRATCH((chans, half, full // 2, LANES)),
-            SCRATCH((chans, count1, full // 2 // count1, half * LANES)),
-            SCRATCH((chans, count2, full // 4 // count2, quarter * LANES)),
+            SCRATCH((chans, count1, SUBLANES, half * LANES)),
+            SCRATCH((chans, count2, SUBLANES, quarter * LANES)),
             SCRATCH((chans, wide, full + spare, LANES)),
             SCRATCH(shape),
             pltpu.SemaphoreType.DMA((1 + chans,)),
         ],
         compiler_params=pltpu.CompilerParams(vmem_limit_bytes=48 * 2**20),
         name="up",
-    )(in_hbm(sweeps), value, right, coarse, *received)
+    )(in_hbm(sweeps), fine, coarse, *received)
 
 
 def local(target, grad_x, grad_y, labels, sweeps):
     parts, around_globe = lax.axis_size("lat"), lax.axis_size("lon")
-    value, right, coarse, *sent = down(parts, sweeps, target, grad_x, grad_y, labels)
+    if parts < 2:
+        raise NotImplementedError
+    fine, coarse, *sent = down(parts, sweeps, target, grad_x, grad_y, labels)
     eastward_pairs = [(i, (i + 1) % around_globe) for i in range(around_globe)]
     westward_pairs = [(j, i) for i, j in eastward_pairs]
     if parts == 2:
@@ -567,7 +537,7 @@
         from_east = lax.ppermute(west, "lon", westward_pairs)
         across_east = lax.ppermute(west_across, ("lon", "lat"), across(westward_pairs))
         received = (packed, from_west, across_west, from_east, across_east)
-        return up(parts, target.shape, sweeps, value, right, coarse, *received)
+        return up(parts, target.shape, sweeps, fine, coarse, *received)
 
     chans, half_rows = coarse.shape[:2]
     coarse = coarse.reshape(chans, half_rows, -1, LANES).transpose(0, 2, 1, 3)
@@ -578,28 +548,22 @@
         from_east = lax.ppermute(westward(parts_of[0], parts_of[-1]), "lon", westward_pairs)
         return jnp.stack(with_edges(parts_of, from_west, from_east), 1)
 
-    value, right, coarse = (shared_lon(f) for f in (value, right, coarse))
-    if parts > 2:
-        rows = target.shape[1]
-        spare = 2 * SUBLANES
-        southward = [(i, i + 1) for i in range(parts - 1)]
-        northward = [(i + 1, i) for i in range(parts - 1)]
-
-        def shared_lat(field):
-            north = lax.ppermute(field[:, :, rows:], "lat", southward)
-            south = lax.ppermute(field[:, :, :spare], "lat", northward)
-            zeros = jnp.zeros_like(south)
-            return field + jnp.concatenate([north, zeros], 2) + jnp.concatenate([zeros, south], 2)
-
-        value, right = shared_lat(value), shared_lat(right)
-        every = lax.all_gather(coarse, "lat")
-        step = rows // 2
-        total = jnp.zeros((chans, coarse.shape[1], parts * step + SUBLANES, LANES), jnp.float32)
-        for i in range(parts):
-            total = total.at[:, :, i * step:i * step + step + SUBLANES].add(every[i])
-        coarse = total[:, :, 4:-4]
-    coarse = coarse.transpose(0, 2, 1, 3).reshape(chans, coarse.shape[2], -1)
-    return up(parts, target.shape, sweeps, value, right, coarse)
+    fine, coarse = shared_lon(fine), shared_lon(coarse)
+    rows = target.shape[1]
+    spare = 2 * SUBLANES
+    southward = [(i, i + 1) for i in range(parts - 1)]
+    northward = [(i + 1, i) for i in range(parts - 1)]
+    north = lax.ppermute(fine[:, :, rows:], "lat", southward)
+    south = lax.ppermute(fine[:, :, :spare], "lat", northward)
+    zeros = jnp.zeros_like(south)
+    fine = fine + jnp.concatenate([north, zeros], 2) + jnp.concatenate([zeros, south], 2)
+    every = lax.all_gather(coarse, "lat")
+    step = rows // 2
+    total = jnp.zeros((chans, coarse.shape[1], parts * step + SUBLANES, LANES), jnp.float32)
+    for i in range(parts):
+        total = total.at[:, :, i * step:i * step + step + SUBLANES].add(every[i])
+    coarse = total[:, :, 4:-4].transpose(0, 2, 1, 3).reshape(chans, parts * step, -1)
+    return up(parts, target.shape, sweeps, fine, coarse)
 
 
 def solution(mesh):

time: 17.3 us -> 17.7 us (1.023)
  Pallas kernels: 6.55 us -> 7.02 us
    pallas_call x1, Pallas kernels: 2.72 us -> 3.21 us  [down(): pl.pallas_call(functools.partial(down_kernel, parts), in_specs=[HBM] * 5,...]
where the time goes in v7:
time: 17.7 us; the launch traced here: 17.6 us
  starting transfers between devices  9.02 us (51%)
  Pallas kernels  7.02 us (40%)
  waiting for transfers between devices  1.55 us (9%)
    pallas_call x1, Pallas kernels, up(): pl.pallas_call(functools.partial(up_kernel, parts), in_specs=[HBM] + [VME...  3.81 us
    pallas_call x1, Pallas kernels, down(): pl.pallas_call(functools.partial(down_kernel, parts), in_specs=[HBM] * 5,...  3.21 us
    ppermute x1, starting transfers between devices, local(): packed = lax.ppermute(packed, 'lat', [(0, 1), (1, 0)])  3 us
    ppermute x1, starting transfers between devices, local(): from_east = lax.ppermute(west, 'lon', westward_pairs)  2.67 us
    ppermute x1, starting transfers between devices, local(): lax.ppermute(east_across, ('lon', 'lat'), across(eastward_pairs))  1.77 us
    ppermute x1, starting transfers between devices, local(): lax.ppermute(west_across, ('lon', 'lat'), across(westward_pairs))  1.57 us
    ppermute x1, waiting for transfers between devices, local(): lax.ppermute(west_across, ('lon', 'lat'), across(westward_pairs))  0.85 us
    ppermute x1, waiting for transfers between devices, local(): lax.ppermute(east_across, ('lon', 'lat'), across(eastward_pairs))  0.69 us
  transfers between devices with their start and end apart: 5, of which 2 were waited for; matrix products, arithmetic and copies ran while one was open for 0% of the time, Pallas kernels for 0%

profile of v7, /device:TPU:0, one launch (start us, length us, event | category | flops | bytes accessed | tf_op | source)
XLA Modules:
  0.0 17.6 jit_solution(11221165285608683344)
XLA Ops:
  0.0 3.2 %down.1 = (f32[3,9,24,128]{3,2,1,0:T(8,128)S(1)}, f32[3,12,640]{2,1,0:T(8,128)S(1)}, f32[3,15,8,128]{3,2,1,0:T(8,128)S(1)}, f32[3,8,128]{2,1,0:T(8,128)S(1)}, f3...) custom-call(s32[3]{0:T(128)} %sweeps_hbm.3, f32[3,16,1024]{2,1,0:T(8,128)} %target.1, ...), custom_call_target="tpu_custom_call" | custom-call | tf_op jit(solution)/shard_map/down/pallas_call | solution.py:378
  3.2 3.0 %collective-permute-start = (f32[3,15,8,128]{3,2,1,0:T(8,128)S(1)}, f32[3,15,8,128]{3,2,1,0:T(8,128)S(1)}, u32[]{:S(2)}, u32[]{:S(2)}) collective-permute-start(f32[3,15,8,128]{3,2,1,0:T(8,128)S(1)} %get-tuple-element.14), channel_id=1, source_target_pairs={{0,1},{1,0},{2,3},{3,2},{4,5},{5,4},{6,7},{7,6},{8,9},{9,8},{10,11... | collective-permute-start | bytes 552968 | tf_op jit(solution)/shard_map/ppermute | solution.py:534
  6.2 0.0 collective-permute-start.1
  6.2 1.8 %collective-permute-start.2 = (f32[3,8,128]{2,1,0:T(8,128)S(1)}, f32[3,8,128]{2,1,0:T(8,128)S(1)}, u32[]{:S(2)}, u32[]{:S(2)}) collective-permute-start(f32[3,8,128]{2,1,0:T(8,128)S(1)} %get-tuple-element.16), channel_id=1, source_target_pairs={{0,3},{1,2},{2,5},{3,4},{4,7},{5,6},{6,9},{7,8},{8,11},{9,10},{10,... | collective-permute-start | bytes 36872 | tf_op jit(solution)/shard_map/ppermute | solution.py:536
  8.0 2.7 %collective-permute-start.3 = (f32[3,8,128]{2,1,0:T(8,128)S(1)}, f32[3,8,128]{2,1,0:T(8,128)S(1)}, u32[]{:S(2)}, u32[]{:S(2)}) collective-permute-start(f32[3,8,128]{2,1,0:T(8,128)S(1)} %get-tuple-element.17), channel_id=1, source_target_pairs={{2,0},{4,2},{6,4},{8,6},{10,8},{12,10},{14,12},{16,14},{18,16},{20... | collective-permute-start | bytes 36872 | tf_op jit(solution)/shard_map/ppermute | solution.py:537
  10.7 1.6 %collective-permute-start.4 = (f32[3,8,128]{2,1,0:T(8,128)S(1)}, f32[3,8,128]{2,1,0:T(8,128)S(1)}, u32[]{:S(2)}, u32[]{:S(2)}) collective-permute-start(f32[3,8,128]{2,1,0:T(8,128)S(1)} %get-tuple-element.18), channel_id=1, source_target_pairs={{2,1},{3,0},{4,3},{5,2},{6,5},{7,4},{8,7},{9,6},{10,9},{11,8},{12,... | collective-permute-start | bytes 36872 | tf_op jit(solution)/shard_map/ppermute | solution.py:538
  12.2 0.0 collective-permute-done.1.refs_1_
  12.2 0.7 %collective-permute-done.2.refs_2_ = f32[3,8,128]{2,1,0:T(8,128)S(1)} collective-permute-done((f32[3,8,128]{2,1,0:T(8,128)S(1)}, f32[3,8,128]{2,1,0:T(8,128)S(1)}, u32[]{:S(2)}, u32[]{:S(2)}) %collective-permute-start.2) | collective-permute-done | bytes 12320 | tf_op jit(solution)/shard_map/ppermute | solution.py:536
  12.9 0.0 collective-permute-done.3.refs_3_
  12.9 0.8 %collective-permute-done.4.refs_4_ = f32[3,8,128]{2,1,0:T(8,128)S(1)} collective-permute-done((f32[3,8,128]{2,1,0:T(8,128)S(1)}, f32[3,8,128]{2,1,0:T(8,128)S(1)}, u32[]{:S(2)}, u32[]{:S(2)}) %collective-permute-start.4) | collective-permute-done | bytes 12320 | tf_op jit(solution)/shard_map/ppermute | solution.py:538
  13.8 0.0 collective-permute-done.refs_0_
  13.8 3.8 %up.1 = f32[3,16,1024]{2,1,0:T(8,128)} custom-call(s32[3]{0:T(128)} %sweeps_hbm.3, f32[3,9,24,128]{3,2,1,0:T(8,128)S(1)} %get-tuple-element.12.fine_ref, f32[3,12,640]{2,1,0:T(8,128)S(1)} %get-tuple-element.13.coarse_ref, f32[3,15,8,128]{3,2,1,0:T(8,128)S(1)} %collective-permute-done.refs_0_, f32[3,8,128]{2,1,0:T(8,128)S(1)} %collective-permute-done.1.refs_1_, ...), custom_call_target="tpu_custom_call" | custom-call | tf_op jit(solution)/shard_map/up/pallas_call | solution.py:503
Async XLA Ops:
  3.2 10.6 %collective-permute-start = (f32[3,15,8,128]{3,2,1,0:T(8,128)S(1)}, f32[3,15,8,128]{3,2,1,0:T(8,128)S(1)}, u32[]{:S(2)}, u32[]{:S(2)}) collective-permute-start(f32[3,15,8,128]{3,2,1,0:T(8,128)S(1)} %get-tuple-element.14), channel_id=1, source_target_pairs={{0,1},{1,0},{2,3},{3,2},{4,5},{5,4},{6,7},{7,6},{8,9},{9,8},{10,11... | collective-permute-start | bytes 552968 | tf_op jit(solution)/shard_map/ppermute | solution.py:534
  6.2 6.0 %collective-permute-start.1 = (f32[3,8,128]{2,1,0:T(8,128)S(1)}, f32[3,8,128]{2,1,0:T(8,128)S(1)}, u32[]{:S(2)}, u32[]{:S(2)}) collective-permute-start(f32[3,8,128]{2,1,0:T(8,128)S(1)} %get-tuple-element.15), channel_id=1, source_target_pairs={{0,2},{2,4},{4,6},{6,8},{8,10},{10,12},{12,14},{14,16},{16,18},{18... | collective-permute-start | bytes 36872 | tf_op jit(solution)/shard_map/ppermute | solution.py:535
  6.2 6.7 %collective-permute-start.2 = (f32[3,8,128]{2,1,0:T(8,128)S(1)}, f32[3,8,128]{2,1,0:T(8,128)S(1)}, u32[]{:S(2)}, u32[]{:S(2)}) collective-permute-start(f32[3,8,128]{2,1,0:T(8,128)S(1)} %get-tuple-element.16), channel_id=1, source_target_pairs={{0,3},{1,2},{2,5},{3,4},{4,7},{5,6},{6,9},{7,8},{8,11},{9,10},{10,... | collective-permute-start | bytes 36872 | tf_op jit(solution)/shard_map/ppermute | solution.py:536
  8.0 4.9 %collective-permute-start.3 = (f32[3,8,128]{2,1,0:T(8,128)S(1)}, f32[3,8,128]{2,1,0:T(8,128)S(1)}, u32[]{:S(2)}, u32[]{:S(2)}) collective-permute-start(f32[3,8,128]{2,1,0:T(8,128)S(1)} %get-tuple-element.17), channel_id=1, source_target_pairs={{2,0},{4,2},{6,4},{8,6},{10,8},{12,10},{14,12},{16,14},{18,16},{20... | collective-permute-start | bytes 36872 | tf_op jit(solution)/shard_map/ppermute | solution.py:537
  10.7 3.1 %collective-permute-start.4 = (f32[3,8,128]{2,1,0:T(8,128)S(1)}, f32[3,8,128]{2,1,0:T(8,128)S(1)}, u32[]{:S(2)}, u32[]{:S(2)}) collective-permute-start(f32[3,8,128]{2,1,0:T(8,128)S(1)} %get-tuple-element.18), channel_id=1, source_target_pairs={{2,1},{3,0},{4,3},{5,2},{6,5},{7,4},{8,7},{9,6},{10,9},{11,8},{12,... | collective-permute-start | bytes 36872 | tf_op jit(solution)/shard_map/ppermute | solution.py:538

commit v8 on v6

--- a/solution.py
+++ b/solution.py
@@ -313,7 +313,6 @@
     for chan in range(chans):
         for copy in copies[chan]:
             copy.wait()
-    for chan in range(chans):
         own = jnp.concatenate([target_v[chan], blank], 1)
         sel_x = jnp.concatenate([chosen(grad_x_v, chan), blank], 1)
         sel_y = jnp.concatenate([chosen(grad_y_v, chan), blank], 1)
@@ -356,7 +355,7 @@
         coarse_ref[chan] = low
         if parts != 2:
             continue
-        packed_ref, east_ref, east_across, west_ref, west_across = sent_refs
+        packed_ref, east_across, east_ref, west_across, west_ref = sent_refs
         wide = value_ref.shape[1]
         value = [value_ref[chan, k] for k in range(wide)]
         right = [right_ref[chan, k] for k in range(wide)]
@@ -428,8 +427,8 @@
 
     def sides(chan, across):
         heights = ACROSS if across else own_heights
-        from_west = unbundle(edge_refs[across][chan], heights, TO_EAST)
-        from_east = unbundle(edge_refs[2 + across][chan], heights, TO_WEST)
+        from_west = unbundle(edge_refs[1 - across][chan], heights, TO_EAST)
+        from_east = unbundle(edge_refs[3 - across][chan], heights, TO_WEST)
         return list(zip(from_west, from_east))
 
     from_partner = []
@@ -556,17 +555,19 @@
     value, right, coarse, *sent = down(parts, sweeps, target, grad_x, grad_y, labels)
     eastward_pairs = [(i, (i + 1) % around_globe) for i in range(around_globe)]
     westward_pairs = [(j, i) for i, j in eastward_pairs]
+    if parts < 2:
+        raise NotImplementedError
     if parts == 2:
         def across(pairs):
             return [(2 * i + k, 2 * j + 1 - k) for i, j in pairs for k in range(2)]
 
-        packed, east, east_across, west, west_across = sent
+        packed, east_across, east, west_across, west = sent
         packed = lax.ppermute(packed, "lat", [(0, 1), (1, 0)])
+        across_west = lax.ppermute(east_across, ("lon", "lat"), across(eastward_pairs))
         from_west = lax.ppermute(east, "lon", eastward_pairs)
-        across_west = lax.ppermute(east_across, ("lon", "lat"), across(eastward_pairs))
+        across_east = lax.ppermute(west_across, ("lon", "lat"), across(westward_pairs))
         from_east = lax.ppermute(west, "lon", westward_pairs)
-        across_east = lax.ppermute(west_across, ("lon", "lat"), across(westward_pairs))
-        received = (packed, from_west, across_west, from_east, across_east)
+        received = (packed, across_west, from_west, across_east, from_east)
         return up(parts, target.shape, sweeps, value, right, coarse, *received)
 
     chans, half_rows = coarse.shape[:2]

time: 17.3 us -> 17.4 us (level); the launches traced: 17.1 us -> 17.6 us
  Pallas kernels: 6.55 us -> 7.21 us
    ppermute x1, starting transfers between devices: 1.57 us -> 3.74 us  [local(): lax.ppermute(west_across, ('lon', 'lat'), across(westward_pairs))]
    ppermute x1, starting transfers between devices: 2.67 us -> 0.68 us  [local(): from_east = lax.ppermute(west, 'lon', westward_pairs)]
    ppermute x1, starting transfers between devices: 1.77 us -> 0.01 us  [local(): lax.ppermute(east_across, ('lon', 'lat'), across(eastward_pairs))]
    ppermute x1, starting transfers between devices: 0.01 us -> 1.6 us  [local(): from_west = lax.ppermute(east, 'lon', eastward_pairs)]
    ppermute x1, waiting for transfers between devices: 0.74 us -> 0.01 us  [local(): lax.ppermute(west_across, ('lon', 'lat'), across(westward_pairs))]
    ppermute x1, waiting for transfers between devices: 0.01 us -> 0.6 us  [local(): from_east = lax.ppermute(west, 'lon', westward_pairs)]
    pallas_call x1, Pallas kernels: 2.72 us -> 3.14 us  [down(): pl.pallas_call(functools.partial(down_kernel, parts), in_specs=[HBM] * 5,...]
    pallas_call x1, Pallas kernels: 3.82 us -> 4.06 us  [up(): pl.pallas_call(functools.partial(up_kernel, parts), in_specs=[HBM] + [VME...]
where the time goes in v8:
time: 17.4 us; the launch traced here: 17.6 us
  starting transfers between devices  9.02 us (52%)
  Pallas kernels  7.21 us (41%)
  waiting for transfers between devices  1.41 us (8%)
    pallas_call x1, Pallas kernels, up(): pl.pallas_call(functools.partial(up_kernel, parts), in_specs=[HBM] + [VME...  4.06 us
    ppermute x1, starting transfers between devices, local(): lax.ppermute(west_across, ('lon', 'lat'), across(westward_pairs))  3.74 us
    pallas_call x1, Pallas kernels, down(): pl.pallas_call(functools.partial(down_kernel, parts), in_specs=[HBM] * 5,...  3.14 us
    ppermute x1, starting transfers between devices, local(): packed = lax.ppermute(packed, 'lat', [(0, 1), (1, 0)])  3 us
    ppermute x1, starting transfers between devices, local(): from_west = lax.ppermute(east, 'lon', eastward_pairs)  1.6 us
    ppermute x1, waiting for transfers between devices, local(): lax.ppermute(east_across, ('lon', 'lat'), across(eastward_pairs))  0.8 us
    ppermute x1, starting transfers between devices, local(): from_east = lax.ppermute(west, 'lon', westward_pairs)  0.68 us
    ppermute x1, waiting for transfers between devices, local(): from_east = lax.ppermute(west, 'lon', westward_pairs)  0.6 us
  transfers between devices with their start and end apart: 5, of which 2 were waited for; matrix products, arithmetic and copies ran while one was open for 0% of the time, Pallas kernels for 0%

profile of v8, /device:TPU:0, one launch (start us, length us, event | category | flops | bytes accessed | tf_op | source)
XLA Modules:
  0.0 17.6 jit_solution(17412667838763931819)
XLA Ops:
  0.0 3.1 %down.1 = (f32[3,9,24,128]{3,2,1,0:T(8,128)S(1)}, f32[3,9,24,128]{3,2,1,0:T(8,128)S(1)}, f32[3,12,640]{2,1,0:T(8,128)S(1)}, f32[3,19,8,128]{3,2,1,0:T(8,128)S(1)...) custom-call(s32[3]{0:T(128)} %sweeps_hbm.3, ...), custom_call_target="tpu_custom_call" | custom-call | tf_op jit(solution)/shard_map/down/pallas_call | solution.py:385
  3.2 3.0 %collective-permute-start = (f32[3,19,8,128]{3,2,1,0:T(8,128)S(1)}, f32[3,19,8,128]{3,2,1,0:T(8,128)S(1)}, u32[]{:S(2)}, u32[]{:S(2)}) collective-permute-start(f32[3,19,8,128]{3,2,1,0:T(8,128)S(1)} %get-tuple-element.16), channel_id=1, source_target_pairs={{0,1},{1,0},{2,3},{3,2},{4,5},{5,4},{6,7},{7,6},{8,9},{9,8},{10,11... | collective-permute-start | bytes 700424 | tf_op jit(solution)/shard_map/ppermute | solution.py:565
  6.2 0.0 collective-permute-start.1
  6.2 1.6 %collective-permute-start.2 = (f32[3,8,128]{2,1,0:T(8,128)S(1)}, f32[3,8,128]{2,1,0:T(8,128)S(1)}, u32[]{:S(2)}, u32[]{:S(2)}) collective-permute-start(f32[3,8,128]{2,1,0:T(8,128)S(1)} %get-tuple-element.18), channel_id=1, source_target_pairs={{0,2},{2,4},{4,6},{6,8},{8,10},{10,12},{12,14},{14,16},{16,18},{18... | collective-permute-start | bytes 36872 | tf_op jit(solution)/shard_map/ppermute | solution.py:567
  7.8 3.7 %collective-permute-start.3 = (f32[3,8,128]{2,1,0:T(8,128)S(1)}, f32[3,8,128]{2,1,0:T(8,128)S(1)}, u32[]{:S(2)}, u32[]{:S(2)}) collective-permute-start(f32[3,8,128]{2,1,0:T(8,128)S(1)} %get-tuple-element.19), channel_id=1, source_target_pairs={{2,1},{3,0},{4,3},{5,2},{6,5},{7,4},{8,7},{9,6},{10,9},{11,8},{12,... | collective-permute-start | bytes 36872 | tf_op jit(solution)/shard_map/ppermute | solution.py:568
  11.5 0.7 %collective-permute-start.4 = (f32[3,8,128]{2,1,0:T(8,128)S(1)}, f32[3,8,128]{2,1,0:T(8,128)S(1)}, u32[]{:S(2)}, u32[]{:S(2)}) collective-permute-start(f32[3,8,128]{2,1,0:T(8,128)S(1)} %get-tuple-element.20), channel_id=1, source_target_pairs={{2,0},{4,2},{6,4},{8,6},{10,8},{12,10},{14,12},{16,14},{18,16},{20... | collective-permute-start | bytes 36872 | tf_op jit(solution)/shard_map/ppermute | solution.py:569
  12.2 0.8 %collective-permute-done.1.refs_1_ = f32[3,8,128]{2,1,0:T(8,128)S(1)} collective-permute-done((f32[3,8,128]{2,1,0:T(8,128)S(1)}, f32[3,8,128]{2,1,0:T(8,128)S(1)}, u32[]{:S(2)}, u32[]{:S(2)}) %collective-permute-start.1) | collective-permute-done | bytes 12320 | tf_op jit(solution)/shard_map/ppermute | solution.py:566
  13.0 0.0 collective-permute-done.2.refs_2_
  13.0 0.0 collective-permute-done.3.refs_3_
  13.0 0.6 %collective-permute-done.4.refs_4_ = f32[3,8,128]{2,1,0:T(8,128)S(1)} collective-permute-done((f32[3,8,128]{2,1,0:T(8,128)S(1)}, f32[3,8,128]{2,1,0:T(8,128)S(1)}, u32[]{:S(2)}, u32[]{:S(2)}) %collective-permute-start.4) | collective-permute-done | bytes 12320 | tf_op jit(solution)/shard_map/ppermute | solution.py:569
  13.6 0.0 collective-permute-done.refs_0_
  13.6 4.1 %up.1 = f32[3,16,1024]{2,1,0:T(8,128)} custom-call(s32[3]{0:T(128)} %sweeps_hbm.3, f32[3,9,24,128]{3,2,1,0:T(8,128)S(1)} %get-tuple-element.13.value_ref, f32[3,9,24,128]{3,2,1,0:T(8,128)S(1)} %get-tuple-element.14.right_ref, f32[3,12,640]{2,1,0:T(8,128)S(1)} %get-tuple-element.15.coarse_ref, f32[3,19,8,128]{3,2,1,0:T(8,128)S(1)} %collective-permute-done.refs_0_, ...), custom_call_target="tpu_custom_call" | custom-call | tf_op jit(solution)/shard_map/up/pallas_call | solution.py:531
Async XLA Ops:
  3.2 10.4 %collective-permute-start = (f32[3,19,8,128]{3,2,1,0:T(8,128)S(1)}, f32[3,19,8,128]{3,2,1,0:T(8,128)S(1)}, u32[]{:S(2)}, u32[]{:S(2)}) collective-permute-start(f32[3,19,8,128]{3,2,1,0:T(8,128)S(1)} %get-tuple-element.16), channel_id=1, source_target_pairs={{0,1},{1,0},{2,3},{3,2},{4,5},{5,4},{6,7},{7,6},{8,9},{9,8},{10,11... | collective-permute-start | bytes 700424 | tf_op jit(solution)/shard_map/ppermute | solution.py:565
  6.2 6.8 %collective-permute-start.1 = (f32[3,8,128]{2,1,0:T(8,128)S(1)}, f32[3,8,128]{2,1,0:T(8,128)S(1)}, u32[]{:S(2)}, u32[]{:S(2)}) collective-permute-start(f32[3,8,128]{2,1,0:T(8,128)S(1)} %get-tuple-element.17), channel_id=1, source_target_pairs={{0,3},{1,2},{2,5},{3,4},{4,7},{5,6},{6,9},{7,8},{8,11},{9,10},{10,... | collective-permute-start | bytes 36872 | tf_op jit(solution)/shard_map/ppermute | solution.py:566
  6.2 6.8 %collective-permute-start.2 = (f32[3,8,128]{2,1,0:T(8,128)S(1)}, f32[3,8,128]{2,1,0:T(8,128)S(1)}, u32[]{:S(2)}, u32[]{:S(2)}) collective-permute-start(f32[3,8,128]{2,1,0:T(8,128)S(1)} %get-tuple-element.18), channel_id=1, source_target_pairs={{0,2},{2,4},{4,6},{6,8},{8,10},{10,12},{12,14},{14,16},{16,18},{18... | collective-permute-start | bytes 36872 | tf_op jit(solution)/shard_map/ppermute | solution.py:567
  7.8 5.2 %collective-permute-start.3 = (f32[3,8,128]{2,1,0:T(8,128)S(1)}, f32[3,8,128]{2,1,0:T(8,128)S(1)}, u32[]{:S(2)}, u32[]{:S(2)}) collective-permute-start(f32[3,8,128]{2,1,0:T(8,128)S(1)} %get-tuple-element.19), channel_id=1, source_target_pairs={{2,1},{3,0},{4,3},{5,2},{6,5},{7,4},{8,7},{9,6},{10,9},{11,8},{12,... | collective-permute-start | bytes 36872 | tf_op jit(solution)/shard_map/ppermute | solution.py:568
  11.5 2.1 %collective-permute-start.4 = (f32[3,8,128]{2,1,0:T(8,128)S(1)}, f32[3,8,128]{2,1,0:T(8,128)S(1)}, u32[]{:S(2)}, u32[]{:S(2)}) collective-permute-start(f32[3,8,128]{2,1,0:T(8,128)S(1)} %get-tuple-element.20), channel_id=1, source_target_pairs={{2,0},{4,2},{6,4},{8,6},{10,8},{12,10},{14,12},{16,14},{18,16},{20... | collective-permute-start | bytes 36872 | tf_op jit(solution)/shard_map/ppermute | solution.py:569
